TPU v7x, 32 devices: a whole 2x2x4 slice. The times are simulated.
32 devices in a mesh: branch: 4 (over y, x), dp: 8 (over z, core).
Axes of the slice: x: 2, y: 2, z: 4, core: 2. Of those that a mesh axis runs over, the one named last changes fastest.
Arguments:
- tokens: bfloat16 [16384, 768], P('dp'), may hold values from -6 to 6
- cotangent: bfloat16 [16384, 768], P('dp'), may hold values from -6 to 6
- gain_before: float32 [768], replicated, may hold values from 0.1 to 1.9
- gain_middle: float32 [768], replicated, may hold values from 0.1 to 1.9
- router_vector: float32 [768], replicated, may hold values from -0.21875 to 0.21875
- local_heads: bfloat16 [768, 3, 512], P(None, None, 'branch'), may hold values from -0.3125 to 0.3125
- local_merge: bfloat16 [512, 768], P('branch'), may hold values from -0.5 to 0.5
- routed_heads: bfloat16 [768, 3, 768], P(None, None, 'branch'), may hold values from -0.3125 to 0.3125
- routed_merge: bfloat16 [768, 768], P('branch'), may hold values from -1.75 to 1.75
- local_expand: bfloat16 [768, 2, 1024], P(None, None, 'branch'), may hold values from -0.21875 to 0.21875
- local_reduce: bfloat16 [1024, 768], P('branch'), may hold values from -0.1875 to 0.1875
- routed_expand: bfloat16 [768, 2, 4096], P(None, None, 'branch'), may hold values from -0.21875 to 0.21875
- routed_reduce: bfloat16 [4096, 768], P('branch'), may hold values from -0.1875 to 0.1875
- routed_slots: int32 [4096], P('dp'), may hold values from 0 to 2047, as said below
- routed_counts: int32 [8], replicated, may hold values from 0 to 512, as said below
Outputs:
- layer_output: float32 [16384, 768], P('dp')
- tokens_delta: float32 [16384, 768], P('dp')
- delta_gain_before: float32 [768], replicated
- delta_gain_middle: float32 [768], replicated
- delta_router: float32 [768], replicated
- delta_local_heads: float32 [768, 3, 512], P(None, None, 'branch')
- delta_local_merge: float32 [512, 768], P('branch')
- delta_routed_heads: float32 [768, 3, 768], P(None, None, 'branch')
- delta_routed_merge: float32 [768, 768], P('branch')
- delta_local_expand: float32 [768, 2, 1024], P(None, None, 'branch')
- delta_local_reduce: float32 [1024, 768], P('branch')
- delta_routed_expand: float32 [768, 2, 4096], P(None, None, 'branch')
- delta_routed_reduce: float32 [4096, 768], P('branch')
Inputs may be any that keep to these rules, and one draw needn't show every extreme that they name: `routed_counts`: entry e counts the routed tokens among the 2048 tokens of block e; blocks 2k and 2k + 1 together hold exactly 512; at least one entry equals 512. `routed_slots`: the 512 entries of block e begin with the positions, within its 2048 tokens, of its routed tokens in increasing order, as many as routed_counts[e]; the other entries are 0 and unused.
All inputs are finite; a program needn't handle non-finite values.
Results may differ from a plain program's by a relative error of at most 0.02.
The roundings to bfloat16 on the way count: a program that leaves them out, or rounds other values in their place, can miss the bound.
Values may be sent and summed in bfloat16 or wider, within the bound.
A program may use at most 384 MiB of HBM per device.

v0:
```python
import jax
import jax.numpy as jnp
from jax import lax
from jax.sharding import PartitionSpec as P

DH = 64
WIN = 128


EPSILON = 1e-06
NEGATIVE = -1e30
HIGHEST_PRECISION = lax.Precision.HIGHEST


def padded(cells, sides, width):
    for axis, dim in sides:
        count = lax.axis_size(axis)
        ends = count - 1
        head = lax.slice_in_dim(cells, 0, width, axis=dim)
        tail = lax.slice_in_dim(cells, cells.shape[dim] - width, cells.shape[dim], axis=dim)
        cells = jnp.concatenate(
            [
                lax.ppermute(tail, axis, [(i, (i + 1) % count) for i in range(ends)]),
                cells,
                lax.ppermute(head, axis, [((i + 1) % count, i) for i in range(ends)]),
            ],
            axis=dim,
        )
    return cells


def norm_rows(values, gain_vector):
    return (
        values
        * lax.rsqrt(jnp.mean(values * values, axis=-1, keepdims=True) + EPSILON)
        * gain_vector
    )


def gated_unit(gate_pair):
    return jax.nn.gelu(gate_pair[:, 0], approximate=True) * gate_pair[:, 1]


def split_heads(values):
    return values.reshape(values.shape[0], -1, DH)


def heads_first(values):
    return values.transpose(1, 0, 2)


def head_scores(query_one, key_one, allowed):
    scores = jnp.dot(query_one, key_one.T, preferred_element_type=jnp.float32) * DH ** (-0.5)
    return jnp.where(allowed, scores, NEGATIVE)


def attend_forward(query_heads, key_heads, value_heads, allowed):

    def one_head(trio):
        query_one, key_one, value_one = trio
        scores = head_scores(query_one, key_one, allowed)
        score_peak = jnp.max(scores, axis=-1, keepdims=True)
        weights = jnp.exp(scores - score_peak)
        exp_total = jnp.sum(weights, axis=-1, keepdims=True)
        rounded_weights = (weights / exp_total).astype(jnp.bfloat16)
        context = jnp.dot(rounded_weights, value_one, preferred_element_type=jnp.float32).astype(
            jnp.bfloat16
        )
        return (context, score_peak + jnp.log(exp_total))

    contexts, logsums = lax.map(
        one_head, (heads_first(query_heads), heads_first(key_heads), heads_first(value_heads))
    )
    return (heads_first(contexts).reshape(query_heads.shape[0], -1), logsums)


def attend_backward(query_heads, key_heads, value_heads, allowed, logsum, grad_context):
    grad_heads = split_heads(grad_context)
    score_scale = DH ** (-0.5)

    def one_head(items):
        query_one, key_one, value_one, logsum_one, grad_one = items
        weights = jnp.exp(head_scores(query_one, key_one, allowed) - logsum_one)
        grad_weights = jnp.dot(grad_one, value_one.T, preferred_element_type=jnp.float32)
        inner_sum = jnp.sum(weights * grad_weights, axis=-1, keepdims=True)
        grad_scores = (weights * (grad_weights - inner_sum)).astype(jnp.bfloat16)
        grad_query = jnp.dot(grad_scores, key_one, preferred_element_type=jnp.float32) * score_scale
        grad_keys = (
            jnp.dot(grad_scores.T, query_one, preferred_element_type=jnp.float32) * score_scale
        )
        grad_values = jnp.dot(
            weights.astype(jnp.bfloat16).T, grad_one, preferred_element_type=jnp.float32
        )
        return (grad_query, grad_keys, grad_values)

    grad_query, grad_keys, grad_values = lax.map(
        one_head,
        (
            heads_first(query_heads),
            heads_first(key_heads),
            heads_first(value_heads),
            logsum,
            heads_first(grad_heads),
        ),
    )
    query_count = query_heads.shape[0]
    key_count = key_heads.shape[0]
    return (
        heads_first(grad_query).reshape(query_count, -1),
        heads_first(grad_keys).reshape(key_count, -1),
        heads_first(grad_values).reshape(key_count, -1),
    )


def feed_both(inputs, grad_seed, expand, narrow):
    gate_pair = jnp.einsum("rd,dcf->rcf", inputs, expand, preferred_element_type=jnp.float32)
    mixed, pull_back = jax.vjp(gated_unit, gate_pair)
    hidden = mixed.astype(jnp.bfloat16)
    output = jnp.dot(hidden, narrow, preferred_element_type=jnp.float32)
    grad_hidden = jnp.einsum("rd,fd->rf", grad_seed, narrow, preferred_element_type=jnp.float32)
    grad_pair = pull_back(grad_hidden)[0].astype(jnp.bfloat16)
    grad_inputs = jnp.einsum("rcf,dcf->rd", grad_pair, expand, preferred_element_type=jnp.float32)
    grad_expand = jnp.einsum("rd,rcf->dcf", inputs, grad_pair, preferred_element_type=jnp.float32)
    grad_narrow = jnp.einsum("rf,rd->fd", hidden, grad_seed, preferred_element_type=jnp.float32)
    return (output, grad_inputs, grad_expand, grad_narrow)


def per_device(
    tokens,
    cotangent,
    gain_before,
    gain_middle,
    router_vector,
    local_heads,
    local_merge,
    routed_heads,
    routed_merge,
    local_expand,
    local_reduce,
    routed_expand,
    routed_reduce,
    routed_slots,
    routed_counts,
):
    row_count = tokens.shape[0]
    devices = lax.axis_size("dp")
    block_index = lax.axis_index("dp")
    capacity = routed_slots.shape[0]
    routed_width = routed_heads.shape[2]
    tokens_float = tokens.astype(jnp.float32)
    cotangent_float = cotangent.astype(jnp.float32)
    first_float, pull_first = jax.vjp(norm_rows, tokens_float, gain_before)
    first_normed = first_float.astype(jnp.bfloat16)
    local_proj = jnp.einsum(
        "td,dcf->tcf", first_normed, local_heads, preferred_element_type=jnp.float32
    ).astype(jnp.bfloat16)
    widened = padded(local_proj[:, 1:], (("dp", 0),), WIN)
    query_place = block_index * row_count + jnp.arange(row_count, dtype=jnp.int32)
    key_place = block_index * row_count - WIN + jnp.arange(row_count + 2 * WIN, dtype=jnp.int32)
    near_mask = (
        (jnp.abs(query_place[:, None] - key_place[None, :]) <= WIN)
        & (key_place[None, :] >= 0)
        & (key_place[None, :] < devices * row_count)
    )
    local_query = split_heads(local_proj[:, 0])
    local_keys = split_heads(widened[:, 0])
    local_values = split_heads(widened[:, 1])
    local_context, local_logsum = attend_forward(local_query, local_keys, local_values, near_mask)
    local_attn = jnp.dot(local_context, local_merge, preferred_element_type=jnp.float32)
    slot_ids = jnp.arange(capacity, dtype=jnp.int32)
    live_slots = slot_ids < routed_counts[block_index]
    picked_first = first_normed[routed_slots]
    gate_value = jax.nn.sigmoid(
        jnp.dot(picked_first.astype(jnp.float32), router_vector, precision=HIGHEST_PRECISION)
    )
    routed_proj = jnp.einsum(
        "rd,dcf->rcf", picked_first, routed_heads, preferred_element_type=jnp.float32
    ).astype(jnp.bfloat16)
    key_rows = jnp.concatenate([routed_proj[:, 1], routed_proj[:, 2]], 1)
    gathered = lax.all_gather(key_rows, "dp", axis=0, tiled=True)
    key_live = (slot_ids[None, :] < routed_counts[:, None]).reshape(-1)
    reach_mask = jnp.broadcast_to(key_live[None, :], (capacity, key_live.shape[0]))
    routed_query = split_heads(routed_proj[:, 0])
    routed_keys = split_heads(gathered[:, :routed_width])
    routed_values = split_heads(gathered[:, routed_width:])
    routed_context, routed_logsum = attend_forward(
        routed_query, routed_keys, routed_values, reach_mask
    )
    routed_attn = jnp.dot(routed_context, routed_merge, preferred_element_type=jnp.float32)
    attn_rows = jnp.where(live_slots[:, None], gate_value[:, None] * routed_attn, 0.0)
    mixed = lax.psum(
        local_attn + jnp.zeros_like(local_attn).at[routed_slots].add(attn_rows), "branch"
    )
    middle = tokens_float + mixed
    second_float, pull_second = jax.vjp(norm_rows, middle, gain_middle)
    second_normed = second_float.astype(jnp.bfloat16)
    local_ff, local_grad, delta_local_expand, delta_local_reduce = feed_both(
        second_normed, cotangent, local_expand, local_reduce
    )
    picked_second = second_normed[routed_slots]
    picked_cotangent = cotangent_float[routed_slots]
    grad_seed = jnp.where(live_slots[:, None], gate_value[:, None] * picked_cotangent, 0.0).astype(
        jnp.bfloat16
    )
    feed_out, feed_grad, delta_routed_expand, delta_routed_reduce = feed_both(
        picked_second, grad_seed, routed_expand, routed_reduce
    )
    ff_rows = jnp.where(live_slots[:, None], gate_value[:, None] * feed_out, 0.0)
    ff_total = lax.psum(
        (local_ff + jnp.zeros_like(local_ff).at[routed_slots].add(ff_rows)).astype(jnp.bfloat16),
        "branch",
    ).astype(jnp.float32)
    layer_output = middle + ff_total
    gate_from_feed = jnp.where(live_slots, jnp.sum(picked_cotangent * feed_out, -1), 0.0)
    second_grad = local_grad + jnp.zeros_like(local_grad).at[routed_slots].add(
        jnp.where(live_slots[:, None], feed_grad, 0.0)
    )
    middle_part, gain_middle_part = pull_second(second_grad)
    middle_sum, delta_gain_middle = lax.psum((middle_part, gain_middle_part), "branch")
    feed_summed = None
    middle_grad = cotangent_float + middle_sum
    middle_low = middle_grad.astype(jnp.bfloat16)
    local_grad_context = jnp.einsum(
        "td,fd->tf", middle_low, local_merge, preferred_element_type=jnp.float32
    ).astype(jnp.bfloat16)
    delta_local_merge = jnp.einsum(
        "tf,td->fd", local_context, middle_low, preferred_element_type=jnp.float32
    )
    grad_query, grad_keys, grad_values = attend_backward(
        local_query, local_keys, local_values, near_mask, local_logsum, local_grad_context
    )
    wide_grad = jnp.stack([grad_keys, grad_values], 1)
    rim_rows = jnp.concatenate([wide_grad[:WIN], wide_grad[row_count + WIN :]], 0)
    came_rims = padded(rim_rows.astype(jnp.bfloat16), (("dp", 0),), WIN).astype(rim_rows.dtype)
    pair_grad = (
        wide_grad[WIN : WIN + row_count]
        .at[:WIN]
        .add(came_rims[:WIN])
        .at[row_count - WIN :]
        .add(came_rims[3 * WIN :])
    )
    local_triple = jnp.concatenate([grad_query[:, None], pair_grad], 1).astype(jnp.bfloat16)
    first_grad = jnp.einsum(
        "tcf,dcf->td", local_triple, local_heads, preferred_element_type=jnp.float32
    )
    delta_local_heads = jnp.einsum(
        "td,tcf->dcf", first_normed, local_triple, preferred_element_type=jnp.float32
    )
    middle_rows = middle_grad[routed_slots]
    routed_seed = jnp.where(live_slots[:, None], gate_value[:, None] * middle_rows, 0.0).astype(
        jnp.bfloat16
    )
    gate_from_attention = jnp.where(live_slots, jnp.sum(middle_rows * routed_attn, -1), 0.0)
    routed_grad_context = jnp.einsum(
        "rd,fd->rf", routed_seed, routed_merge, preferred_element_type=jnp.float32
    ).astype(jnp.bfloat16)
    delta_routed_merge = jnp.einsum(
        "rf,rd->fd", routed_context, routed_seed, preferred_element_type=jnp.float32
    )
    routed_grad_query, routed_grad_keys, routed_grad_values = attend_backward(
        routed_query, routed_keys, routed_values, reach_mask, routed_logsum, routed_grad_context
    )
    own_keys = lax.psum_scatter(
        jnp.concatenate([routed_grad_keys, routed_grad_values], 1).astype(jnp.bfloat16),
        "dp",
        scatter_dimension=0,
        tiled=True,
    ).astype(jnp.float32)
    routed_triple = jnp.stack(
        [routed_grad_query, own_keys[:, :routed_width], own_keys[:, routed_width:]], 1
    ).astype(jnp.bfloat16)
    picked_grad = jnp.einsum(
        "rcf,dcf->rd", routed_triple, routed_heads, preferred_element_type=jnp.float32
    )
    logit_grad = (gate_from_attention + gate_from_feed) * gate_value * (1.0 - gate_value)
    picked_grad = picked_grad + logit_grad[:, None] * router_vector[None, :]
    router_part = jnp.dot(logit_grad, picked_first.astype(jnp.float32), precision=HIGHEST_PRECISION)
    delta_routed_heads = jnp.einsum(
        "rd,rcf->dcf", picked_first, routed_triple, preferred_element_type=jnp.float32
    )
    first_grad = first_grad + jnp.zeros_like(first_grad).at[routed_slots].add(
        jnp.where(live_slots[:, None], picked_grad, 0.0)
    )
    tokens_part, gain_before_part = pull_first(first_grad)
    tokens_sum, delta_gain_before, delta_router = lax.psum(
        (tokens_part, gain_before_part, router_part), "branch"
    )
    tokens_delta = middle_grad + tokens_sum
    whole_sum = (
        lax.psum(delta_local_heads.astype(jnp.bfloat16), "dp").astype(jnp.float32),
        lax.psum(delta_local_merge.astype(jnp.bfloat16), "dp").astype(jnp.float32),
        lax.psum(delta_routed_heads.astype(jnp.bfloat16), "dp").astype(jnp.float32),
        lax.psum(delta_routed_merge.astype(jnp.bfloat16), "dp").astype(jnp.float32),
        lax.psum(delta_gain_before.astype(jnp.bfloat16), "dp").astype(jnp.float32),
        lax.psum(delta_router.astype(jnp.bfloat16), "dp").astype(jnp.float32),
        lax.psum(delta_local_expand.astype(jnp.bfloat16), "dp").astype(jnp.float32),
        lax.psum(delta_local_reduce.astype(jnp.bfloat16), "dp").astype(jnp.float32),
        lax.psum(delta_routed_expand.astype(jnp.bfloat16), "dp").astype(jnp.float32),
        lax.psum(delta_routed_reduce.astype(jnp.bfloat16), "dp").astype(jnp.float32),
        lax.psum(delta_gain_middle.astype(jnp.bfloat16), "dp").astype(jnp.float32),
    )
    attention_summed = whole_sum[:6]
    feed_summed = whole_sum[6:]
    return (
        layer_output,
        tokens_delta,
        attention_summed[4],
        feed_summed[4],
        attention_summed[5],
        attention_summed[0],
        attention_summed[1],
        attention_summed[2],
        attention_summed[3],
        feed_summed[0],
        feed_summed[1],
        feed_summed[2],
        feed_summed[3],
    )


def solution(mesh):
    return jax.shard_map(
        per_device,
        mesh=mesh,
        in_specs=(
            P("dp", None),
            P("dp", None),
            P(),
            P(),
            P(),
            P(None, None, "branch"),
            P("branch", None),
            P(None, None, "branch"),
            P("branch", None),
            P(None, None, "branch"),
            P("branch", None),
            P(None, None, "branch"),
            P("branch", None),
            P("dp"),
            P(),
        ),
        out_specs=(
            P("dp", None),
            P("dp", None),
            P(),
            P(),
            P(),
            P(None, None, "branch"),
            P("branch", None),
            P(None, None, "branch"),
            P("branch", None),
            P(None, None, "branch"),
            P("branch", None),
            P(None, None, "branch"),
            P("branch", None),
        ),
        check_vma=False,
    )
```

profile of v0, /device:TPU:0, one launch (start us, length us, event | category | flops | bytes accessed | tf_op | source)
XLA Modules:
  0.0 1185.2 jit_solution(170552281021442162)
XLA Ops:
  54.5 61.7 %while.58 = (s32[]{:T(128)}, bf16[2,2048,64]{1,2,0:T(8,128)(2,1)}, f32[2,2048,1]{1,2,0:T(1,128)S(1)}, bf16[2,2048,64]{2,1,0:T(8,128)(2,1)}, bf16[2,2304,64]{2,1,...) while((s32[]{:T(128)}, bf16[2,2048,64]{1,2,0:T(8,128)(2,1)}, ...), condition=%wide.region_4.5_spmd.clone, body=%wide.region_1.4_spmd.clone.sunk | while | flops 1269430272 | bytes 58695288 | solution.py:71
  54.5 12.7 %fusion.269 = (f32[2048]{0:T(1024)S(1)}, f32[2048,2304]{1,0:T(8,128)}) fusion(bf16[2,2304,64]{2,1,0:T(8,128)(2,1)} %get-tuple-element.776, s32[]{:T(128)S(6)} %copy.90, bf16[2,2048,64]{2,1,0:T(8,128)(2,1)} %get-tuple-element.775, pred[2304]{0:T(1024)(128)(4,1)S(1)} %get-tuple-element.781, pred[2304]{0:T(1024)(128)(4,1)S(1)} %get-tuple-element.780, ...), kind=kOutput, calls=%fused_computation.280.clone.1 | convolution fusion | flops 641726464 | bytes 20019712 | tf_op jit(solution)/shard_map/while/body/eval_jaxpr/dot_general | solution.py:53
  67.2 9.0 fusion.270
  76.2 9.2 fusion.271
  85.4 12.6 %fusion.269 = (f32[2048]{0:T(1024)S(1)}, f32[2048,2304]{1,0:T(8,128)}) fusion(bf16[2,2304,64]{2,1,0:T(8,128)(2,1)} %get-tuple-element.776, s32[]{:T(128)S(6)} %copy.90, bf16[2,2048,64]{2,1,0:T(8,128)(2,1)} %get-tuple-element.775, pred[2304]{0:T(1024)(128)(4,1)S(1)} %get-tuple-element.781, pred[2304]{0:T(1024)(128)(4,1)S(1)} %get-tuple-element.780, ...), kind=kOutput, calls=%fused_computation.280.clone.1 | convolution fusion | flops 641726464 | bytes 20019712 | tf_op jit(solution)/shard_map/while/body/eval_jaxpr/dot_general | solution.py:53
  98.1 9.0 fusion.270
  107.0 9.2 fusion.271
  133.3 29.2 %while.59 = (s32[]{:T(128)}, bf16[3,512,64]{1,2,0:T(8,128)(2,1)}, f32[3,512,1]{1,2,0:T(1,128)}, bf16[3,512,64]{2,1,0:T(8,128)(2,1)S(1)}, bf16[3,4096,64]{2,1,0:T...) while((s32[]{:T(128)}, bf16[3,512,64]{1,2,0:T(8,128)(2,1)}, ...), condition=%wide.region_8.9_spmd.clone, body=%wide.region_5.8_spmd.clone.sunk | while | flops 562068992 | bytes 27494496 | solution.py:71
  165.1 10.6 scatter_custom_fusion
  187.0 131.8 %all-reduce.13.cloned.1.call-done = f32[2048,768]{1,0:T(8,128)} async-done(((f32[2048,768]{1,0:T(8,128)}), f32[2048,768]{1,0:T(8,128)}) %all-reduce.13.cloned.1.call-update) | async-done | bytes 6291472 | tf_op jit(solution)/shard_map/psum | solution.py:191
  355.2 10.8 scatter_custom_fusion.1
  381.4 10.6 scatter_custom_fusion.2
  398.1 59.9 %all-reduce.15.cloned.1.call-done = bf16[2048,768]{1,0:T(8,128)(2,1)} async-done(((bf16[2048,768]{1,0:T(8,128)(2,1)}), bf16[2048,768]{1,0:T(8,128)(2,1)}) %all-reduce.15.cloned.1.call-update) | async-done | bytes 3145744 | tf_op jit(solution)/shard_map/psum | solution.py:209
  458.0 10.2 add_add_fusion.1
  483.1 123.7 %all-reduce.17.cloned.1.call-done = f32[2048,768]{1,0:T(8,128)} async-done(((f32[2048,768]{1,0:T(8,128)}), f32[2048,768]{1,0:T(8,128)}) %all-reduce.17.cloned.1.call-update) | async-done | bytes 6291472 | tf_op jit(solution)/shard_map/psum | solution.py:219
  630.3 83.5 %while.61 = (s32[]{:T(128)}, bf16[3,512,64]{1,2,0:T(8,128)(2,1)}, bf16[3,4096,64]{1,2,0:T(8,128)(2,1)}, bf16[3,4096,64]{1,2,0:T(8,128)(2,1)}, bf16[3,512,64]{2,1...) while((s32[]{:T(128)}, bf16[3,512,64]{1,2,0:T(8,128)(2,1)}, ...), condition=%wide.region_22.23_spmd.clone, body=%wide.region_20.22_spmd.clone.sunk | while | flops 1361346048 | bytes 145902960 | solution.py:96
  639.4 10.1 multiply_convert_fusion.8
  667.2 10.1 multiply_convert_fusion.8
  695.0 10.1 multiply_convert_fusion.8
  719.4 107.4 %while.60 = (s32[]{:T(128)}, bf16[2,2048,64]{1,2,0:T(8,128)(2,1)S(1)}, f32[2,2304,64]{1,2,0:T(8,128)}, f32[2,2304,64]{1,2,0:T(8,128)}, bf16[2,2048,64]{2,1,0:T(8...) while((s32[]{:T(128)}, ...), condition=%wide.region_19.20_spmd.clone, body=%wide.region_17.19_spmd.clone.sunk | while | flops 3086235648 | bytes 168172832 | solution.py:96
  719.7 9.1 fusion.284
  728.8 17.7 %multiply_reduce_fusion.9 = (f32[2048]{0:T(1024)S(1)}, f32[2048,2304]{1,0:T(8,128)}) fusion(f32[2048,2304]{1,0:T(8,128)} %fusion.284, f32[2048]{0:T(1024)S(1)} %bitcast.391, bf16[2,2304,64]{2,1,0:T(8,128)(2,1)S(1)} %get-tuple-element.840, s32[]{:T(128)S(6)} %copy.115, bf16[2,2048,64]{2,1,0:T(8,128)(2,1)S(1)} %copy-done.18, ...), kind=kOutput, calls=%fused_computation.57.clone.1 | convolution fusion | flops 651163648 | bytes 38906880 | tf_op jit(solution)/shard_map/while/body/eval_jaxpr/dot_general | solution.py:53
  746.5 13.0 %multiply_convert_fusion.7 = bf16[2048,2304]{1,0:T(8,128)(2,1)S(1)} fusion(f32[2048,2304]{1,0:T(8,128)} %get-tuple-element.736, f32[2048,2304]{1,0:T(8,128)} %fusion.284, f32[2048]{0:T(1024)S(1)} %get-tuple-element.737), kind=kLoop, calls=%fused_computation.56.clone.1 | loop fusion | flops 14155776 | bytes 47194112 | tf_op jit(solution)/shard_map/while/body/eval_jaxpr/convert_element_type | solution.py:86
  773.6 9.0 fusion.284
  782.6 17.5 %multiply_reduce_fusion.9 = (f32[2048]{0:T(1024)S(1)}, f32[2048,2304]{1,0:T(8,128)}) fusion(f32[2048,2304]{1,0:T(8,128)} %fusion.284, f32[2048]{0:T(1024)S(1)} %bitcast.391, bf16[2,2304,64]{2,1,0:T(8,128)(2,1)S(1)} %get-tuple-element.840, s32[]{:T(128)S(6)} %copy.115, bf16[2,2048,64]{2,1,0:T(8,128)(2,1)S(1)} %copy-done.18, ...), kind=kOutput, calls=%fused_computation.57.clone.1 | convolution fusion | flops 651163648 | bytes 38906880 | tf_op jit(solution)/shard_map/while/body/eval_jaxpr/dot_general | solution.py:53
  800.1 12.6 %multiply_convert_fusion.7 = bf16[2048,2304]{1,0:T(8,128)(2,1)S(1)} fusion(f32[2048,2304]{1,0:T(8,128)} %get-tuple-element.736, f32[2048,2304]{1,0:T(8,128)} %fusion.284, f32[2048]{0:T(1024)S(1)} %get-tuple-element.737), kind=kLoop, calls=%fused_computation.56.clone.1 | loop fusion | flops 14155776 | bytes 47194112 | tf_op jit(solution)/shard_map/while/body/eval_jaxpr/convert_element_type | solution.py:86
  864.9 10.8 scatter_custom_fusion.3
  885.5 15.3 %all-reduce.4 = (bf16[768]{0:T(1024)(128)(2,1)S(1)}, bf16[768]{0:T(1024)(128)(2,1)S(1)}, bf16[768]{0:T(1024)(128)(2,1)S(1)}) all-reduce(f32[768]{0:T(1024)S(1)} %get-tuple-element.357, f32[768]{0:T(1024)S(1)} %copy-done.80, f32[768]{0:T(1024)S(1)} %convolution_reduce_fusion), channel_id=1, replica_groups=mesh['branch'=4,'dp'=8] {'branch'}, use_global_device_ids=true, to_apply=%region_30.31 | all-reduce | flops 2304 | bytes 13824 | tf_op jit(solution)/shard_map/psum | solution.py:285
  900.8 16.8 %all-reduce.5 = (bf16[768]{0:T(1024)(128)(2,1)S(1)}, bf16[768]{0:T(1024)(128)(2,1)S(1)}, bf16[768]{0:T(1024)(128)(2,1)S(1)}) all-reduce(bf16[768]{0:T(1024)(128)(2,1)S(1)} %get-tuple-element.439, bf16[768]{0:T(1024)(128)(2,1)S(1)} %get-tuple-element.440, ...), channel_id=1, replica_groups=mesh['branch'=4,'dp'=8] {'dp'}, use_global_device_ids=true, to_apply=%region_31.32 | all-reduce | flops 2304 | bytes 9216 | tf_op jit(solution)/shard_map/psum | solution.py:294
  919.4 107.9 %all-reduce.21.cloned.1.call-done = (bf16[768,2,256]{2,0,1:T(8,128)(2,1)}, bf16[768,2,1024]{2,0,1:T(8,128)(2,1)}, bf16[768,3,128]{2,0,1:T(8,128)(2,1)}, bf16[128...) async-done(((bf16[768,2,256]{2,0,1:T(8,128)(2,1)}, ...) | async-done | bytes 7864336 | tf_op jit(solution)/shard_map/psum | solution.py:296
  1045.3 124.3 %all-reduce.19.cloned.1.call-done = f32[2048,768]{1,0:T(8,128)} async-done(((f32[2048,768]{1,0:T(8,128)}), f32[2048,768]{1,0:T(8,128)}) %all-reduce.19.cloned.1.call-update) | async-done | bytes 6291472 | tf_op jit(solution)/shard_map/psum | solution.py:285
  1169.6 8.2 add.233
  (427 shorter events, 356.8 us)
Async XLA Ops:
  7.2 339.4 %copy-start = (bf16[768,2,1024]{2,1,0:T(2,128)(2,1)S(1)}, bf16[768,2,1024]{2,1,0:T(2,128)(2,1)}, u32[]{:S(2)}) copy-start(bf16[768,2,1024]{2,1,0:T(2,128)(2,1)} %param.38) | copy-start | bytes 9437188
  7.2 113.9 %all-gather.2.cloned.1.call-start = ((), (), s32[]{:S(2)}) async-start(), calls=%async_computation.1 | async-start | bytes 3538944 | tf_op jit(solution)/shard_map/all_gather | solution.py:180
  23.4 295.4 %all-reduce.13.cloned.1.call-start = ((), (), s32[]{:S(2)}) async-start(), calls=%async_computation.2 | async-start | bytes 12582912 | tf_op jit(solution)/shard_map/psum | solution.py:191
  29.0 10.2 copy-start.98
  29.0 10.9 copy-start.81
  31.1 16.4 %collective-permute-start = (bf16[128,2,128]{0,2,1:T(8,128)(2,1)}, bf16[128,2,128]{0,2,1:T(8,128)(2,1)S(1)}, u32[]{:S(2)}, u32[]{:S(2)}) collective-permute-start(bf16[128,2,128]{0,2,1:T(8,128)(2,1)} %get-tuple-element.475), channel_id=1, source_target_pairs={{0,1},{1,2},{2,3},{3,4},{4,5},{5,6},{6,7},{8,9},{9,10},{10,11},{11... | collective-permute-start | bytes 196616 | tf_op jit(solution)/shard_map/ppermute | solution.py:23
  33.4 14.1 %collective-permute-start.1 = (bf16[128,2,128]{0,2,1:T(8,128)(2,1)}, bf16[128,2,128]{0,2,1:T(8,128)(2,1)S(1)}, u32[]{:S(2)}, u32[]{:S(2)}) collective-permute-start(bf16[128,2,128]{0,2,1:T(8,128)(2,1)} %get-tuple-element.476), channel_id=1, source_target_pairs={{1,0},{2,1},{3,2},{4,3},{5,4},{6,5},{7,6},{9,8},{10,9},{11,10},{12... | collective-permute-start | bytes 196616 | tf_op jit(solution)/shard_map/ppermute | solution.py:25
  54.5 61.7 %copy-start.47 = (bf16[128,768]{1,0:T(8,128)(2,1)S(1)}, bf16[128,768]{1,0:T(8,128)(2,1)}, u32[]{:S(2)}) copy-start(bf16[128,768]{1,0:T(8,128)(2,1)} %param.33) | copy-start | bytes 589828
  133.3 31.8 %copy-start.75 = (f32[512]{0:T(512)S(1)}, f32[512]{0:T(512)}, u32[]{:S(2)}) copy-start(f32[512]{0:T(512)} %add_divide_fusion) | copy-start | bytes 6148
  133.3 31.8 %copy-start.83 = (pred[512]{0:T(512)(128)(4,1)S(1)}, pred[512]{0:T(512)(128)(4,1)}, u32[]{:S(2)}) copy-start(pred[512]{0:T(512)(128)(4,1)} %iota_compare_fusion.1) | copy-start | bytes 1540
  175.8 282.3 %all-reduce.15.cloned.1.call-start = ((), (), s32[]{:S(2)}) async-start(), calls=%async_computation.3 | async-start | bytes 6291456 | tf_op jit(solution)/shard_map/psum | solution.py:209
  187.0 139.1 %copy-start.69 = (f32[768]{0:T(1024)S(1)}, f32[768]{0:T(1024)}, u32[]{:S(2)}) copy-start(f32[768]{0:T(1024)} %param.30) | copy-start | bytes 9220
  370.8 236.1 %all-reduce.17.cloned.1.call-start = ((), (), s32[]{:S(2)}) async-start(), calls=%async_computation.4 | async-start | bytes 12582912 | tf_op jit(solution)/shard_map/psum | solution.py:219
  468.3 383.6 %reduce-scatter.2.cloned.1.call-start = ((), (), s32[]{:S(2)}) async-start(), calls=%async_computation.5 | async-start | bytes 3538944 | tf_op jit(solution)/shard_map/reduce_scatter | solution.py:263
  483.1 130.8 %copy-start.48 = (bf16[128,768]{1,0:T(8,128)(2,1)S(1)}, bf16[128,768]{1,0:T(8,128)(2,1)}, u32[]{:S(2)}) copy-start(bf16[128,768]{1,0:T(8,128)(2,1)} %param.33) | copy-start | bytes 589828
  622.5 7.8 copy-start.5
  639.4 10.1 copy-start.34
  667.2 10.1 copy-start.34
  695.0 10.1 copy-start.34
  717.7 309.6 %all-reduce.21.cloned.1.call-start = ((), (), s32[]{:S(2)}) async-start(), calls=%async_computation.7 | async-start | bytes 15728640 | tf_op jit(solution)/shard_map/psum | solution.py:296
  719.6 9.1 copy-start.18
  746.5 13.0 %copy-start.38 = (f32[2,2304,64]{1,2,0:T(8,128)S(1)}, f32[2,2304,64]{1,2,0:T(8,128)}, u32[]{:S(2)}) copy-start(f32[2,2304,64]{1,2,0:T(8,128)} %get-tuple-element.824) | copy-start | bytes 3538948 | tf_op jit(solution)/shard_map/while
  773.6 9.0 copy-start.18
  800.1 12.6 %copy-start.38 = (f32[2,2304,64]{1,2,0:T(8,128)S(1)}, f32[2,2304,64]{1,2,0:T(8,128)}, u32[]{:S(2)}) copy-start(f32[2,2304,64]{1,2,0:T(8,128)} %get-tuple-element.824) | copy-start | bytes 3538948 | tf_op jit(solution)/shard_map/while
  830.9 12.3 %collective-permute-start.2 = (bf16[128,2,128]{2,0,1:T(8,128)(2,1)S(1)}, bf16[128,2,128]{2,0,1:T(8,128)(2,1)S(1)}, u32[]{:S(2)}, u32[]{:S(2)}) collective-permute-start(bf16[128,2,128]{2,0,1:T(8,128)(2,1)S(1)} %get-tuple-element.477), channel_id=1, source_target_pairs={{0,1},{1,2},{2,3},{3,4},{4,5},{5,6},{6,7},{8,9},{9,10},{10,11},{11... | collective-permute-start | bytes 196616 | tf_op jit(solution)/shard_map/ppermute | solution.py:23
  832.9 10.3 collective-permute-start.3
  855.8 313.8 %all-reduce.19.cloned.1.call-start = ((), (), s32[]{:S(2)}) async-start(), calls=%async_computation.6 | async-start | bytes 12582912 | tf_op jit(solution)/shard_map/psum | solution.py:285
  864.9 10.8 copy-start.8
  864.9 10.8 copy-start.62
  864.9 10.8 copy-start.71
  1027.3 7.7 copy-start.52
  1169.6 8.3 copy-start.1
  (103 other events, 325.4 us)
Sparse Core Ops, SparseCore 0:
  23.5 41.6 all-gather.1
  175.9 142.9 all-reduce.12
  370.9 87.0 all-reduce.14
  468.4 138.4 all-reduce.16
  717.9 40.3 reduce-scatter.1
  855.9 171.3 all-reduce.20
  1031.0 138.5 all-reduce.18
where the time goes:
time: 1190 us
  waiting for transfers between devices  548 us (46%)
  matrix products  267 us (22%)
  other arithmetic  213 us (18%)
  local copies, waits for them, and re-layouts  101 us (8%)
  blocking collectives  32.1 us (3%)
  between operations  15.5 us (1%)
    psum x1, waiting for transfers between devices, per_device(): lax.psum(local_attn + jnp.zeros_like(local_attn).at[routed_slots].add(att...  132 us
    psum x1, waiting for transfers between devices, per_device(): lax.psum((tokens_part, gain_before_part, router_part), 'branch')  124 us
    psum x1, waiting for transfers between devices, per_device(): lax.psum((middle_part, gain_middle_part), 'branch')  124 us
    psum x1, waiting for transfers between devices, per_device(): lax.psum(delta_local_expand.astype(jnp.bfloat16), 'dp').astype(jnp.float32)  108 us
    dot_general x10, matrix products, head_scores(): jnp.dot(query_one, key_one.T, preferred_element_type=jnp.float32)  85.3 us
    psum x1, waiting for transfers between devices, per_device(): lax.psum((local_ff + jnp.zeros_like(local_ff).at[routed_slots].add(ff_row...  59.9 us
    convert_element_type x5, other arithmetic, one_head(): grad_scores = (weights * (grad_weights - inner_sum)).astype(jnp.bfloat16)  55.9 us
    dot_general x5, matrix products, one_head(): jnp.dot(rounded_weights, value_one, preferred_element_type=jnp.float32)  30.9 us
  transfers between devices with their start and end apart: 11, of which 5 were waited for; matrix products, arithmetic and copies ran while one was open for 27% of the time, Pallas kernels for 0%

commit v1 on v0

v1 whole, which is shorter than its diff:
```python
import jax
import jax.numpy as jnp
from jax import lax
from jax.sharding import Mesh
from jax.sharding import PartitionSpec as P

DH = 64
WIN = 128
EPSILON = 1e-06
NEGATIVE = -1e30
HIGHEST = lax.Precision.HIGHEST
F32 = jnp.float32
BF16 = jnp.bfloat16
SCALE = DH ** (-0.5)
DP = ("zz", "core")
GROUP = ("branch", "core")


def mm(a, b, ca, cb):
    return lax.dot_general(a, b, (((ca,), (cb,)), ((), ())), preferred_element_type=F32)


def norm_parts(values):
    r = lax.rsqrt(jnp.mean(values * values, axis=-1, keepdims=True) + EPSILON)
    return r, values * r


def norm_back(dn, xh, r, gain):
    g = dn * gain
    return r * (g - xh * jnp.mean(g * xh, axis=-1, keepdims=True))


def gelu_parts(u):
    c = 0.7978845608028654
    t = jnp.tanh(c * (u + 0.044715 * u * u * u))
    g = 0.5 * u * (1.0 + t)
    dg = 0.5 * (1.0 + t) + 0.5 * u * (1.0 - t * t) * c * (1.0 + 3 * 0.044715 * u * u)
    return g, dg


def feed(n, seed, w_gate, w_up, w_down):
    u = mm(n, w_gate, 1, 0)
    v = mm(n, w_up, 1, 0)
    g, dg = gelu_parts(u)
    hidden = (g * v).astype(BF16)
    out = mm(hidden, w_down, 1, 0)
    dh = mm(seed, w_down, 1, 1)
    du = (dh * v * dg).astype(BF16)
    dv = (dh * g).astype(BF16)
    dn = mm(du, w_gate, 1, 1) + mm(dv, w_up, 1, 1)
    dwg = mm(n, du, 0, 0)
    dwu = mm(n, dv, 0, 0)
    dwd = mm(hidden, seed, 0, 0)
    return out, dn, dwg, dwu, dwd


def windows(x, count):
    return jnp.stack([x[i * WIN : (i + 3) * WIN] for i in range(count)], 0)


def local_scores(q4, kw, allowed):
    s = jnp.einsum("nqhe,nkhe->nhqk", q4, kw, preferred_element_type=F32) * SCALE
    return jnp.where(allowed[:, None], s, NEGATIVE)


def per_device(
    tokens,
    cotangent,
    gain_before,
    gain_middle,
    router_vector,
    local_heads,
    local_merge,
    routed_heads,
    routed_merge,
    local_expand,
    local_reduce,
    routed_expand,
    routed_reduce,
    routed_slots,
    routed_counts,
):
    nb = lax.axis_size("branch")
    nz = lax.axis_size("zz")
    ndp = 2 * nz
    b = lax.axis_index("branch")
    z = lax.axis_index("zz")
    core = lax.axis_index("core")
    d = 2 * z + core
    rows, D = tokens.shape
    own = rows // nb
    cap = routed_slots.shape[0]
    half = cap // 2
    hl = local_heads.shape[2]
    fl = local_expand.shape[2]
    fh = routed_expand.shape[2] // 2
    rw = routed_heads.shape[2]
    heads_l = nb * hl // DH
    heads_r = rw // DH
    blocks = own // WIN

    lh = lax.all_gather(local_heads.transpose(1, 0, 2), "branch")
    lm = lax.all_gather(local_merge, "branch", axis=0, tiled=True)
    le = lax.all_gather(local_expand.transpose(1, 0, 2), "branch")
    lr = lax.all_gather(local_reduce, "branch", axis=0, tiled=True)
    lh3 = lh.transpose(1, 2, 0, 3).reshape(3, D, nb * hl)
    le2 = le.transpose(1, 2, 0, 3).reshape(2, D, nb * fl)

    n_own = routed_counts[d]
    offset = jnp.where(core == 0, 0, cap - n_own)
    ranks = jnp.arange(cap, dtype=jnp.int32)
    live = (ranks >= offset) & (ranks < offset + n_own)
    rolled = jnp.take(routed_slots, jnp.mod(ranks - offset, cap), axis=0)
    ids = jnp.where(live, rolled, -1)
    pick = (ids[:, None] == jnp.arange(rows, dtype=jnp.int32)[None, :]).astype(BF16)
    pick_own = lax.dynamic_slice(pick, (0, b * own), (cap, own))
    mask_own = (jnp.sum(pick_own.astype(F32), 0) > 0.5)[:, None]

    pair_rows = mm(pick, jnp.concatenate([tokens, cotangent], 1), 1, 0).astype(BF16)
    pair_rows = lax.psum(pair_rows, "core").astype(F32)
    tok_r, cot_r = pair_rows[:, :D], pair_rows[:, D:]
    r1r, xh1r = norm_parts(tok_r)
    first_r = (xh1r * gain_before).astype(BF16)
    gate = jax.nn.sigmoid(jnp.dot(first_r.astype(F32), router_vector, precision=HIGHEST))[:, None]
    first_half = lax.dynamic_slice(first_r, (core * half, 0), (half, D))
    gate_half = lax.dynamic_slice(gate, (core * half, 0), (half, 1))
    proj_r = jnp.einsum("rd,dcf->rcf", first_half, routed_heads, preferred_element_type=F32).astype(BF16)
    kv = lax.all_gather(
        jnp.concatenate([proj_r[:, 1], proj_r[:, 2]], 1), DP, axis=0, tiled=True
    )

    perm_up = [(i, i + 1) for i in range(ndp - 1)]
    perm_down = [(i + 1, i) for i in range(ndp - 1)]
    before = lax.ppermute(tokens[rows - WIN :], DP, perm_up)
    after = lax.ppermute(tokens[:WIN], DP, perm_down)
    wide = jnp.concatenate([before, tokens, after], 0)
    wide_own = lax.dynamic_slice(wide, (b * own, 0), (own + 2 * WIN, D)).astype(F32)
    cot_own = lax.dynamic_slice(cotangent, (b * own, 0), (own, D))
    r1w, xh1w = norm_parts(wide_own)
    first_w = (xh1w * gain_before).astype(BF16)
    first_own = first_w[WIN : WIN + own]
    tok_own, r1, xh1 = (v[WIN : WIN + own] for v in (wide_own, r1w, xh1w))

    q = mm(first_own, lh3[0], 1, 0).astype(BF16)
    k = mm(first_w, lh3[1], 1, 0).astype(BF16)
    v = mm(first_w, lh3[2], 1, 0).astype(BF16)
    q4 = q.reshape(blocks, WIN, heads_l, DH)
    kw = windows(k.reshape(-1, heads_l, DH), blocks)
    vw = windows(v.reshape(-1, heads_l, DH), blocks)
    qpos = jnp.arange(WIN, dtype=jnp.int32)
    kpos = jnp.arange(3 * WIN, dtype=jnp.int32)
    near = jnp.abs(qpos[:, None] + WIN - kpos[None, :]) <= WIN
    first_key = d * rows + b * own - WIN + jnp.arange(blocks, dtype=jnp.int32)[:, None] * WIN + kpos[None, :]
    inside = (first_key >= 0) & (first_key < ndp * rows)
    allowed = near[None] & inside[:, None, :]
    s = local_scores(q4, kw, allowed)
    peak = jnp.max(s, -1, keepdims=True)
    w = jnp.exp(s - peak)
    tot = jnp.sum(w, -1, keepdims=True)
    lse_l = peak + jnp.log(tot)
    probs = (w / tot).astype(BF16)
    ctx_l = jnp.einsum("nhqk,nkhe->nqhe", probs, vw, preferred_element_type=F32).astype(BF16)
    ctx_l = ctx_l.reshape(own, heads_l * DH)
    local_attn = mm(ctx_l, lm, 1, 0)

    qr = proj_r[:, 0].reshape(half, heads_r, DH)
    kr = kv[:, :rw].reshape(-1, heads_r, DH)
    vr = kv[:, rw:].reshape(-1, heads_r, DH)
    sr = jnp.einsum("qhe,khe->hqk", qr, kr, preferred_element_type=F32) * SCALE
    peak_r = jnp.max(sr, -1, keepdims=True)
    wr = jnp.exp(sr - peak_r)
    tot_r = jnp.sum(wr, -1, keepdims=True)
    lse_r = peak_r + jnp.log(tot_r)
    ctx_r = jnp.einsum("hqk,khe->qhe", (wr / tot_r).astype(BF16), vr, preferred_element_type=F32)
    ctx_r = ctx_r.astype(BF16).reshape(half, rw)
    attn_r = mm(ctx_r, routed_merge, 1, 0)

    def at_half(x):
        return lax.dynamic_update_slice(jnp.zeros((cap, x.shape[1]), x.dtype), x, (core * half, 0))

    part = mm(pick_own, local_attn.astype(BF16), 1, 0) + at_half(gate_half * attn_r)
    mixed_r = lax.psum(part.astype(BF16), GROUP)
    mixed_own = jnp.where(mask_own, mm(pick_own, mixed_r, 0, 0), local_attn)
    middle_own = tok_own + mixed_own
    middle_r = tok_r + mixed_r.astype(F32)
    r2, xh2 = norm_parts(middle_own)
    second_own = (xh2 * gain_middle).astype(BF16)
    r2r, xh2r = norm_parts(middle_r)
    second_r = (xh2r * gain_middle).astype(BF16)

    ff_l, dn_l, d_lg, d_lu, d_ld = feed(second_own, cot_own, le2[0], le2[1], lr)
    re_half = lax.dynamic_slice(routed_expand, (0, 0, core * fh), (D, 2, fh))
    rr_half = lax.dynamic_slice(routed_reduce, (core * fh, 0), (fh, D))
    seed_r = (gate * cot_r).astype(BF16)
    ff_r, dn_r, d_rg, d_ru, d_rd = feed(second_r, seed_r, re_half[:, 0], re_half[:, 1], rr_half)
    gate_feed = jnp.sum(cot_r * ff_r, -1, keepdims=True)

    both = jnp.concatenate(
        [ff_r.astype(BF16), (dn_r + mm(pick_own, dn_l.astype(BF16), 1, 0)).astype(BF16)], 1
    )
    both = lax.psum(both, GROUP)
    ffr_sum, dn2_r = both[:, :D].astype(F32), both[:, D:]
    layer_own = (
        middle_own + ff_l + mm(pick_own, (gate * ffr_sum).astype(BF16), 0, 0)
    ).astype(BF16)
    layer_output = lax.all_gather(layer_own, "branch", axis=0, tiled=True).astype(F32)

    dn2_own = jnp.where(mask_own, mm(pick_own, dn2_r, 0, 0), dn_l)
    gm_own = cot_own.astype(F32) + norm_back(dn2_own, xh2, r2, gain_middle)
    gm_r = cot_r + norm_back(dn2_r.astype(F32), xh2r, r2r, gain_middle)
    delta_gain_middle = jnp.sum(dn2_own * xh2, 0)

    gm_low = gm_own.astype(BF16)
    dctx = mm(gm_low, lm, 1, 1).astype(BF16)
    d_lm = mm(ctx_l, gm_low, 0, 0)
    do4 = dctx.reshape(blocks, WIN, heads_l, DH)
    p = jnp.exp(local_scores(q4, kw, allowed) - lse_l)
    dp_ = jnp.einsum("nqhe,nkhe->nhqk", do4, vw, preferred_element_type=F32)
    inner = jnp.sum(p * dp_, -1, keepdims=True)
    ds = (p * (dp_ - inner)).astype(BF16)
    dq = jnp.einsum("nhqk,nkhe->nqhe", ds, kw, preferred_element_type=F32) * SCALE
    dkw = jnp.einsum("nhqk,nqhe->nkhe", ds, q4, preferred_element_type=F32) * SCALE
    dvw = jnp.einsum("nhqk,nqhe->nkhe", p.astype(BF16), do4, preferred_element_type=F32)
    dkv = jnp.concatenate(
        [dkw.reshape(blocks, 3 * WIN, -1), dvw.reshape(blocks, 3 * WIN, -1)], 2
    )
    ext = jnp.zeros((own + 2 * WIN, dkv.shape[2]), F32)
    for i in range(blocks):
        ext = ext.at[i * WIN : (i + 3) * WIN].add(dkv[i])
    total_dev = nb * ndp
    place = [(i % nb) * ndp + i // nb for i in range(total_dev)]
    up = [(place[i], place[i + 1]) for i in range(total_dev - 1)]
    down = [(place[i + 1], place[i]) for i in range(total_dev - 1)]
    everyone = ("branch",) + DP
    from_prev = lax.ppermute(ext[own + WIN :].astype(BF16), everyone, up).astype(F32)
    from_next = lax.ppermute(ext[:WIN].astype(BF16), everyone, down).astype(F32)
    dkv_own = ext[WIN : WIN + own].at[:WIN].add(from_prev).at[own - WIN :].add(from_next)
    dkv_own = dkv_own.astype(BF16)
    wl = heads_l * DH
    dq_own = dq.reshape(own, wl).astype(BF16)
    dk_own, dv_own = dkv_own[:, :wl], dkv_own[:, wl:]
    gf_l = mm(dq_own, lh3[0], 1, 1) + mm(dk_own, lh3[1], 1, 1) + mm(dv_own, lh3[2], 1, 1)
    d_lh = jnp.stack([mm(first_own, x, 0, 0) for x in (dq_own, dk_own, dv_own)], 0)

    gm_half = lax.dynamic_slice(gm_r, (core * half, 0), (half, D))
    seed_a = (gate_half * gm_half).astype(BF16)
    dctx_r = mm(seed_a, routed_merge, 1, 1).astype(BF16).reshape(half, heads_r, DH)
    d_rm = mm(ctx_r, seed_a, 0, 0)
    gate_attn = jnp.sum(gm_half * attn_r, -1, keepdims=True)
    pr = jnp.exp(sr - lse_r)
    dpr = jnp.einsum("qhe,khe->hqk", dctx_r, vr, preferred_element_type=F32)
    inner_r = jnp.sum(pr * dpr, -1, keepdims=True)
    dsr = (pr * (dpr - inner_r)).astype(BF16)
    dqr = jnp.einsum("hqk,khe->qhe", dsr, kr, preferred_element_type=F32) * SCALE
    dkr = jnp.einsum("hqk,qhe->khe", dsr, qr, preferred_element_type=F32) * SCALE
    dvr = jnp.einsum("hqk,qhe->khe", pr.astype(BF16), dctx_r, preferred_element_type=F32)
    dkvr = jnp.concatenate([dkr.reshape(-1, rw), dvr.reshape(-1, rw)], 1).astype(BF16)
    dkvr = lax.psum_scatter(dkvr, DP, scatter_dimension=0, tiled=True)
    triple = jnp.stack([dqr.reshape(half, rw).astype(BF16), dkvr[:, :rw], dkvr[:, rw:]], 1)
    picked = jnp.einsum("rcf,dcf->rd", triple, routed_heads, preferred_element_type=F32)
    d_rh = jnp.einsum("rd,rcf->dcf", first_half, triple, preferred_element_type=F32)
    d_logit = (at_half(gate_attn) + gate_feed) * gate * (1.0 - gate)
    router_part = jnp.sum(d_logit * first_r.astype(F32), 0)

    part3 = at_half(picked) + d_logit * router_vector[None, :] + mm(pick_own, gf_l.astype(BF16), 1, 0)
    gf_r = lax.psum(part3.astype(BF16), GROUP)
    gf_own = jnp.where(mask_own, mm(pick_own, gf_r, 0, 0), gf_l)
    td_own = (gm_own + norm_back(gf_own, xh1, r1, gain_before)).astype(BF16)
    delta_gain_before = jnp.sum(gf_own * xh1, 0)
    tokens_delta = lax.all_gather(td_own, "branch", axis=0, tiled=True).astype(F32)

    vectors = lax.psum(
        jnp.stack([delta_gain_before, delta_gain_middle, router_part]).astype(F32),
        ("branch",) + DP,
    )

    def over_branch(x, dim):
        return lax.psum_scatter(x.astype(BF16), "branch", scatter_dimension=dim, tiled=True)

    g_le = lax.psum(over_branch(jnp.stack([d_lg, d_lu], 0), 2), DP)
    g_lr = lax.psum(over_branch(d_ld, 0), DP)
    g_lh = lax.psum(over_branch(d_lh, 2), DP)
    g_lm = lax.psum(over_branch(d_lm, 0), DP)
    g_re = lax.all_gather(
        lax.psum(jnp.stack([d_rg, d_ru], 0).astype(BF16), "zz"), "core", axis=2, tiled=True
    )
    g_rr = lax.all_gather(lax.psum(d_rd.astype(BF16), "zz"), "core", axis=0, tiled=True)
    g_rh = lax.psum(d_rh.astype(BF16), DP)
    g_rm = lax.psum(d_rm.astype(BF16), DP)
    return (
        layer_output,
        tokens_delta,
        vectors[0],
        vectors[1],
        vectors[2],
        g_lh.transpose(1, 0, 2).astype(F32),
        g_lm.astype(F32),
        g_rh.astype(F32),
        g_rm.astype(F32),
        g_le.transpose(1, 0, 2).astype(F32),
        g_lr.astype(F32),
        g_re.transpose(1, 0, 2).astype(F32),
        g_rr.astype(F32),
    )


def solution(mesh):
    nb = mesh.shape["branch"]
    fine = Mesh(mesh.devices.reshape(nb, -1, 2), ("branch", "zz", "core"))
    rows = P(DP, None)
    cols = P(None, None, "branch")
    deep = P("branch", None)
    return jax.shard_map(
        per_device,
        mesh=fine,
        in_specs=(
            rows, rows, P(), P(), P(), cols, deep, cols, deep, cols, deep, cols, deep, P(DP), P(),
        ),
        out_specs=(
            rows, rows, P(), P(), P(), cols, deep, cols, deep, cols, deep, cols, deep,
        ),
        check_vma=False,
    )
```

time: 1190 us -> 699 us (0.59)
  waiting for transfers between devices: 548 us -> 356 us
  matrix products: 267 us -> 99.4 us
  other arithmetic: 213 us -> 60.8 us
  blocking collectives: 32.1 us -> 55.4 us
  local copies, waits for them, and re-layouts: 101 us -> 88 us
    psum x5 -> x6, waiting for transfers between devices: 548 us -> 206 us  [the longest x1 54.6 us: per_device(): both = lax.psum(both, GROUP)]
    dot_general x58 -> x55, matrix products: 259 us -> 98.6 us  [the longest x41 76.3 us: mm(): lax.dot_general(a, b, (((ca,), (cb,)), ((), ())), preferred_element_type=...]
    reduce_scatter x1 -> x4, waiting for transfers between devices: 0.01 us -> 95.4 us  [the longest x3 95.3 us: over_branch(): lax.psum_scatter(x.astype(BF16), 'branch', scatter_dimension=dim, tiled=T...]
    convert_element_type x21 -> x20, other arithmetic: 82.6 us -> 35.1 us  [the longest x1 5.2 us: per_device(): lax.all_gather(td_own, 'branch', axis=0, tiled=True).astype(F32)]
    scatter-add x6 -> x4, other arithmetic: 46.1 us -> 0.85 us  [the longest x2 0.68 us: per_device(): ext = ext.at[i * WIN:(i + 3) * WIN].add(dkv[i])]
    all_gather x1 -> x8, waiting for transfers between devices: 0.02 us -> 44.3 us  [the longest x1 38.2 us: per_device(): lax.all_gather(td_own, 'branch', axis=0, tiled=True).astype(F32)]
    reduce_sum x10 -> x8, other arithmetic: 45.4 us -> 10.4 us  [the longest x3 4.11 us: norm_parts(): r = lax.rsqrt(jnp.mean(values * values, axis=-1, keepdims=True) + EPSILON)]
    slice x6 -> x19, local copies, waits for them, and re-layouts: 9.85 us -> 30.4 us  [the longest x3 8.96 us: per_device(): ff_l, dn_l, d_lg, d_lu, d_ld = feed(second_own, cot_own, le2[0], le2[1], lr)]
  transfers between devices with their start and end apart: 11 -> 23, of which waited for: 5 -> 12; matrix products, arithmetic and copies ran while one was open for 27% -> 26% of each run, Pallas kernels for 0% -> 0%
where the time goes in v1:
time: 699 us; the launch traced here: 689 us
  waiting for transfers between devices  356 us (51%)
  matrix products  99.4 us (14%)
  local copies, waits for them, and re-layouts  88 us (13%)
  other arithmetic  60.8 us (9%)
  blocking collectives  55.4 us (8%)
  between operations  19.3 us (3%)
  starting transfers between devices  10.8 us (2%)
    reduce_scatter x3, waiting for transfers between devices, over_branch(): lax.psum_scatter(x.astype(BF16), 'branch', scatter_dimension=dim, tiled=T...  95.3 us
    dot_general x41, matrix products, mm(): lax.dot_general(a, b, (((ca,), (cb,)), ((), ())), preferred_element_type=...  76.3 us
    psum x1, waiting for transfers between devices, per_device(): both = lax.psum(both, GROUP)  54.6 us
    psum x1, waiting for transfers between devices, per_device(): g_le = lax.psum(over_branch(jnp.stack([d_lg, d_lu], 0), 2), DP)  50.5 us
    unnamed x276, local copies, waits for them, and re-layouts  44 us
    psum x1, waiting for transfers between devices, per_device(): mixed_r = lax.psum(part.astype(BF16), GROUP)  43.8 us
    psum x1, blocking collectives, per_device(): lax.psum(jnp.stack([delta_gain_before, delta_gain_middle, router_part]).a...  40 us
    all_gather x1, waiting for transfers between devices, per_device(): lax.all_gather(td_own, 'branch', axis=0, tiled=True).astype(F32)  38.2 us
  transfers between devices with their start and end apart: 23, of which 12 were waited for; matrix products, arithmetic and copies ran while one was open for 26% of the time, Pallas kernels for 0%

profile of v1, /device:TPU:0, one launch (start us, length us, event | category | flops | bytes accessed | tf_op | source)
XLA Modules:
  0.0 689.3 jit_solution(11196961993233400131)
XLA Ops:
  10.8 3.6 gather_fusion
  14.4 7.5 %fusion.17 = bf16[512,1536]{1,0:T(8,128)(2,1)} fusion(bf16[2048,768]{1,0:T(8,128)(2,1)} %param.28, bf16[2048,768]{1,0:T(8,128)(2,1)} %param.27, s32[512]{0:T(512)S(1)} %select_select_fusion), kind=kOutput, calls=%fused_computation.42 | convolution fusion | flops 3235643392 | bytes 7866368 | tf_op jit(solution)/shard_map/dot_general | solution.py:20
  22.5 22.6 %all-reduce.10.cloned.1.call-done = bf16[512,1536]{1,0:T(8,128)(2,1)} async-done(((bf16[512,1536]{1,0:T(8,128)(2,1)}), bf16[512,1536]{1,0:T(8,128)(2,1)}) %all-reduce.10.cloned.1.call-update) | async-done | bytes 1572880 | tf_op jit(solution)/shard_map/psum | solution.py:120
  53.3 3.7 collective-permute-start
  59.7 15.4 %all_gather.35 = bf16[512,768]{1,0:T(8,128)(2,1)} all-gather(bf16[128,768]{1,0:T(8,128)(2,1)} %param.33), channel_id=1, replica_groups=mesh['branch'=4,'zz'=4,'core'=2] {'branch'}, dimensions={0}, use_global_device_ids=true | all-gather | bytes 983040 | tf_op jit(solution)/shard_map/all_gather | solution.py:103
  82.0 2.9 fusion.141
  109.6 2.7 fusion.75
  123.9 7.5 %constant_dynamic-slice_fusion = (bf16[768,1,512]{2,1,0:T(2,128)(2,1)}, bf16[768,1,512]{2,1,0:T(2,128)(2,1)}) fusion(bf16[768,2,1024]{2,1,0:T(2,128)(2,1)} %param.38, s32[]{:T(128)S(6)} %add.388, s32[]{:T(128)S(6)} %select_n.110), kind=kLoop, calls=%fused_computation.244 | loop fusion | bytes 3145736 | tf_op jit(solution)/shard_map/slice | solution.py:195
  133.1 6.0 all-gather.25.cloned.1.call-done
  139.1 3.8 fusion.139
  148.1 43.8 %all-reduce.12.cloned.1.call-done = bf16[512,768]{1,0:T(8,128)(2,1)} async-done(((bf16[512,768]{1,0:T(8,128)(2,1)}), bf16[512,768]{1,0:T(8,128)(2,1)}) %all-reduce.12.cloned.1.call-update) | async-done | bytes 786448 | tf_op jit(solution)/shard_map/psum | solution.py:182
  203.8 6.2 multiply_convert_fusion.3
  225.3 54.6 %all-reduce.14.cloned.1.call-done = bf16[512,1536]{1,0:T(8,128)(2,1)} async-done(((bf16[512,1536]{1,0:T(8,128)(2,1)}), bf16[512,1536]{1,0:T(8,128)(2,1)}) %all-reduce.14.cloned.1.call-update) | async-done | bytes 1572880 | tf_op jit(solution)/shard_map/psum | solution.py:201
  280.0 5.8 multiply_reduce_fusion.5
  311.8 4.6 multiply_reduce_fusion
  328.9 7.6 %collective-permute-done.3 = bf16[128,1024]{0,1:T(8,128)(2,1)S(1)} collective-permute-done((bf16[128,1024]{0,1:T(8,128)(2,1)S(1)}, bf16[128,1024]{0,1:T(8,128)(2,1)S(1)}, u32[]{:S(2)}, u32[]{:S(2)}) %collective-permute-start.3) | collective-permute-done | bytes 262176 | tf_op jit(solution)/shard_map/ppermute | solution.py:236
  340.0 4.6 copy.96
  349.7 3.4 convolution_convert_fusion
  372.3 34.6 %all-reduce.20.cloned.1.call-done = (bf16[2,768,512]{2,1,0:T(8,128)(2,1)}, bf16[512,768]{1,0:T(8,128)(2,1)}) async-done(((bf16[2,768,512]{2,1,0:T(8,128)(2,1)}, bf16[512,768]{1,0:T(8,128)(2,1)}), (bf16[2,768,512]{2,1,0:T(8,128)(2,1)}, bf16[512,768]{1,0:T(8,128)(2,1)})) %all-reduce.20.cloned.1.call-update) | async-done | bytes 2359312 | tf_op jit(solution)/shard_map/psum | solution.py:285
  407.7 2.8 fusion.150
  410.6 2.7 add_convert_fusion.2
  419.6 12.6 %reduce-scatter.10.cloned.1.call-done = bf16[128,768]{1,0:T(8,128)(2,1)} async-done(((bf16[512,768]{1,0:T(8,128)(2,1)}), bf16[128,768]{1,0:T(8,128)(2,1)}) %reduce-scatter.10.cloned.1.call-update) | async-done | bytes 196624 | tf_op jit(solution)/shard_map/reduce_scatter | solution.py:278
  432.2 35.2 %reduce-scatter.14.cloned.1.call-done = bf16[256,768]{1,0:T(8,128)(2,1)} async-done(((bf16[1024,768]{1,0:T(8,128)(2,1)}), bf16[256,768]{1,0:T(8,128)(2,1)}) %reduce-scatter.14.cloned.1.call-update) | async-done | bytes 393232 | tf_op jit(solution)/shard_map/reduce_scatter | solution.py:278
  467.3 47.6 %reduce-scatter.12.cloned.1.call-done = bf16[2,768,256]{2,1,0:T(8,128)(2,1)} async-done(((bf16[2,768,1024]{2,1,0:T(8,128)(2,1)}), bf16[2,768,256]{2,1,0:T(8,128)(2,1)}) %reduce-scatter.12.cloned.1.call-update) | async-done | bytes 786448 | tf_op jit(solution)/shard_map/reduce_scatter | solution.py:278
  515.6 2.7 multiply_reduce_fusion.6
  519.9 3.3 convert_element_type.319
  523.2 40.0 %psum.95 = f32[3,768]{1,0:T(4,128)S(1)} all-reduce(f32[3,768]{1,0:T(4,128)S(1)} %pad_maximum_fusion.14), channel_id=1, replica_groups=mesh['branch'=4,'zz'=4,'core'=2] {'branch','zz','core'}, use_global_device_ids=true, to_apply=%region_24.25 | all-reduce | flops 2304 | bytes 18432 | tf_op jit(solution)/shard_map/psum | solution.py:272
  566.5 7.6 %copy.95 = f32[768,2,1024]{2,1,0:T(2,128)} copy(f32[768,2,1024]{2,0,1:T(8,128)S(1)} %convert_bitcast_fusion) | data formatting | bytes 12582912
  574.1 5.1 convert_element_type.279
  579.2 50.5 %all-reduce.18.cloned.1.call-done = (bf16[768,2,256]{2,0,1:T(8,128)(2,1)}, bf16[768,3,128]{2,0,1:T(8,128)(2,1)}, bf16[128,768]{1,0:T(8,128)(2,1)}, bf16[768,3,19...) async-done(((bf16[768,2,256]{2,0,1:T(8,128)(2,1)}, bf16[768,3,128]{2,0,1:T(8,128)(2,1)}, bf16[128,768]{1,0:T(8,128)(2,1)}, ...) | async-done | bytes 3145744 | tf_op jit(solution)/shard_map/psum | solution.py:280
  637.8 38.2 %all-gather.17.cloned.1.call-done = bf16[2048,768]{1,0:T(8,128)(2,1)} async-done(((bf16[512,768]{1,0:T(8,128)(2,1)}), bf16[2048,768]{1,0:T(8,128)(2,1)}) %all-gather.17.cloned.1.call-update) | async-done | bytes 3145744 | tf_op jit(solution)/shard_map/all_gather | solution.py:270
  676.1 5.2 convert_element_type.302
  (471 shorter events, 175.6 us)
Async XLA Ops:
  8.0 123.4 %copy-start = (bf16[1024,768]{1,0:T(8,128)(2,1)S(1)}, bf16[1024,768]{1,0:T(8,128)(2,1)}, u32[]{:S(2)}) copy-start(bf16[1024,768]{1,0:T(8,128)(2,1)} %param.39) | copy-start | bytes 4718596
  8.0 37.1 %all-reduce.10.cloned.1.call-start = ((), (), s32[]{:S(2)}) async-start(), calls=%async_computation.5 | async-start | bytes 3145728 | tf_op jit(solution)/shard_map/psum | solution.py:120
  21.9 60.1 %all-gather.23.cloned.1.call-start = ((), (), s32[]{:S(2)}) async-start(), calls=%async_computation.19 | async-start | bytes 2949120 | tf_op jit(solution)/shard_map/all_gather | solution.py:102
  22.5 89.8 %all-gather.11.cloned.1.call-start = ((), (), s32[]{:S(2)}) async-start(), calls=%async_computation.6 | async-start | bytes 1769472 | tf_op jit(solution)/shard_map/all_gather | solution.py:128
  48.8 31.5 %copy-start.24 = (bf16[512,768]{1,0:T(8,128)(2,1)}, bf16[512,768]{1,0:T(8,128)(2,1)S(1)}, u32[]{:S(2)}) copy-start(bf16[512,768]{1,0:T(8,128)(2,1)S(1)} %multiply_convert_fusion.9) | copy-start | bytes 2359300
  50.9 88.2 %all-gather.25.cloned.1.call-start = ((), (), s32[]{:S(2)}) async-start(), calls=%async_computation.20 | async-start | bytes 3932160 | tf_op jit(solution)/shard_map/all_gather | solution.py:104
  52.0 24.1 %collective-permute-start.1 = (bf16[128,768]{1,0:T(8,128)(2,1)S(1)}, bf16[128,768]{1,0:T(8,128)(2,1)}, u32[]{:S(2)}, u32[]{:S(2)}) collective-permute-start(bf16[128,768]{1,0:T(8,128)(2,1)S(1)} %get-tuple-element.184), channel_id=1, source_target_pairs={{1,0},{2,1},{3,2},{4,3},{5,4},{6,5},{7,6},{9,8},{10,9},{11,10},{12... | collective-permute-start | bytes 589832 | tf_op jit(solution)/shard_map/ppermute | solution.py:135
  53.3 22.8 %collective-permute-start = (bf16[128,768]{1,0:T(8,128)(2,1)S(1)}, bf16[128,768]{1,0:T(8,128)(2,1)}, u32[]{:S(2)}, u32[]{:S(2)}) collective-permute-start(bf16[128,768]{1,0:T(8,128)(2,1)S(1)} %get-tuple-element.183), channel_id=1, source_target_pairs={{0,1},{1,2},{2,3},{3,4},{4,5},{5,6},{6,7},{8,9},{9,10},{10,11},{11... | collective-permute-start | bytes 589832 | tf_op jit(solution)/shard_map/ppermute | solution.py:134
  58.0 17.4 %copy-start.111 = (f32[768]{0:T(1024)S(1)}, f32[768]{0:T(1024)}, u32[]{:S(2)}) copy-start(f32[768]{0:T(1024)} %param.31) | copy-start | bytes 9220
  58.0 133.8 %all-reduce.12.cloned.1.call-start = ((), (), s32[]{:S(2)}) async-start(), calls=%async_computation.7 | async-start | bytes 1572864 | tf_op jit(solution)/shard_map/psum | solution.py:182
  81.9 49.5 %copy-start.100 = (f32[512]{0:T(512)}, f32[512]{0:T(512)S(1)}, u32[]{:S(2)}) copy-start(f32[512]{0:T(512)S(1)} %get-tuple-element.169) | copy-start | bytes 6148
  82.0 37.5 %copy-start.114 = (f32[256]{0:T(256)}, f32[256]{0:T(256)S(1)}, u32[]{:S(2)}) copy-start(f32[256]{0:T(256)S(1)} %dynamic-slice.52) | copy-start | bytes 3076
  91.1 9.7 %copy-start.42 = (bf16[4,128,8,64]{1,3,2,0:T(8,128)(2,1)}, bf16[4,128,8,64]{1,3,2,0:T(8,128)(2,1)S(1)}, u32[]{:S(2)}) copy-start(bf16[4,128,8,64]{1,3,2,0:T(8,128)(2,1)S(1)} %copy.83) | copy-start | bytes 1572868
  121.8 82.1 %all-gather.13.cloned.1.call-start = ((), (), s32[]{:S(2)}) async-start(), calls=%async_computation.8 | async-start | bytes 1966080 | tf_op jit(solution)/shard_map/all_gather | solution.py:105
  122.5 157.5 %all-reduce.14.cloned.1.call-start = ((), (), s32[]{:S(2)}) async-start(), calls=%async_computation.9 | async-start | bytes 3145728 | tf_op jit(solution)/shard_map/psum | solution.py:201
  123.9 70.0 %copy-start.120 = (pred[512]{0:T(512)(128)(4,1)}, pred[512]{0:T(512)(128)(4,1)S(1)}, u32[]{:S(2)}) copy-start(pred[512]{0:T(512)(128)(4,1)S(1)} %broadcast_compare_fusion) | copy-start | bytes 1540
  196.4 83.6 %copy-start.104 = (f32[512]{0:T(512)}, f32[512]{0:T(512)S(1)}, u32[]{:S(2)}) copy-start(f32[512]{0:T(512)S(1)} %get-tuple-element.228) | copy-start | bytes 6148
  221.6 145.5 %reduce-scatter.8.cloned.1.call-start = ((), (), s32[]{:S(2)}) async-start(), calls=%async_computation.11 | async-start | bytes 1769472 | tf_op jit(solution)/shard_map/reduce_scatter | solution.py:258
  222.1 66.1 %slice-start = ((s8[6291456]{0:T(1024)(128)(4,1)}), s8[2097152]{0:T(1024)(128)(4,1)S(1)}, s32[]{:S(2)}) async-start(s8[6291456]{0:T(1024)(128)(4,1)} %bitcast.206), calls=%async_computation.24 | async-start | bytes 4194304
  295.9 110.9 %all-reduce.20.cloned.1.call-start = ((), (), s32[]{:S(2)}) async-start(), calls=%async_computation.23 | async-start | bytes 4718592 | tf_op jit(solution)/shard_map/psum | solution.py:285
  303.7 113.3 %reduce-scatter.16.cloned.1.call-start = ((), (), s32[]{:S(2)}) async-start(), calls=%async_computation.21 | async-start | bytes 2949120
  321.6 7.3 %collective-permute-start.2 = (bf16[128,1024]{0,1:T(8,128)(2,1)S(1)}, bf16[128,1024]{0,1:T(8,128)(2,1)S(1)}, u32[]{:S(2)}, u32[]{:S(2)}) collective-permute-start(bf16[128,1024]{0,1:T(8,128)(2,1)S(1)} %slice.456), channel_id=1, source_target_pairs={{0,8},{8,16},{16,24},{24,1},{1,9},{9,17},{17,25},{25,2},{2,10},{10... | collective-permute-start | bytes 786440 | tf_op jit(solution)/shard_map/ppermute | solution.py:235
  326.5 10.1 %collective-permute-start.3 = (bf16[128,1024]{0,1:T(8,128)(2,1)S(1)}, bf16[128,1024]{0,1:T(8,128)(2,1)S(1)}, u32[]{:S(2)}, u32[]{:S(2)}) collective-permute-start(bf16[128,1024]{0,1:T(8,128)(2,1)S(1)} %slice.455), channel_id=1, source_target_pairs={{8,0},{16,8},{24,16},{1,24},{9,1},{17,9},{25,17},{2,25},{10,2},{18... | collective-permute-start | bytes 786440 | tf_op jit(solution)/shard_map/ppermute | solution.py:236
  346.6 85.6 %reduce-scatter.10.cloned.1.call-start = ((), (), s32[]{:S(2)}) async-start(), calls=%async_computation.14 | async-start | bytes 983040 | tf_op jit(solution)/shard_map/reduce_scatter | solution.py:278
  349.6 117.8 %reduce-scatter.14.cloned.1.call-start = ((), (), s32[]{:S(2)}) async-start(), calls=%async_computation.16 | async-start | bytes 1966080 | tf_op jit(solution)/shard_map/reduce_scatter | solution.py:278
  353.1 161.8 %reduce-scatter.12.cloned.1.call-start = ((), (), s32[]{:S(2)}) async-start(), calls=%async_computation.15 | async-start | bytes 3932160 | tf_op jit(solution)/shard_map/reduce_scatter | solution.py:278
  358.2 157.3 %all-reduce.16.cloned.1.call-start = ((), (), s32[]{:S(2)}) async-start(), calls=%async_computation.12 | async-start | bytes 1572864 | tf_op jit(solution)/shard_map/psum | solution.py:266
  372.3 147.6 %all-gather.21.cloned.1.call-start = ((), (), s32[]{:S(2)}) async-start(), calls=%async_computation.18 | async-start | bytes 2359296 | tf_op jit(solution)/shard_map/all_gather | solution.py:287
  406.9 157.0 %all-gather.19.cloned.1.call-start = ((), (), s32[]{:S(2)}) async-start(), calls=%async_computation.17 | async-start | bytes 4718592 | tf_op jit(solution)/shard_map/all_gather | solution.py:284
  407.6 166.4 %all-gather.15.cloned.1.call-start = ((), (), s32[]{:S(2)}) async-start(), calls=%async_computation.10 | async-start | bytes 3932160 | tf_op jit(solution)/shard_map/all_gather | solution.py:206
  413.3 216.4 %all-reduce.18.cloned.1.call-start = ((), (), s32[]{:S(2)}) async-start(), calls=%async_computation.22 | async-start | bytes 6291456 | tf_op jit(solution)/shard_map/psum | solution.py:280
  514.9 161.2 %all-gather.17.cloned.1.call-start = ((), (), s32[]{:S(2)}) async-start(), calls=%async_computation.13 | async-start | bytes 3932160 | tf_op jit(solution)/shard_map/all_gather | solution.py:270
  (125 other events, 307.7 us)
Sparse Core Ops, SparseCore 0:
  22.0 23.0 all-reduce.9
  121.9 69.8 all-reduce.11
  221.7 58.1 all-reduce.13
  303.8 102.9 all-reduce.19
  410.4 60.0 all-reduce.15
  471.9 9.7 all-gather.20
  483.2 13.2 all-gather.18
  498.9 48.2 all-gather.14
  551.3 78.4 all-reduce.17
  632.0 44.0 all-gather.16
Sparse Core Ops, SparseCore 1:
  24.4 40.0 all-gather.22
  66.5 26.9 all-gather.10
  95.9 43.1 all-gather.24
  141.1 31.4 all-gather.12
  296.0 67.7 reduce-scatter.7
  366.8 36.3 reduce-scatter.15
  406.0 26.2 reduce-scatter.9
  435.0 32.2 reduce-scatter.13
  470.8 44.1 reduce-scatter.11

commit v2 on v1

--- a/solution.py
+++ b/solution.py
@@ -1,6 +1,10 @@
+import functools
+
 import jax
 import jax.numpy as jnp
 from jax import lax
+from jax.experimental import pallas as pl
+from jax.experimental.pallas import tpu as pltpu
 from jax.sharding import Mesh
 from jax.sharding import PartitionSpec as P
 
@@ -61,6 +65,280 @@
 def local_scores(q4, kw, allowed):
     s = jnp.einsum("nqhe,nkhe->nhqk", q4, kw, preferred_element_type=F32) * SCALE
     return jnp.where(allowed[:, None], s, NEGATIVE)
+
+
+MESH = pl.DeviceIdType.MESH
+
+
+def remote(src, dst, send, recv, device):
+    return pltpu.make_async_remote_copy(
+        src_ref=src, dst_ref=dst, send_sem=send, recv_sem=recv, device_id=device, device_id_type=MESH
+    )
+
+
+def greet(devices):
+    barrier = pltpu.get_barrier_semaphore()
+    for device in devices:
+        pl.semaphore_signal(barrier, inc=1, device_id=device, device_id_type=MESH)
+    pl.semaphore_wait(barrier, len(devices))
+
+
+def here():
+    return lax.axis_index("branch"), lax.axis_index("zz"), lax.axis_index("core")
+
+
+def others(me, count):
+    return [lax.rem(me + k, count) for k in range(1, count)]
+
+
+def band(start, size):
+    return pl.ds(pl.multiple_of(start, size), size)
+
+
+def group_sum_kernel(nb, x, o, sib, part, came, sib_s, sib_r, rs_s, rs_r, ag_s, ag_r, fw_s, fw_r):
+    b, z, c = here()
+    half = x.shape[0] // 2
+    ch = half // nb
+    twin = (b, z, 1 - c)
+    peers = others(b, nb)
+
+    def rows(core, j):
+        return band(core * half + j * ch, ch)
+
+    greet([twin] + [(j, z, c) for j in peers])
+    order = peers + [b]
+    to_twin = [remote(x.at[rows(1 - c, j)], sib.at[j], sib_s.at[j], sib_r.at[j], twin) for j in order]
+    for copy in to_twin:
+        copy.start()
+    sends = []
+    for j, copy in zip(peers, to_twin):
+        copy.wait_recv()
+        part[j] = (x[rows(c, j)].astype(F32) + sib[j].astype(F32)).astype(BF16)
+        send = remote(part.at[j], came.at[b], rs_s.at[j], rs_r.at[b], (j, z, c))
+        send.start()
+        sends.append(send)
+    to_twin[-1].wait_recv()
+    total = x[rows(c, b)].astype(F32) + sib[b].astype(F32)
+    for j in peers:
+        remote(part.at[j], came.at[j], rs_s.at[j], rs_r.at[j], (j, z, c)).wait_recv()
+        total = total + came[j].astype(F32)
+    mine = o.at[rows(c, b)]
+    mine[...] = total.astype(BF16)
+    for j in peers:
+        send = remote(mine, mine, ag_s.at[j], ag_r.at[b], (j, z, c))
+        send.start()
+        sends.append(send)
+    send = remote(mine, mine, fw_s.at[b], fw_r.at[b], twin)
+    send.start()
+    sends.append(send)
+    for j in peers:
+        piece = o.at[rows(c, j)]
+        remote(piece, piece, ag_s.at[j], ag_r.at[j], (j, z, c)).wait_recv()
+        send = remote(piece, piece, fw_s.at[j], fw_r.at[j], twin)
+        send.start()
+        sends.append(send)
+    for j in order:
+        piece = o.at[rows(1 - c, j)]
+        remote(piece, piece, fw_s.at[j], fw_r.at[j], twin).wait_recv()
+    for copy in to_twin + sends:
+        copy.wait_send()
+
+
+def group_sum(x, nb, cid):
+    rows, width = x.shape
+    ch = rows // 2 // nb
+    dma = pltpu.SemaphoreType.DMA((nb,))
+    return pl.pallas_call(
+        functools.partial(group_sum_kernel, nb),
+        out_shape=jax.ShapeDtypeStruct(x.shape, BF16),
+        in_specs=[pl.BlockSpec(memory_space=pltpu.VMEM)],
+        out_specs=pl.BlockSpec(memory_space=pltpu.VMEM),
+        scratch_shapes=[pltpu.VMEM((nb, ch, width), BF16)] * 3 + [dma] * 8,
+        compiler_params=pltpu.CompilerParams(
+            collective_id=cid, has_side_effects=True, vmem_limit_bytes=40 << 20
+        ),
+    )(x)
+
+
+def block_sum_kernel(nz, x, o, sib, part, came, sib_s, sib_r, rs_s, rs_r):
+    b, z, c = here()
+    ch = o.shape[0]
+    twin = (b, z, 1 - c)
+    peers = others(z, nz)
+
+    def rows(core, j):
+        return band((2 * j + core) * ch, ch)
+
+    greet([twin] + [(b, j, c) for j in peers])
+    order = peers + [z]
+    to_twin = [remote(x.at[rows(1 - c, j)], sib.at[j], sib_s.at[j], sib_r.at[j], twin) for j in order]
+    for copy in to_twin:
+        copy.start()
+    sends = []
+    for j, copy in zip(peers, to_twin):
+        copy.wait_recv()
+        part[j] = (x[rows(c, j)].astype(F32) + sib[j].astype(F32)).astype(BF16)
+        send = remote(part.at[j], came.at[z], rs_s.at[j], rs_r.at[z], (b, j, c))
+        send.start()
+        sends.append(send)
+    to_twin[-1].wait_recv()
+    total = x[rows(c, z)].astype(F32) + sib[z].astype(F32)
+    for j in peers:
+        remote(part.at[j], came.at[j], rs_s.at[j], rs_r.at[j], (b, j, c)).wait_recv()
+        total = total + came[j].astype(F32)
+    o[...] = total.astype(BF16)
+    for copy in to_twin + sends:
+        copy.wait_send()
+
+
+def block_sum(x, nz, cid):
+    rows, width = x.shape
+    ch = rows // (2 * nz)
+    dma = pltpu.SemaphoreType.DMA((nz,))
+    return pl.pallas_call(
+        functools.partial(block_sum_kernel, nz),
+        out_shape=jax.ShapeDtypeStruct((ch, width), BF16),
+        in_specs=[pl.BlockSpec(memory_space=pltpu.VMEM)],
+        out_specs=pl.BlockSpec(memory_space=pltpu.VMEM),
+        scratch_shapes=[pltpu.VMEM((nz, ch, width), BF16)] * 3 + [dma] * 4,
+        compiler_params=pltpu.CompilerParams(
+            collective_id=cid, has_side_effects=True, vmem_limit_bytes=40 << 20
+        ),
+    )(x)
+
+
+def prep_kernel(
+    nb, nz,
+    tokens, cotangent, ids, gain, router, heads, lh, lm, le, lr,
+    tok_o, cot_o, first_o, gate_o, q_o, kv_o, lh_o, lm_o, le_o, lr_o,
+    picks, sib, sib_s, sib_r, own_s, w_s, w_r, wf_s, wf_r, kv_s, kv_r, kf_s, kf_r,
+):
+    b, z, c = here()
+    twin = (b, z, 1 - c)
+    bpeers = others(b, nb)
+    zpeers = others(z, nz)
+    cap, D = tok_o.shape
+    half = cap // 2
+    rw = q_o.shape[1]
+    greet([twin] + [(j, z, c) for j in bpeers] + [(b, j, c) for j in zpeers])
+
+    pairs = [(lh, lh_o), (lm, lm_o), (le, le_o), (lr, lr_o)]
+
+    def cut(ref, array, core):
+        if array == 0:
+            size = ref.shape[1] // 2
+            return ref.at[:, band(core * size, size)]
+        size = ref.shape[0] // 2
+        return ref.at[band(core * size, size)]
+
+    sends = []
+    for i, (src, dst) in enumerate(pairs):
+        own = pltpu.make_async_copy(src, dst.at[b], own_s.at[i])
+        own.start()
+        sends.append(own)
+        for j in bpeers:
+            copy = remote(cut(src, i, c), cut(dst.at[b], i, c), w_s.at[i, j], w_r.at[i, b], (j, z, c))
+            copy.start()
+            sends.append(copy)
+
+    step = cap // 4
+    for k in range(4):
+        at = pl.ds(k * step, step)
+        spot = lax.broadcasted_iota(jnp.int32, (step, tokens.shape[0]), 1)
+        hot = jnp.where(ids[at] == spot, 1.0, 0.0).astype(BF16)
+        picks[at, :D] = mm(hot, tokens[...], 1, 0).astype(BF16)
+        picks[at, D:] = mm(hot, cotangent[...], 1, 0).astype(BF16)
+        copy = remote(picks.at[at], sib.at[at], sib_s.at[k], sib_r.at[k], twin)
+        copy.start()
+        sends.append(copy)
+    for k in range(4):
+        at = pl.ds(k * step, step)
+        remote(picks.at[at], sib.at[at], sib_s.at[k], sib_r.at[k], twin).wait_recv()
+        tok = picks[at, :D].astype(F32) + sib[at, :D].astype(F32)
+        tok_o[at] = tok.astype(BF16)
+        cot_o[at] = (picks[at, D:].astype(F32) + sib[at, D:].astype(F32)).astype(BF16)
+        r = lax.rsqrt(jnp.mean(tok * tok, axis=-1, keepdims=True) + EPSILON)
+        first = (tok * r * gain[...]).astype(BF16)
+        first_o[at] = first
+        logit = jnp.sum(first.astype(F32) * router[...], axis=-1, keepdims=True)
+        gate_o[at] = 1.0 / (1.0 + jnp.exp(-logit))
+
+    own_rows = first_o[band(c * half, half)]
+    q_o[...] = mm(own_rows, heads[0], 1, 1).astype(BF16)
+    mine = kv_o.at[band((2 * z + c) * half, half)]
+    mine[:, :rw] = mm(own_rows, heads[1], 1, 1).astype(BF16)
+    mine[:, rw:] = mm(own_rows, heads[2], 1, 1).astype(BF16)
+    for j in zpeers:
+        copy = remote(mine, mine, kv_s.at[j], kv_r.at[z], (b, j, c))
+        copy.start()
+        sends.append(copy)
+    copy = remote(mine, mine, kf_s.at[z], kf_r.at[z], twin)
+    copy.start()
+    sends.append(copy)
+
+    def pass_weights(i):
+        for j in bpeers:
+            dst = cut(pairs[i][1].at[j], i, c)
+            remote(dst, dst, w_s.at[i, j], w_r.at[i, j], (j, z, c)).wait_recv()
+            copy = remote(dst, dst, wf_s.at[i, j], wf_r.at[i, j], twin)
+            copy.start()
+            sends.append(copy)
+
+    pass_weights(0)
+    for j in zpeers:
+        piece = kv_o.at[band((2 * j + c) * half, half)]
+        remote(piece, piece, kv_s.at[j], kv_r.at[j], (b, j, c)).wait_recv()
+        copy = remote(piece, piece, kf_s.at[j], kf_r.at[j], twin)
+        copy.start()
+        sends.append(copy)
+    for i in range(1, 4):
+        pass_weights(i)
+    for j in zpeers + [z]:
+        piece = kv_o.at[band((2 * j + 1 - c) * half, half)]
+        remote(piece, piece, kf_s.at[j], kf_r.at[j], twin).wait_recv()
+    for i in range(4):
+        for j in bpeers:
+            dst = cut(pairs[i][1].at[j], i, 1 - c)
+            remote(dst, dst, wf_s.at[i, j], wf_r.at[i, j], twin).wait_recv()
+    for copy in sends:
+        if copy.is_remote:
+            copy.wait_send()
+        else:
+            copy.wait()
+
+
+def prep(nb, nz, tokens, cotangent, ids, gain, router, heads, lh, lm, le, lr):
+    cap = ids.shape[0]
+    D = tokens.shape[1]
+    rw = heads.shape[1]
+    half = cap // 2
+    vmem = pl.BlockSpec(memory_space=pltpu.VMEM)
+    hbm = pl.BlockSpec(memory_space=pl.ANY)
+    like = lambda x: jax.ShapeDtypeStruct((nb,) + x.shape, BF16)
+    rows = jax.ShapeDtypeStruct((cap, D), BF16)
+    dma = lambda *shape: pltpu.SemaphoreType.DMA(shape)
+    return pl.pallas_call(
+        functools.partial(prep_kernel, nb, nz),
+        out_shape=(
+            rows, rows, rows,
+            jax.ShapeDtypeStruct((cap, 1), F32),
+            jax.ShapeDtypeStruct((half, rw), BF16),
+            jax.ShapeDtypeStruct((2 * nz * half, 2 * rw), BF16),
+            like(lh), like(lm), like(le), like(lr),
+        ),
+        in_specs=[vmem] * 6 + [hbm] * 4,
+        out_specs=(vmem,) * 6 + (hbm,) * 4,
+        scratch_shapes=[
+            pltpu.VMEM((cap, 2 * D), BF16),
+            pltpu.VMEM((cap, 2 * D), BF16),
+            dma(4), dma(4), dma(4),
+            dma(4, nb), dma(4, nb), dma(4, nb), dma(4, nb),
+            dma(nz), dma(nz), dma(nz), dma(nz),
+        ],
+        compiler_params=pltpu.CompilerParams(
+            collective_id=0, has_side_effects=True, vmem_limit_bytes=40 << 20
+        ),
+    )(tokens, cotangent, ids, gain, router, heads, lh, lm, le, lr)
 
 
 def per_device(
@@ -99,35 +377,30 @@
     heads_r = rw // DH
     blocks = own // WIN
 
-    lh = lax.all_gather(local_heads.transpose(1, 0, 2), "branch")
-    lm = lax.all_gather(local_merge, "branch", axis=0, tiled=True)
-    le = lax.all_gather(local_expand.transpose(1, 0, 2), "branch")
-    lr = lax.all_gather(local_reduce, "branch", axis=0, tiled=True)
-    lh3 = lh.transpose(1, 2, 0, 3).reshape(3, D, nb * hl)
-    le2 = le.transpose(1, 2, 0, 3).reshape(2, D, nb * fl)
-
     n_own = routed_counts[d]
     offset = jnp.where(core == 0, 0, cap - n_own)
     ranks = jnp.arange(cap, dtype=jnp.int32)
     live = (ranks >= offset) & (ranks < offset + n_own)
-    rolled = jnp.take(routed_slots, jnp.mod(ranks - offset, cap), axis=0)
+    twice = jnp.concatenate([routed_slots, routed_slots])
+    rolled = lax.dynamic_slice(twice, (jnp.mod(cap - offset, cap),), (cap,))
     ids = jnp.where(live, rolled, -1)
-    pick = (ids[:, None] == jnp.arange(rows, dtype=jnp.int32)[None, :]).astype(BF16)
-    pick_own = lax.dynamic_slice(pick, (0, b * own), (cap, own))
+    own_ids = ids[:, None] - b * own
+    pick_own = (own_ids == jnp.arange(own, dtype=jnp.int32)[None, :]).astype(BF16)
     mask_own = (jnp.sum(pick_own.astype(F32), 0) > 0.5)[:, None]
 
-    pair_rows = mm(pick, jnp.concatenate([tokens, cotangent], 1), 1, 0).astype(BF16)
-    pair_rows = lax.psum(pair_rows, "core").astype(F32)
-    tok_r, cot_r = pair_rows[:, :D], pair_rows[:, D:]
+    tok_r, cot_r, first_r, gate, qr, kv, lh, lm, le, lr = prep(
+        nb, nz, tokens, cotangent, ids[:, None], gain_before[None], router_vector[None],
+        routed_heads.transpose(1, 2, 0),
+        local_heads.transpose(1, 0, 2), local_merge, local_expand.transpose(1, 0, 2), local_reduce,
+    )
+    tok_r, cot_r = tok_r.astype(F32), cot_r.astype(F32)
     r1r, xh1r = norm_parts(tok_r)
-    first_r = (xh1r * gain_before).astype(BF16)
-    gate = jax.nn.sigmoid(jnp.dot(first_r.astype(F32), router_vector, precision=HIGHEST))[:, None]
     first_half = lax.dynamic_slice(first_r, (core * half, 0), (half, D))
     gate_half = lax.dynamic_slice(gate, (core * half, 0), (half, 1))
-    proj_r = jnp.einsum("rd,dcf->rcf", first_half, routed_heads, preferred_element_type=F32).astype(BF16)
-    kv = lax.all_gather(
-        jnp.concatenate([proj_r[:, 1], proj_r[:, 2]], 1), DP, axis=0, tiled=True
-    )
+    lm = lm.reshape(nb * hl, D)
+    lr = lr.reshape(nb * fl, D)
+    lh3 = lh.transpose(1, 2, 0, 3).reshape(3, D, nb * hl)
+    le2 = le.transpose(1, 2, 0, 3).reshape(2, D, nb * fl)
 
     perm_up = [(i, i + 1) for i in range(ndp - 1)]
     perm_down = [(i + 1, i) for i in range(ndp - 1)]
@@ -163,7 +436,7 @@
     ctx_l = ctx_l.reshape(own, heads_l * DH)
     local_attn = mm(ctx_l, lm, 1, 0)
 
-    qr = proj_r[:, 0].reshape(half, heads_r, DH)
+    qr = qr.reshape(half, heads_r, DH)
     kr = kv[:, :rw].reshape(-1, heads_r, DH)
     vr = kv[:, rw:].reshape(-1, heads_r, DH)
     sr = jnp.einsum("qhe,khe->hqk", qr, kr, preferred_element_type=F32) * SCALE
@@ -179,7 +452,7 @@
         return lax.dynamic_update_slice(jnp.zeros((cap, x.shape[1]), x.dtype), x, (core * half, 0))
 
     part = mm(pick_own, local_attn.astype(BF16), 1, 0) + at_half(gate_half * attn_r)
-    mixed_r = lax.psum(part.astype(BF16), GROUP)
+    mixed_r = group_sum(part.astype(BF16), nb, 1)
     mixed_own = jnp.where(mask_own, mm(pick_own, mixed_r, 0, 0), local_attn)
     middle_own = tok_own + mixed_own
     middle_r = tok_r + mixed_r.astype(F32)
@@ -198,7 +471,7 @@
     both = jnp.concatenate(
         [ff_r.astype(BF16), (dn_r + mm(pick_own, dn_l.astype(BF16), 1, 0)).astype(BF16)], 1
     )
-    both = lax.psum(both, GROUP)
+    both = group_sum(both, nb, 2)
     ffr_sum, dn2_r = both[:, :D].astype(F32), both[:, D:]
     layer_own = (
         middle_own + ff_l + mm(pick_own, (gate * ffr_sum).astype(BF16), 0, 0)
@@ -255,7 +528,7 @@
     dkr = jnp.einsum("hqk,qhe->khe", dsr, qr, preferred_element_type=F32) * SCALE
     dvr = jnp.einsum("hqk,qhe->khe", pr.astype(BF16), dctx_r, preferred_element_type=F32)
     dkvr = jnp.concatenate([dkr.reshape(-1, rw), dvr.reshape(-1, rw)], 1).astype(BF16)
-    dkvr = lax.psum_scatter(dkvr, DP, scatter_dimension=0, tiled=True)
+    dkvr = block_sum(dkvr, nz, 4)
     triple = jnp.stack([dqr.reshape(half, rw).astype(BF16), dkvr[:, :rw], dkvr[:, rw:]], 1)
     picked = jnp.einsum("rcf,dcf->rd", triple, routed_heads, preferred_element_type=F32)
     d_rh = jnp.einsum("rd,rcf->dcf", first_half, triple, preferred_element_type=F32)
@@ -263,7 +536,7 @@
     router_part = jnp.sum(d_logit * first_r.astype(F32), 0)
 
     part3 = at_half(picked) + d_logit * router_vector[None, :] + mm(pick_own, gf_l.astype(BF16), 1, 0)
-    gf_r = lax.psum(part3.astype(BF16), GROUP)
+    gf_r = group_sum(part3.astype(BF16), nb, 3)
     gf_own = jnp.where(mask_own, mm(pick_own, gf_r, 0, 0), gf_l)
     td_own = (gm_own + norm_back(gf_own, xh1, r1, gain_before)).astype(BF16)
     delta_gain_before = jnp.sum(gf_own * xh1, 0)

time: 699 us -> 597 us (0.85)
  waiting for transfers between devices: 356 us -> 118 us
  Pallas kernels: 0 us -> 137 us
  local copies, waits for them, and re-layouts: 88 us -> 111 us
  matrix products: 99.4 us -> 83.4 us
  blocking collectives: 55.4 us -> 41.3 us
    pallas_call x0 -> x5, Pallas kernels: none -> 137 us  [the longest x3 64.3 us: group_sum(): pl.pallas_call(functools.partial(group_sum_kernel, nb), out_shape=jax.Sha...]
    psum x4 -> x0, waiting for transfers between devices: 121 us -> none  [the longest x1 54.6 us: per_device(): both = lax.psum(both, GROUP)]
    reduce_scatter x3, waiting for transfers between devices: 95.3 us -> 55.2 us  [over_branch(): lax.psum_scatter(x.astype(BF16), 'branch', scatter_dimension=dim, tiled=T...]
    psum x1, waiting for transfers between devices: 50.5 us -> 11.7 us  [per_device(): g_le = lax.psum(over_branch(jnp.stack([d_lg, d_lu], 0), 2), DP)]
    all_gather x1, waiting for transfers between devices: 38.2 us -> 0.01 us  [per_device(): lax.all_gather(td_own, 'branch', axis=0, tiled=True).astype(F32)]
    dot_general x41 -> x40, matrix products: 76.3 us -> 49.5 us  [mm(): lax.dot_general(a, b, (((ca,), (cb,)), ((), ())), preferred_element_type=...]
    all_gather x1 -> x0, blocking collectives: 15.4 us -> none  [per_device(): lm = lax.all_gather(local_merge, 'branch', axis=0, tiled=True)]
    unnamed x276 -> x271, local copies, waits for them, and re-layouts: 44 us -> 55.5 us
  transfers between devices with their start and end apart: 23 -> 14, of which waited for: 12 -> 5; matrix products, arithmetic and copies ran while one was open for 26% -> 27% of each run, Pallas kernels for 0% -> 16%
where the time goes in v2:
time: 597 us; the launch traced here: 586 us
  Pallas kernels  137 us (23%)
  waiting for transfers between devices  118 us (20%)
  local copies, waits for them, and re-layouts  111 us (19%)
  matrix products  83.4 us (14%)
  other arithmetic  66.6 us (11%)
  blocking collectives  41.3 us (7%)
  between operations  18.8 us (3%)
  starting transfers between devices  10.4 us (2%)
    pallas_call x3, Pallas kernels, group_sum(): pl.pallas_call(functools.partial(group_sum_kernel, nb), out_shape=jax.Sha...  64.3 us
    unnamed x271, local copies, waits for them, and re-layouts  55.5 us
    reduce_scatter x3, waiting for transfers between devices, over_branch(): lax.psum_scatter(x.astype(BF16), 'branch', scatter_dimension=dim, tiled=T...  55.2 us
    pallas_call x1, Pallas kernels, prep(): pl.pallas_call(functools.partial(prep_kernel, nb, nz), out_shape=(rows, r...  54.3 us
    dot_general x40, matrix products, mm(): lax.dot_general(a, b, (((ca,), (cb,)), ((), ())), preferred_element_type=...  49.5 us
    psum x1, blocking collectives, per_device(): lax.psum(jnp.stack([delta_gain_before, delta_gain_middle, router_part]).a...  41.3 us
    psum x1, waiting for transfers between devices, per_device(): lax.psum(jnp.stack([d_rg, d_ru], 0).astype(BF16), 'zz')  41 us
    pallas_call x1, Pallas kernels, block_sum(): pl.pallas_call(functools.partial(block_sum_kernel, nz), out_shape=jax.Sha...  18.3 us
  transfers between devices with their start and end apart: 14, of which 5 were waited for; matrix products, arithmetic and copies ran while one was open for 27% of the time, Pallas kernels for 16%

profile of v2, /device:TPU:0, one launch (start us, length us, event | category | flops | bytes accessed | tf_op | source)
XLA Modules:
  0.0 586.4 jit_solution(17562057965083442816)
XLA Ops:
  11.3 3.7 collective-permute-start
  23.0 54.3 %shard_map.246 = (bf16[512,768]{1,0:T(8,128)(2,1)S(1)}, bf16[512,768]{1,0:T(8,128)(2,1)S(1)}, bf16[512,768]{1,0:T(8,128)(2,1)S(1)}, f32[512,1]{1,0:T(8,128)S(1)}...) custom-call(bf16[2048,768]{1,0:T(8,128)(2,1)} %tokens.1, ...), custom_call_target="tpu_custom_call" | custom-call | tf_op jit(solution)/shard_map/pallas_call | solution.py:320
  88.5 3.3 fusion.135
  97.8 3.7 fusion.132
  116.8 7.5 %constant_dynamic-slice_fusion = (bf16[768,1,512]{2,1,0:T(2,128)(2,1)}, bf16[768,1,512]{2,1,0:T(2,128)(2,1)}) fusion(bf16[768,2,1024]{2,1,0:T(2,128)(2,1)} %param.38, s32[]{:T(128)S(6)} %add.333, s32[]{:T(128)S(6)} %select_n.63), kind=kLoop, calls=%fused_computation.236 | loop fusion | bytes 3145736 | tf_op jit(solution)/shard_map/slice | solution.py:468
  154.5 16.5 %shard_map.247 = bf16[512,768]{1,0:T(8,128)(2,1)S(1)} custom-call(bf16[512,768]{1,0:T(8,128)(2,1)S(1)} %convert_element_type.251.x), custom_call_target="tpu_custom_call" | custom-call | tf_op jit(solution)/shard_map/pallas_call | solution.py:151
  178.0 3.1 multiply_convert_fusion.3
  189.7 26.5 %shard_map.248 = bf16[512,1536]{1,0:T(8,128)(2,1)S(1)} custom-call(bf16[512,1536]{1,0:T(8,128)(2,1)S(1)} %pad_maximum_fusion.5.x), custom_call_target="tpu_custom_call" | custom-call | tf_op jit(solution)/shard_map/pallas_call | solution.py:151
  216.2 3.0 multiply_reduce_fusion.5
  224.7 4.5 multiply_reduce_fusion
  229.2 3.9 fusion.6
  237.3 3.7 multiply_convert_fusion
  247.7 3.3 fusion.27
  253.9 3.1 collective-permute-start.2
  263.3 7.2 %collective-permute-done.3 = bf16[128,1024]{0,1:T(8,128)(2,1)S(1)} collective-permute-done((bf16[128,1024]{0,1:T(8,128)(2,1)S(1)}, bf16[128,1024]{0,1:T(8,128)(2,1)S(1)}, u32[]{:S(2)}, u32[]{:S(2)}) %collective-permute-start.3) | collective-permute-done | bytes 262176 | tf_op jit(solution)/shard_map/ppermute | solution.py:509
  274.0 5.7 copy.129
  279.7 3.9 copy.140
  287.6 3.7 convolution_convert_fusion
  304.4 41.0 %all-reduce.8.cloned.1.call-done = (bf16[2,768,512]{2,1,0:T(8,128)(2,1)}, bf16[512,768]{1,0:T(8,128)(2,1)}) async-done(((bf16[2,768,512]{2,1,0:T(8,128)(2,1)}, bf16[512,768]{1,0:T(8,128)(2,1)}), (bf16[2,768,512]{2,1,0:T(8,128)(2,1)}, bf16[512,768]{1,0:T(8,128)(2,1)})) %all-reduce.8.cloned.1.call-update) | async-done | bytes 2359312 | tf_op jit(solution)/shard_map/psum | solution.py:558
  345.5 5.0 fusion.14
  357.0 7.1 %multiply_reduce_fusion.1 = (f32[3,256]{1,0:T(4,128)S(1)}, f32[3,256,2048]{2,1,0:T(8,128)}) fusion(f32[3,256,2048]{2,1,0:T(8,128)} %copy-done.16, f32[3,256]{1,0:T(4,128)S(1)} %log_add_fusion.1, bf16[256,3,64]{0,2,1:T(8,128)(2,1)S(1)} %bitcast.244, bf16[2048,3,64]{0,2,1:T(8,128)(2,1)S(1)} %bitcast.216), kind=kOutput, calls=%fused_computation.11 | convolution fusion | flops 207617280 | bytes 13473792 | tf_op jit(solution)/shard_map/qhe,khe->hqk/dot_general | solution.py:524
  364.4 5.7 multiply_convert_fusion.1
  375.5 18.3 %shard_map.249 = bf16[256,384]{1,0:T(8,128)(2,1)S(1)} custom-call(bf16[2048,384]{1,0:T(8,128)(2,1)S(1)} %pad_maximum_fusion.6.x), custom_call_target="tpu_custom_call" | custom-call | tf_op jit(solution)/shard_map/pallas_call | solution.py:198
  401.6 21.2 %shard_map.250 = bf16[512,768]{1,0:T(8,128)(2,1)S(1)} custom-call(bf16[512,768]{1,0:T(8,128)(2,1)S(1)} %add_convert_fusion.1.x), custom_call_target="tpu_custom_call" | custom-call | tf_op jit(solution)/shard_map/pallas_call | solution.py:151
  431.9 55.2 %reduce-scatter.9.cloned.1.call-done = bf16[2,768,256]{2,1,0:T(8,128)(2,1)} async-done(((bf16[2,768,1024]{2,1,0:T(8,128)(2,1)}), bf16[2,768,256]{2,1,0:T(8,128)(2,1)}) %reduce-scatter.9.cloned.1.call-update) | async-done | bytes 786448 | tf_op jit(solution)/shard_map/reduce_scatter | solution.py:551
  487.8 41.3 %psum.63 = f32[3,768]{1,0:T(4,128)S(1)} all-reduce(f32[3,768]{1,0:T(4,128)S(1)} %pad_maximum_fusion.13), channel_id=1, replica_groups=mesh['branch'=4,'zz'=4,'core'=2] {'branch','zz','core'}, use_global_device_ids=true, to_apply=%region_18.19 | all-reduce | flops 2304 | bytes 18432 | tf_op jit(solution)/shard_map/psum | solution.py:545
  529.7 3.3 convert_element_type.310
  533.1 5.1 convert_element_type.270
  538.2 5.2 convert_element_type.293
  543.3 5.3 convert_bitcast_fusion
  548.6 10.4 %copy.127 = f32[768,2,1024]{2,1,0:T(2,128)} copy(f32[768,2,1024]{2,0,1:T(8,128)} %convert_bitcast_fusion) | data formatting | bytes 12582912
  559.0 11.7 %all-reduce.6.cloned.1.call-done = (bf16[768,2,256]{2,0,1:T(8,128)(2,1)}, bf16[768,3,128]{2,0,1:T(8,128)(2,1)}, bf16[128,768]{1,0:T(8,128)(2,1)}, bf16[768,3,192...) async-done(((bf16[768,2,256]{2,0,1:T(8,128)(2,1)}, bf16[768,3,128]{2,0,1:T(8,128)(2,1)}, bf16[128,768]{1,0:T(8,128)(2,1)}, ...) | async-done | bytes 3145744 | tf_op jit(solution)/shard_map/psum | solution.py:553
  (440 shorter events, 171.2 us)
Async XLA Ops:
  8.0 116.3 %copy-start = (bf16[1024,768]{1,0:T(8,128)(2,1)S(1)}, bf16[1024,768]{1,0:T(8,128)(2,1)}, u32[]{:S(2)}) copy-start(bf16[1024,768]{1,0:T(8,128)(2,1)} %param.39) | copy-start | bytes 4718596
  8.0 12.8 %copy-start.80 = (bf16[768,2,256]{2,1,0:T(2,128)(2,1)S(1)}, bf16[768,2,256]{2,1,0:T(2,128)(2,1)}, u32[]{:S(2)}) copy-start(bf16[768,2,256]{2,1,0:T(2,128)(2,1)} %param.36) | copy-start | bytes 2359300
  8.0 337.4 %all-reduce.8.cloned.1.call-start = ((), (), s32[]{:S(2)}) async-start(), calls=%async_computation.13 | async-start | bytes 4718592 | tf_op jit(solution)/shard_map/psum | solution.py:558
  10.0 116.5 %collective-permute-start.1 = (bf16[128,768]{1,0:T(8,128)(2,1)}, bf16[128,768]{1,0:T(8,128)(2,1)}, u32[]{:S(2)}, u32[]{:S(2)}) collective-permute-start(bf16[128,768]{1,0:T(8,128)(2,1)} %get-tuple-element.191), channel_id=1, source_target_pairs={{1,0},{2,1},{3,2},{4,3},{5,4},{6,5},{7,6},{9,8},{10,9},{11,10},{12... | collective-permute-start | bytes 589832 | tf_op jit(solution)/shard_map/ppermute | solution.py:408
  11.3 115.2 %collective-permute-start = (bf16[128,768]{1,0:T(8,128)(2,1)}, bf16[128,768]{1,0:T(8,128)(2,1)}, u32[]{:S(2)}, u32[]{:S(2)}) collective-permute-start(bf16[128,768]{1,0:T(8,128)(2,1)} %get-tuple-element.190), channel_id=1, source_target_pairs={{0,1},{1,2},{2,3},{3,4},{4,5},{5,6},{6,7},{8,9},{9,10},{10,11},{11... | collective-permute-start | bytes 589832 | tf_op jit(solution)/shard_map/ppermute | solution.py:407
  18.5 78.5 %copy-start.102 = (s32[512]{0:T(512)}, s32[512]{0:T(512)S(1)}, u32[]{:S(2)}) copy-start(s32[512]{0:T(512)S(1)} %get-tuple-element.177) | copy-start | bytes 6148
  116.8 36.2 %copy-start.95 = (bf16[3,64,256]{2,1,0:T(8,128)(2,1)}, bf16[3,64,256]{2,1,0:T(8,128)(2,1)S(1)}, u32[]{:S(2)}) copy-start(bf16[3,64,256]{2,1,0:T(8,128)(2,1)S(1)} %fusion.54) | copy-start | bytes 294916
  116.8 7.5 %copy-start.112 = (f32[512]{0:T(512)S(1)}, f32[512]{0:T(512)}, u32[]{:S(2)}) copy-start(f32[512]{0:T(512)} %reduce.13) | copy-start | bytes 6148
  116.8 9.7 %copy-start.34 = (bf16[2048,768]{1,0:T(8,128)(2,1)S(1)}, bf16[2048,768]{1,0:T(8,128)(2,1)}, u32[]{:S(2)}) copy-start(bf16[2048,768]{1,0:T(8,128)(2,1)} %tokens.1) | copy-start | bytes 9437188
  154.4 16.6 %copy-start.33 = (f32[768,768]{1,0:T(8,128)S(1)}, f32[768,768]{1,0:T(8,128)}, u32[]{:S(2)}) copy-start(f32[768,768]{1,0:T(8,128)} %copy-done.32) | copy-start | bytes 7077892
  154.4 16.6 %copy-start.122 = (pred[512]{0:T(512)(128)(4,1)S(1)}, pred[512]{0:T(512)(128)(4,1)}, u32[]{:S(2)}) copy-start(pred[512]{0:T(512)(128)(4,1)} %broadcast_compare_fusion) | copy-start | bytes 1540
  172.0 47.2 %copy-start.22 = (f32[512,768]{1,0:T(8,128)}, f32[512,768]{1,0:T(8,128)S(1)}, u32[]{:S(2)}) copy-start(f32[512,768]{1,0:T(8,128)S(1)} %get-tuple-element.223) | copy-start | bytes 4718596
  173.2 12.2 %copy-start.52 = (bf16[512,768]{1,0:T(8,128)(2,1)}, bf16[512,768]{1,0:T(8,128)(2,1)S(1)}, u32[]{:S(2)}) copy-start(bf16[512,768]{1,0:T(8,128)(2,1)S(1)} %get-tuple-element.175) | copy-start | bytes 2359300
  173.2 43.0 %copy-start.36 = (f32[512,768]{1,0:T(8,128)}, f32[512,768]{1,0:T(8,128)S(1)}, u32[]{:S(2)}) copy-start(f32[512,768]{1,0:T(8,128)S(1)} %get-tuple-element.176) | copy-start | bytes 4718596
  233.2 9.8 %copy-start.20 = (f32[4,8,64,384]{3,2,1,0:T(8,128)}, f32[4,8,64,384]{3,2,1,0:T(8,128)S(1)}, u32[]{:S(2)}) copy-start(f32[4,8,64,384]{3,2,1,0:T(8,128)S(1)} %fusion.6) | copy-start | bytes 9437188
  247.6 181.8 %reduce-scatter.13.cloned.1.call-start = ((), (), s32[]{:S(2)}) async-start(), calls=%async_computation.11 | async-start | bytes 2949120
  253.9 9.3 %collective-permute-start.2 = (bf16[128,1024]{0,1:T(8,128)(2,1)S(1)}, bf16[128,1024]{0,1:T(8,128)(2,1)S(1)}, u32[]{:S(2)}, u32[]{:S(2)}) collective-permute-start(bf16[128,1024]{0,1:T(8,128)(2,1)S(1)} %slice.405), channel_id=1, source_target_pairs={{0,8},{8,16},{16,24},{24,1},{1,9},{9,17},{17,25},{25,2},{2,10},{10... | collective-permute-start | bytes 786440 | tf_op jit(solution)/shard_map/ppermute | solution.py:508
  259.2 11.3 %collective-permute-start.3 = (bf16[128,1024]{0,1:T(8,128)(2,1)S(1)}, bf16[128,1024]{0,1:T(8,128)(2,1)S(1)}, u32[]{:S(2)}, u32[]{:S(2)}) collective-permute-start(bf16[128,1024]{0,1:T(8,128)(2,1)S(1)} %slice.404), channel_id=1, source_target_pairs={{8,0},{16,8},{24,16},{1,24},{9,1},{17,9},{25,17},{2,25},{10,2},{18... | collective-permute-start | bytes 786440 | tf_op jit(solution)/shard_map/ppermute | solution.py:509
  283.6 148.3 %reduce-scatter.7.cloned.1.call-start = ((), (), s32[]{:S(2)}) async-start(), calls=%async_computation.6 | async-start | bytes 983040 | tf_op jit(solution)/shard_map/reduce_scatter | solution.py:551
  287.5 144.4 %reduce-scatter.11.cloned.1.call-start = ((), (), s32[]{:S(2)}) async-start(), calls=%async_computation.8 | async-start | bytes 1966080 | tf_op jit(solution)/shard_map/reduce_scatter | solution.py:551
  291.3 195.8 %reduce-scatter.9.cloned.1.call-start = ((), (), s32[]{:S(2)}) async-start(), calls=%async_computation.7 | async-start | bytes 3932160 | tf_op jit(solution)/shard_map/reduce_scatter | solution.py:551
  297.8 231.9 %all-gather.11.cloned.1.call-start = ((), (), s32[]{:S(2)}) async-start(), calls=%async_computation.10 | async-start | bytes 2359296 | tf_op jit(solution)/shard_map/all_gather | solution.py:560
  302.1 43.3 %copy-start.38 = (f32[256,768]{1,0:T(8,128)}, f32[256,768]{1,0:T(8,128)S(1)}, u32[]{:S(2)}) copy-start(f32[256,768]{1,0:T(8,128)S(1)} %get-tuple-element.174) | copy-start | bytes 2359300
  345.4 187.7 %all-gather.5.cloned.1.call-start = ((), (), s32[]{:S(2)}) async-start(), calls=%async_computation.4 | async-start | bytes 3932160 | tf_op jit(solution)/shard_map/all_gather | solution.py:479
  364.1 174.0 %all-gather.7.cloned.1.call-start = ((), (), s32[]{:S(2)}) async-start(), calls=%async_computation.5 | async-start | bytes 3932160 | tf_op jit(solution)/shard_map/all_gather | solution.py:543
  373.5 20.3 %copy-start.27 = (bf16[3,256,2048]{2,1,0:T(8,128)(2,1)S(1)}, bf16[3,256,2048]{2,1,0:T(8,128)(2,1)}, u32[]{:S(2)}) copy-start(bf16[3,256,2048]{2,1,0:T(8,128)(2,1)} %copy-done.26) | copy-start | bytes 9437188
  375.5 18.3 %copy-start.37 = (bf16[2048,192]{0,1:T(8,128)(2,1)S(1)}, bf16[2048,192]{0,1:T(8,128)(2,1)}, u32[]{:S(2)}) copy-start(bf16[2048,192]{0,1:T(8,128)(2,1)} %copy.110) | copy-start | bytes 2359300
  400.9 22.0 %copy-start.35 = (f32[768,768]{1,0:T(8,128)S(1)}, f32[768,768]{1,0:T(8,128)}, u32[]{:S(2)}) copy-start(f32[768,768]{1,0:T(8,128)} %get-tuple-element.180) | copy-start | bytes 7077892
  401.6 21.3 %copy-start.106 = (f32[768]{0:T(1024)S(1)}, f32[768]{0:T(1024)}, u32[]{:S(2)}) copy-start(f32[768]{0:T(1024)} %param.29) | copy-start | bytes 9220
  401.6 21.3 %copy-start.123 = (pred[512]{0:T(512)(128)(4,1)S(1)}, pred[512]{0:T(512)(128)(4,1)}, u32[]{:S(2)}) copy-start(pred[512]{0:T(512)(128)(4,1)} %broadcast_compare_fusion) | copy-start | bytes 1540
  425.6 117.7 %all-gather.9.cloned.1.call-start = ((), (), s32[]{:S(2)}) async-start(), calls=%async_computation.9 | async-start | bytes 4718592 | tf_op jit(solution)/shard_map/all_gather | solution.py:557
  426.2 144.5 %all-reduce.6.cloned.1.call-start = ((), (), s32[]{:S(2)}) async-start(), calls=%async_computation.12 | async-start | bytes 6291456 | tf_op jit(solution)/shard_map/psum | solution.py:553
  (114 other events, 248.4 us)
Sparse Core Ops, SparseCore 0:
  247.7 97.6 all-reduce.7
  346.9 8.8 all-gather.10
  364.2 49.1 all-gather.4
  425.7 52.1 all-gather.6
  479.3 12.1 all-gather.8
Sparse Core Ops, SparseCore 1:
  283.7 46.1 reduce-scatter.12
  332.7 25.9 reduce-scatter.6
  361.5 57.3 reduce-scatter.10
  422.4 64.6 reduce-scatter.8
  491.1 79.5 all-reduce.5

commit v3 on v1

v3 whole, which is shorter than its diff:
```python
import functools

import jax
import jax.numpy as jnp
from jax import lax
from jax.experimental import pallas as pl
from jax.experimental.pallas import tpu as pltpu
from jax.sharding import Mesh
from jax.sharding import PartitionSpec as P

DH = 64
WIN = 128
EPSILON = 1e-06
NEGATIVE = -1e30
HIGHEST = lax.Precision.HIGHEST
F32 = jnp.float32
BF16 = jnp.bfloat16
SCALE = DH ** (-0.5)
DP = ("zz", "core")


def mm(a, b, ca, cb):
    return lax.dot_general(a, b, (((ca,), (cb,)), ((), ())), preferred_element_type=F32)


def norm_parts(values):
    r = lax.rsqrt(jnp.mean(values * values, axis=-1, keepdims=True) + EPSILON)
    return r, values * r


def norm_back(dn, xh, r, gain):
    g = dn * gain
    return r * (g - xh * jnp.mean(g * xh, axis=-1, keepdims=True))


def gelu_parts(u):
    c = 0.7978845608028654
    t = jnp.tanh(c * (u + 0.044715 * u * u * u))
    g = 0.5 * u * (1.0 + t)
    dg = 0.5 * (1.0 + t) + 0.5 * u * (1.0 - t * t) * c * (1.0 + 3 * 0.044715 * u * u)
    return g, dg


def feed(n, seed, w_gate, w_up, w_down):
    u = mm(n, w_gate, 1, 0)
    v = mm(n, w_up, 1, 0)
    g, dg = gelu_parts(u)
    hidden = (g * v).astype(BF16)
    out = mm(hidden, w_down, 1, 0)
    dh = mm(seed, w_down, 1, 1)
    du = (dh * v * dg).astype(BF16)
    dv = (dh * g).astype(BF16)
    dn = mm(du, w_gate, 1, 1) + mm(dv, w_up, 1, 1)
    dwg = mm(n, du, 0, 0)
    dwu = mm(n, dv, 0, 0)
    dwd = mm(hidden, seed, 0, 0)
    return out, dn, dwg, dwu, dwd


MESH = pl.DeviceIdType.MESH


def remote(src, dst, send, recv, device):
    return pltpu.make_async_remote_copy(
        src_ref=src, dst_ref=dst, send_sem=send, recv_sem=recv, device_id=device, device_id_type=MESH
    )


def greet(devices):
    barrier = pltpu.get_barrier_semaphore()
    for device in devices:
        pl.semaphore_signal(barrier, inc=1, device_id=device, device_id_type=MESH)
    pl.semaphore_wait(barrier, len(devices))


def here():
    return lax.axis_index("branch"), lax.axis_index("zz"), lax.axis_index("core")


def others(me, count):
    return [lax.rem(me + k, count) for k in range(1, count)]


def band(start, size):
    return pl.ds(pl.multiple_of(start, size), size)


def finish(copies):
    for copy in copies:
        if copy.is_remote:
            copy.wait_send()
        else:
            copy.wait()


class Pool:
    def __init__(self):
        self.names = []
        self.shapes = []

    def add(self, name, shape):
        self.names.append(name)
        self.shapes.append(shape)

    def vmem(self, name, shape, dtype=BF16):
        self.add(name, pltpu.VMEM(shape, dtype))

    def dma(self, name, *shape):
        self.add(name, pltpu.SemaphoreType.DMA(shape))

    def bind(self, refs):
        return dict(zip(self.names, refs, strict=True))


def group_sum_scratch(pool, nb, rows, width):
    for name in ("gs_sib", "gs_part", "gs_came"):
        pool.vmem(name, (nb, rows // 2 // nb, width))
    for name in ("sib", "rs", "ag", "fw"):
        pool.dma(f"gs_{name}_s", nb)
        pool.dma(f"gs_{name}_r", nb)


def group_sum_steps(nb, x, o, m, meanwhile=()):
    b, z, c = here()
    half = x.shape[0] // 2
    ch = half // nb
    twin = (b, z, 1 - c)
    peers = others(b, nb)
    sib, part, came = m["gs_sib"], m["gs_part"], m["gs_came"]
    work = list(meanwhile)

    def aside():
        if work:
            work.pop(0)()

    def rows(core, j):
        return band(core * half + j * ch, ch)

    order = peers + [b]
    to_twin = [
        remote(x.at[rows(1 - c, j)], sib.at[j], m["gs_sib_s"].at[j], m["gs_sib_r"].at[j], twin)
        for j in order
    ]
    for copy in to_twin:
        copy.start()
    sends = []
    for j, copy in zip(peers, to_twin):
        copy.wait_recv()
        part[j] = (x[rows(c, j)].astype(F32) + sib[j].astype(F32)).astype(BF16)
        send = remote(part.at[j], came.at[b], m["gs_rs_s"].at[j], m["gs_rs_r"].at[b], (j, z, c))
        send.start()
        sends.append(send)
    aside()
    to_twin[-1].wait_recv()
    total = x[rows(c, b)].astype(F32) + sib[b].astype(F32)
    for j in peers:
        remote(part.at[j], came.at[j], m["gs_rs_s"].at[j], m["gs_rs_r"].at[j], (j, z, c)).wait_recv()
        total = total + came[j].astype(F32)
    mine = o.at[rows(c, b)]
    mine[...] = total.astype(BF16)
    for j in peers:
        send = remote(mine, mine, m["gs_ag_s"].at[j], m["gs_ag_r"].at[b], (j, z, c))
        send.start()
        sends.append(send)
    send = remote(mine, mine, m["gs_fw_s"].at[b], m["gs_fw_r"].at[b], twin)
    send.start()
    sends.append(send)
    aside()
    for j in peers:
        piece = o.at[rows(c, j)]
        remote(piece, piece, m["gs_ag_s"].at[j], m["gs_ag_r"].at[j], (j, z, c)).wait_recv()
        send = remote(piece, piece, m["gs_fw_s"].at[j], m["gs_fw_r"].at[j], twin)
        send.start()
        sends.append(send)
    while work:
        aside()
    for j in order:
        piece = o.at[rows(1 - c, j)]
        remote(piece, piece, m["gs_fw_s"].at[j], m["gs_fw_r"].at[j], twin).wait_recv()
    finish(to_twin + sends)


def sum_kernel(nb, pool, x, o, *scratch):
    b, z, c = here()
    greet([(b, z, 1 - c)] + [(j, z, c) for j in others(b, nb)])
    group_sum_steps(nb, x, o, pool.bind(scratch))


def group_sum(x, nb, cid):
    rows, width = x.shape
    pool = Pool()
    group_sum_scratch(pool, nb, rows, width)
    return pl.pallas_call(
        functools.partial(sum_kernel, nb, pool),
        out_shape=jax.ShapeDtypeStruct(x.shape, BF16),
        in_specs=[VM],
        out_specs=VM,
        scratch_shapes=pool.shapes,
        compiler_params=pltpu.CompilerParams(
            collective_id=cid, has_side_effects=True, vmem_limit_bytes=40 << 20
        ),
    )(x)


VM = pl.BlockSpec(memory_space=pltpu.VMEM)
HB = pl.BlockSpec(memory_space=pl.ANY)


def normed(x, gain):
    x = x.astype(F32)
    r = lax.rsqrt(jnp.mean(x * x, axis=-1, keepdims=True) + EPSILON)
    return (x * r * gain).astype(BF16)


def head_lanes(shape, h, dim):
    place = lax.broadcasted_iota(jnp.int32, shape, dim)
    return (place >= h * DH) & (place < (h + 1) * DH)


def only_head(x, h):
    return jnp.where(head_lanes(x.shape, h, 1), x, jnp.zeros_like(x))


def near_keys(shape, key_dim, first, total):
    key = lax.broadcasted_iota(jnp.int32, shape, key_dim)
    query = lax.broadcasted_iota(jnp.int32, shape, 1 - key_dim)
    gap = key - query
    return (gap >= 0) & (gap <= 2 * WIN) & (key + first >= 0) & (key + first < total)


def hot_rows(ids, count):
    spot = lax.broadcasted_iota(jnp.int32, (ids.shape[0], count), 1)
    return jnp.where(ids == spot, 1.0, 0.0).astype(BF16)


FRONT_OUT = (
    "tok_r", "cot_r", "first_r", "gate", "qr", "kv", "lh", "lm", "le", "lr", "first_w",
    "q", "k", "v", "ctx_l", "attn_l", "ctx_r", "attn_r", "mixed",
)


def front_kernel(nb, nz, pool, *refs):
    tokens, cotangent, ids, gain, router, rheads, rmerge, s_lh, s_lm, s_le, s_lr = refs[:11]
    out = dict(zip(FRONT_OUT, refs[11 : 11 + len(FRONT_OUT)]))
    m = pool.bind(refs[11 + len(FRONT_OUT) :])
    b, z, c = here()
    twin = (b, z, 1 - c)
    bpeers, zpeers = others(b, nb), others(z, nz)
    rows, D = tokens.shape
    own = rows // nb
    cap = ids.shape[0]
    half = cap // 2
    rw = rmerge.shape[0]
    after = (b, lax.rem(z + c, nz), 1 - c)
    before = (b, lax.rem(z + nz - 1 + c, nz), 1 - c)
    far = (b, lax.rem(z + nz - 1 + 2 * c, nz), 1 - c)
    greet([twin, far] + [(j, z, c) for j in bpeers] + [(b, j, c) for j in zpeers])
    sends = []

    def go(copy):
        copy.start()
        sends.append(copy)

    pairs = [(s_lh, out["lh"]), (s_lm, out["lm"]), (s_le, out["le"]), (s_lr, out["lr"])]

    def place(i, j):
        src, dst = pairs[i]
        if i in (0, 2):
            return dst.at[:, :, band(j * src.shape[2], src.shape[2])]
        return dst.at[band(j * src.shape[0], src.shape[0])]

    def cut(i, ref, core):
        if i in (0, 2):
            size = ref.shape[1] // 2
            return ref.at[:, band(core * size, size)]
        size = ref.shape[0] // 2
        return ref.at[band(core * size, size)]

    for i in range(4):
        for j in bpeers:
            go(remote(cut(i, pairs[i][0], c), cut(i, place(i, b), c), m["w_s"].at[i, j], m["w_r"].at[i, b], (j, z, c)))
    for i in range(4):
        go(pltpu.make_async_copy(pairs[i][0], place(i, b), m["own_s"].at[i]))
    halo = m["halo"]
    go(remote(tokens.at[pl.ds(rows - WIN, WIN)], halo.at[0], m["halo_s"].at[0], m["halo_r"].at[0], after))
    go(remote(tokens.at[pl.ds(0, WIN)], halo.at[1], m["halo_s"].at[1], m["halo_r"].at[1], before))

    picks, sib = m["picks"], m["sib"]
    step = cap // 4
    for k in range(4):
        at = pl.ds(k * step, step)
        hot = hot_rows(ids[at], rows)
        picks[at, :D] = mm(hot, tokens[...], 1, 0).astype(BF16)
        picks[at, D:] = mm(hot, cotangent[...], 1, 0).astype(BF16)
        go(remote(picks.at[at], sib.at[at], m["pick_s"].at[k], m["pick_r"].at[k], twin))
    for k in range(4):
        at = pl.ds(k * step, step)
        remote(picks.at[at], sib.at[at], m["pick_s"].at[k], m["pick_r"].at[k], twin).wait_recv()
        tok = picks[at, :D].astype(F32) + sib[at, :D].astype(F32)
        out["tok_r"][at] = tok.astype(BF16)
        out["cot_r"][at] = (picks[at, D:].astype(F32) + sib[at, D:].astype(F32)).astype(BF16)
        first = normed(tok, gain[...])
        out["first_r"][at] = first
        logit = jnp.sum(first.astype(F32) * router[...], axis=-1, keepdims=True)
        out["gate"][at] = 1.0 / (1.0 + jnp.exp(-logit))

    own_rows = out["first_r"][band(c * half, half)]
    out["qr"][...] = mm(own_rows, rheads[0], 1, 1).astype(BF16)
    kv = out["kv"]
    mine = kv.at[band((2 * z + c) * half, half)]
    mine[:, :rw] = mm(own_rows, rheads[1], 1, 1).astype(BF16)
    mine[:, rw:] = mm(own_rows, rheads[2], 1, 1).astype(BF16)
    for j in zpeers:
        go(remote(mine, mine, m["kv_s"].at[j], m["kv_r"].at[z], (b, j, c)))
    go(remote(mine, mine, m["kf_s"].at[z], m["kf_r"].at[z], twin))

    first_w = out["first_w"]
    first_w[pl.ds(WIN, own)] = normed(tokens[band(b * own, own)], gain[...])
    for i in range(2):
        remote(halo.at[i], halo.at[i], m["halo_s"].at[i], m["halo_r"].at[i], twin).wait_recv()
    lead = tokens[band(jnp.maximum(b * own - WIN, 0), WIN)]
    trail = tokens[band(jnp.minimum((b + 1) * own, rows - WIN), WIN)]
    first_w[pl.ds(0, WIN)] = normed(jnp.where(b > 0, lead, halo[0]), gain[...])
    first_w[pl.ds(WIN + own, WIN)] = normed(jnp.where(b < nb - 1, trail, halo[1]), gain[...])

    def pass_weights(i):
        for j in bpeers:
            dst = cut(i, place(i, j), c)
            remote(dst, dst, m["w_s"].at[i, j], m["w_r"].at[i, j], (j, z, c)).wait_recv()
            go(remote(dst, dst, m["wf_s"].at[i, j], m["wf_r"].at[i, j], twin))

    def take_weights(i):
        for j in bpeers:
            dst = cut(i, place(i, j), 1 - c)
            remote(dst, dst, m["wf_s"].at[i, j], m["wf_r"].at[i, j], twin).wait_recv()

    pass_weights(0)
    for j in zpeers:
        piece = kv.at[band((2 * j + c) * half, half)]
        remote(piece, piece, m["kv_s"].at[j], m["kv_r"].at[j], (b, j, c)).wait_recv()
        go(remote(piece, piece, m["kf_s"].at[j], m["kf_r"].at[j], twin))
    take_weights(0)
    pltpu.make_async_copy(pairs[0][0], place(0, b), m["own_s"].at[0]).wait()
    lh, q, k, v = out["lh"], out["q"], out["k"], out["v"]
    q[...] = mm(first_w[pl.ds(WIN, own)], lh[0], 1, 0).astype(BF16)
    k[...] = mm(first_w[...], lh[1], 1, 0).astype(BF16)
    v[...] = mm(first_w[...], lh[2], 1, 0).astype(BF16)
    pass_weights(1)

    blocks = own // WIN
    ctx = out["ctx_l"]
    first_key = (2 * z + c) * rows + b * own - WIN
    total = 2 * nz * rows

    def light(i, carry):
        g, n = i // blocks, lax.rem(i, blocks)
        lanes = band(g * 2 * DH, 2 * DH)
        at = band(n * WIN, WIN)
        keys = pl.ds(pl.multiple_of(n * WIN, WIN), 3 * WIN)
        q2, k2, v2 = q[at, lanes], k[keys, lanes], v[keys, lanes]
        allowed = near_keys((WIN, 3 * WIN), 1, first_key + n * WIN, total)
        parts = []
        for h in range(2):
            s = jnp.where(allowed, mm(only_head(q2, h), k2, 1, 1) * SCALE, NEGATIVE)
            w = jnp.exp(s - jnp.max(s, axis=-1, keepdims=True))
            p = (w / jnp.sum(w, axis=-1, keepdims=True)).astype(BF16)
            parts.append(mm(p, v2, 1, 0))
        ctx[at, lanes] = jnp.where(head_lanes((WIN, 2 * DH), 0, 1), parts[0], parts[1]).astype(BF16)
        return carry

    lax.fori_loop(0, blocks * (q.shape[1] // (2 * DH)), light, 0)
    take_weights(1)
    pltpu.make_async_copy(pairs[1][0], place(1, b), m["own_s"].at[1]).wait()
    attn_l = out["attn_l"]
    attn_l[...] = mm(ctx[...], out["lm"][...], 1, 0)

    for j in zpeers + [z]:
        piece = kv.at[band((2 * j + 1 - c) * half, half)]
        remote(piece, piece, m["kf_s"].at[j], m["kf_r"].at[j], twin).wait_recv()
    keys, values, qr, ctx_r = m["keys"], m["values"], out["qr"], out["ctx_r"]
    keys[...] = kv[:, :rw]
    values[...] = kv[:, rw:]
    some = 64

    def heavy(i, carry):
        at = band(i * some, some)
        got = jnp.zeros((some, rw), F32)
        for h in range(rw // DH):
            s = mm(only_head(qr[at], h), keys[...], 1, 1) * SCALE
            w = jnp.exp(s - jnp.max(s, axis=-1, keepdims=True))
            p = (w / jnp.sum(w, axis=-1, keepdims=True)).astype(BF16)
            got = jnp.where(head_lanes((some, rw), h, 1), mm(p, values[...], 1, 0), got)
        ctx_r[at] = got.astype(BF16)
        return carry

    lax.fori_loop(0, half // some, heavy, 0)
    attn_r = out["attn_r"]
    attn_r[...] = mm(ctx_r[...], rmerge[...], 1, 0)

    part = m["part"]
    mine_at, other_at = band(c * half, half), band((1 - c) * half, half)
    low = attn_l[...].astype(BF16)
    part[other_at] = mm(hot_rows(ids[other_at] - b * own, own), low, 1, 0).astype(BF16)
    part[mine_at] = (
        mm(hot_rows(ids[mine_at] - b * own, own), low, 1, 0) + out["gate"][mine_at] * attn_r[...]
    ).astype(BF16)
    group_sum_steps(nb, part, out["mixed"], m, [lambda: pass_weights(2), lambda: pass_weights(3)])
    take_weights(2)
    take_weights(3)
    finish([copy for copy in sends if copy.is_remote])
    for i in (2, 3):
        pltpu.make_async_copy(pairs[i][0], place(i, b), m["own_s"].at[i]).wait()


def front(nb, nz, tokens, cotangent, ids, gain, router, rheads, rmerge, s_lh, s_lm, s_le, s_lr):
    rows, D = tokens.shape
    own = rows // nb
    cap = ids.shape[0]
    half = cap // 2
    rw = rmerge.shape[0]
    wl = nb * s_lm.shape[0]
    shape = lambda *dims: jax.ShapeDtypeStruct(dims, BF16)
    shape32 = lambda *dims: jax.ShapeDtypeStruct(dims, F32)
    outs = dict(
        tok_r=shape(cap, D), cot_r=shape(cap, D), first_r=shape(cap, D), gate=shape32(cap, 1),
        qr=shape(half, rw), kv=shape(2 * nz * half, 2 * rw),
        lh=shape(3, D, wl), lm=shape(wl, D),
        le=shape(2, D, nb * s_le.shape[2]), lr=shape(nb * s_lr.shape[0], D),
        first_w=shape(own + 2 * WIN, D), q=shape(own, wl), k=shape(own + 2 * WIN, wl),
        v=shape(own + 2 * WIN, wl), ctx_l=shape(own, wl), attn_l=shape32(own, D),
        ctx_r=shape(half, rw), attn_r=shape32(half, D), mixed=shape(cap, D),
    )
    pool = Pool()
    pool.vmem("picks", (cap, 2 * D))
    pool.vmem("sib", (cap, 2 * D))
    pool.vmem("halo", (2, WIN, D))
    pool.vmem("keys", (2 * nz * half, rw))
    pool.vmem("values", (2 * nz * half, rw))
    pool.vmem("part", (cap, D))
    group_sum_scratch(pool, nb, cap, D)
    pool.dma("own_s", 4)
    pool.dma("halo_s", 2)
    pool.dma("halo_r", 2)
    pool.dma("pick_s", 4)
    pool.dma("pick_r", 4)
    for name in ("w", "wf"):
        pool.dma(f"{name}_s", 4, nb)
        pool.dma(f"{name}_r", 4, nb)
    for name in ("kv", "kf"):
        pool.dma(f"{name}_s", nz)
        pool.dma(f"{name}_r", nz)
    got = pl.pallas_call(
        functools.partial(front_kernel, nb, nz, pool),
        out_shape=tuple(outs[name] for name in FRONT_OUT),
        in_specs=[VM] * 7 + [HB] * 4,
        out_specs=tuple(HB if name in ("le", "lr") else VM for name in FRONT_OUT),
        scratch_shapes=pool.shapes,
        compiler_params=pltpu.CompilerParams(
            collective_id=0, has_side_effects=True, vmem_limit_bytes=56 << 20
        ),
    )(tokens, cotangent, ids, gain, router, rheads, rmerge, s_lh, s_lm, s_le, s_lr)
    return dict(zip(FRONT_OUT, got))


BACK_OUT = ("gf_r", "gf_l", "d_lh", "d_lm", "d_rh", "d_rm", "router")
BACK_IN = (
    "gm_own", "gm_r", "gate", "gate_feed", "ids", "q", "k", "v", "lm", "lh", "first_w", "ctx_l",
    "qr", "kv", "rmerge", "rheads", "first_r", "ctx_r", "attn_r", "router_vector",
)


def back_names(inner):
    return BACK_IN if inner else BACK_IN + ("trio",)


def heavy_back(i, m, seed, x):
    kv, qr = i["kv"], i["qr"]
    half, rw = qr.shape
    keys, values, keys_t, dk, dv, dq_t, do = (
        m[n] for n in ("keys", "values", "keys_t", "dk", "dv", "dq_t", "do")
    )
    keys[...] = kv[:, :rw]
    values[...] = kv[:, rw:]
    keys_t[...] = keys[...].T
    do[...] = mm(seed, i["rmerge"][...], 1, 1).astype(BF16)
    dk[...] = jnp.zeros_like(dk)
    dv[...] = jnp.zeros_like(dv)
    dq_t[...] = jnp.zeros_like(dq_t)
    some = 128

    def heavy(n, carry):
        at = band(n * some, some)
        for h in range(rw // DH):
            qh, doh = only_head(qr[at], h), only_head(do[at], h)
            s = mm(keys[...], qh, 1, 1) * SCALE
            w = jnp.exp(s - jnp.max(s, axis=0, keepdims=True))
            p = w * (1.0 / jnp.sum(w, axis=0, keepdims=True))
            dp = mm(values[...], doh, 1, 1)
            ds = (p * (dp - jnp.sum(p * dp, axis=0, keepdims=True))).astype(BF16)
            dk[...] += mm(ds, qh, 1, 0)
            dv[...] += mm(p.astype(BF16), doh, 1, 0)
            got = mm(keys_t[...], ds, 1, 0)
            dq_t[:, at] += jnp.where(head_lanes(got.shape, h, 0), got, 0.0)
        return carry

    lax.fori_loop(0, half // some, heavy, 0)
    x[:, :rw] = (dk[...] * SCALE).astype(BF16)
    x[:, rw:] = dv[...].astype(BF16)


def heavy_back_plain(i):
    half, rw = i["qr"].shape
    split = lambda y: y.reshape(y.shape[0], -1, DH)
    at = lax.axis_index("core") * half
    seed = (i["gate"] * i["gm_r"]).astype(BF16)
    seed = lax.dynamic_slice(seed, (at, 0), (half, seed.shape[1]))
    do = split(mm(seed, i["rmerge"], 1, 1).astype(BF16))
    q, k, v = split(i["qr"]), split(i["kv"][:, :rw]), split(i["kv"][:, rw:])
    p = jax.nn.softmax(jnp.einsum("qhe,khe->hqk", q, k, preferred_element_type=F32) * SCALE, axis=-1)
    dp = jnp.einsum("qhe,khe->hqk", do, v, preferred_element_type=F32)
    ds = (p * (dp - jnp.sum(p * dp, -1, keepdims=True))).astype(BF16)
    dq = jnp.einsum("hqk,khe->qhe", ds, k, preferred_element_type=F32) * SCALE
    dk = jnp.einsum("hqk,qhe->khe", ds, q, preferred_element_type=F32) * SCALE
    dv = jnp.einsum("hqk,qhe->khe", p.astype(BF16), do, preferred_element_type=F32)
    both = jnp.concatenate([dk.reshape(-1, rw), dv.reshape(-1, rw)], 1).astype(BF16)
    both = lax.psum_scatter(both, DP, scatter_dimension=0, tiled=True)
    return jnp.stack([dq.reshape(half, rw).astype(BF16), both[:, :rw], both[:, rw:]], 0)


def back_kernel(nb, nz, pool, inner, *refs):
    names = back_names(inner)
    i = dict(zip(names, refs[: len(names)]))
    out = dict(zip(BACK_OUT, refs[len(names) : len(names) + len(BACK_OUT)]))
    m = pool.bind(refs[len(names) + len(BACK_OUT) :])
    b, z, c = here()
    twin = (b, z, 1 - c)
    bpeers, zpeers = others(b, nb), others(z, nz)
    own, D = i["gm_own"].shape
    rows = own * nb
    cap = i["ids"].shape[0]
    half = cap // 2
    rw = i["rmerge"].shape[0]
    wl = i["q"].shape[1]
    last, first = b == nb - 1, b == 0
    after = (
        jnp.where(last, 0, b + 1), jnp.where(last, lax.rem(z + c, nz), z), jnp.where(last, 1 - c, c),
    )
    before = (
        jnp.where(first, nb - 1, b - 1),
        jnp.where(first, lax.rem(z + nz - 1 + c, nz), z),
        jnp.where(first, 1 - c, c),
    )
    greet([twin, after, before] + [(j, z, c) for j in bpeers] + [(b, j, c) for j in zpeers])
    mine_at, other_at = band(c * half, half), band((1 - c) * half, half)
    sends = []

    def go(copy):
        copy.start()
        sends.append(copy)

    gm_half = i["gm_r"][mine_at]
    gate_half = i["gate"][mine_at]
    seed = (gate_half * gm_half).astype(BF16)
    out["d_rm"][...] = mm(i["ctx_r"][...], seed, 0, 0).astype(BF16)
    trio = m["trio"] if inner else i["trio"]

    def spot(core, j):
        return band((2 * j + core) * half, half)

    def to_twin(j):
        return remote(x.at[spot(1 - c, j)], sib.at[j], m["bs_sib_s"].at[j], m["bs_sib_r"].at[j], twin)

    if inner:
        x, sib, part, came = m["dkv"], m["bs_sib"], m["bs_part"], m["bs_came"]
        heavy_back(i, m, seed, x)
        for j in zpeers + [z]:
            go(to_twin(j))

    low, do_l = m["low"], m["do_l"]
    low[...] = i["gm_own"][...].astype(BF16)
    do_l[...] = mm(low[...], i["lm"][...], 1, 1).astype(BF16)
    for j in zpeers if inner else []:
        to_twin(j).wait_recv()
        part[j] = (x[spot(c, j)].astype(F32) + sib[j].astype(F32)).astype(BF16)
        go(remote(part.at[j], came.at[z], m["bs_rs_s"].at[j], m["bs_rs_r"].at[z], (b, j, c)))

    q, k, v = i["q"], i["k"], i["v"]
    lk_t, dkl, dvl, dql = m["lk_t"], m["dkl"], m["dvl"], m["dql"]
    lk_t[...] = k[...].T
    dkl[...] = jnp.zeros_like(dkl)
    dvl[...] = jnp.zeros_like(dvl)
    blocks = own // WIN
    first_key = (2 * z + c) * rows + b * own - WIN
    total = 2 * nz * rows

    def light(n_, carry):
        g, n = n_ // blocks, lax.rem(n_, blocks)
        lanes = band(g * 2 * DH, 2 * DH)
        at = band(n * WIN, WIN)
        near = pl.ds(pl.multiple_of(n * WIN, WIN), 3 * WIN)
        q2, do2, k2, v2, kt2 = q[at, lanes], do_l[at, lanes], k[near, lanes], v[near, lanes], lk_t[lanes, near]
        allowed = near_keys((3 * WIN, WIN), 0, first_key + n * WIN, total)
        got_k = got_v = None
        got_q = []
        for h in range(2):
            qh, doh = only_head(q2, h), only_head(do2, h)
            s = jnp.where(allowed, mm(k2, qh, 1, 1) * SCALE, NEGATIVE)
            w = jnp.exp(s - jnp.max(s, axis=0, keepdims=True))
            p = w * (1.0 / jnp.sum(w, axis=0, keepdims=True))
            dp = mm(v2, doh, 1, 1)
            ds = (p * (dp - jnp.sum(p * dp, axis=0, keepdims=True))).astype(BF16)
            one_k, one_v = mm(ds, qh, 1, 0), mm(p.astype(BF16), doh, 1, 0)
            got_k = one_k if got_k is None else got_k + one_k
            got_v = one_v if got_v is None else got_v + one_v
            got_q.append(mm(kt2, ds, 1, 0))
        dkl[near, lanes] += got_k
        dvl[near, lanes] += got_v
        both = jnp.where(head_lanes((2 * DH, WIN), 0, 0), got_q[0], got_q[1])
        dql[at, lanes] = (both.T * SCALE).astype(BF16)
        return carry

    lax.fori_loop(0, blocks * (wl // (2 * DH)), light, 0)
    rim, came_rim = m["rim"], m["came_rim"]
    for n, start in ((0, WIN + own), (1, 0)):
        rim[n, :, :wl] = (dkl[pl.ds(start, WIN)] * SCALE).astype(BF16)
        rim[n, :, wl:] = dvl[pl.ds(start, WIN)].astype(BF16)
    go(remote(rim.at[0], came_rim.at[0], m["rim_s"].at[0], m["rim_r"].at[0], after))
    go(remote(rim.at[1], came_rim.at[1], m["rim_s"].at[1], m["rim_r"].at[1], before))

    if inner:
        to_twin(z).wait_recv()
        mine = x[spot(c, z)].astype(F32) + sib[z].astype(F32)
        for j in zpeers:
            remote(part.at[j], came.at[j], m["bs_rs_s"].at[j], m["bs_rs_r"].at[j], (b, j, c)).wait_recv()
            mine = mine + came[j].astype(F32)
        trio[0] = (m["dq_t"][...].T * SCALE).astype(BF16)
        trio[1] = mine[:, :rw].astype(BF16)
        trio[2] = mine[:, rw:].astype(BF16)
    rheads = i["rheads"]
    picked = mm(trio[0], rheads[0], 1, 0) + mm(trio[1], rheads[1], 1, 0) + mm(trio[2], rheads[2], 1, 0)

    for n, device in ((0, before), (1, after)):
        remote(rim.at[n], came_rim.at[n], m["rim_s"].at[n], m["rim_r"].at[n], device).wait_recv()
    dkl[pl.ds(WIN, WIN)] += came_rim[0, :, :wl].astype(F32) * (1.0 / SCALE)
    dvl[pl.ds(WIN, WIN)] += came_rim[0, :, wl:].astype(F32)
    dkl[pl.ds(own, WIN)] += came_rim[1, :, :wl].astype(F32) * (1.0 / SCALE)
    dvl[pl.ds(own, WIN)] += came_rim[1, :, wl:].astype(F32)
    dk_own, dv_own = m["dk_own"], m["dv_own"]
    dk_own[...] = (dkl[pl.ds(WIN, own)] * SCALE).astype(BF16)
    dv_own[...] = dvl[pl.ds(WIN, own)].astype(BF16)
    lh = i["lh"]
    gf_l = out["gf_l"]
    gf_l[...] = mm(dql[...], lh[0], 1, 1) + mm(dk_own[...], lh[1], 1, 1) + mm(dv_own[...], lh[2], 1, 1)

    gate, first_r = i["gate"], i["first_r"]
    gate_attn = jnp.sum(gm_half * i["attn_r"][...], axis=-1, keepdims=True)
    total_part = m["part"]
    low_gf = gf_l[...].astype(BF16)
    router_sum = None
    for at, extra, more in ((other_at, None, None), (mine_at, gate_attn, picked)):
        g = gate[at]
        d_gate = i["gate_feed"][at] if extra is None else i["gate_feed"][at] + extra
        d_logit = d_gate * g * (1.0 - g)
        one = jnp.sum(d_logit * first_r[at].astype(F32), axis=0, keepdims=True)
        router_sum = one if router_sum is None else router_sum + one
        sum_ = mm(hot_rows(i["ids"][at] - b * own, own), low_gf, 1, 0) + d_logit * i["router_vector"][...]
        if more is not None:
            sum_ = sum_ + more
        total_part[at] = sum_.astype(BF16)
    out["router"][...] = router_sum

    def weights_light():
        first_t = m["first_t"]
        first_t[...] = i["first_w"][pl.ds(WIN, own)].T
        out["d_lh"][0] = mm(first_t[...], dql[...], 1, 0).astype(BF16)
        out["d_lh"][1] = mm(first_t[...], dk_own[...], 1, 0).astype(BF16)

    def weights_rest():
        out["d_lh"][2] = mm(m["first_t"][...], dv_own[...], 1, 0).astype(BF16)
        out["d_lm"][...] = mm(i["ctx_l"][...], low[...], 0, 0).astype(BF16)
        first_half = first_r[mine_at]
        for n in range(3):
            out["d_rh"][n] = mm(trio[n], first_half, 0, 0).astype(BF16)

    group_sum_steps(nb, total_part, out["gf_r"], m, [weights_light, weights_rest])
    finish(sends)


def back(nb, nz, given):
    own, D = given["gm_own"].shape
    cap = given["ids"].shape[0]
    half = cap // 2
    rw = given["rmerge"].shape[0]
    wl = given["q"].shape[1]
    deep = 2 * nz * half
    shape = lambda *dims: jax.ShapeDtypeStruct(dims, BF16)
    outs = dict(
        gf_r=shape(cap, D), gf_l=jax.ShapeDtypeStruct((own, D), F32), d_lh=shape(3, D, wl),
        d_lm=shape(wl, D), d_rh=shape(3, rw, D), d_rm=shape(rw, D),
        router=jax.ShapeDtypeStruct((1, D), F32),
    )
    pool = Pool()
    inner = deep <= 4096
    if inner:
        pool.vmem("keys", (deep, rw))
        pool.vmem("values", (deep, rw))
        pool.vmem("keys_t", (rw, deep))
        pool.vmem("dk", (deep, rw), F32)
        pool.vmem("dv", (deep, rw), F32)
        pool.vmem("dq_t", (rw, half), F32)
        pool.vmem("do", (half, rw))
        pool.vmem("trio", (3, half, rw))
        pool.vmem("dkv", (deep, 2 * rw))
        for name in ("bs_sib", "bs_part", "bs_came"):
            pool.vmem(name, (nz, half, 2 * rw))
    pool.vmem("low", (own, D))
    pool.vmem("do_l", (own, wl))
    pool.vmem("lk_t", (wl, own + 2 * WIN))
    pool.vmem("dkl", (own + 2 * WIN, wl), F32)
    pool.vmem("dvl", (own + 2 * WIN, wl), F32)
    pool.vmem("dql", (own, wl))
    pool.vmem("dk_own", (own, wl))
    pool.vmem("dv_own", (own, wl))
    pool.vmem("rim", (2, WIN, 2 * wl))
    pool.vmem("came_rim", (2, WIN, 2 * wl))
    pool.vmem("first_t", (D, own))
    pool.vmem("part", (cap, D))
    group_sum_scratch(pool, nb, cap, D)
    for name in ("bs_sib", "bs_rs") if inner else ():
        pool.dma(f"{name}_s", nz)
        pool.dma(f"{name}_r", nz)
    if not inner:
        given = dict(given, trio=heavy_back_plain(given))
    pool.dma("rim_s", 2)
    pool.dma("rim_r", 2)
    got = pl.pallas_call(
        functools.partial(back_kernel, nb, nz, pool, inner),
        out_shape=tuple(outs[name] for name in BACK_OUT),
        in_specs=[VM] * len(back_names(inner)),
        out_specs=(VM,) * len(BACK_OUT),
        scratch_shapes=pool.shapes,
        compiler_params=pltpu.CompilerParams(
            collective_id=3, has_side_effects=True, vmem_limit_bytes=60 << 20
        ),
    )(*(given[name] for name in back_names(inner)))
    return dict(zip(BACK_OUT, got))


def per_device(
    tokens,
    cotangent,
    gain_before,
    gain_middle,
    router_vector,
    local_heads,
    local_merge,
    routed_heads,
    routed_merge,
    local_expand,
    local_reduce,
    routed_expand,
    routed_reduce,
    routed_slots,
    routed_counts,
):
    nb = lax.axis_size("branch")
    nz = lax.axis_size("zz")
    b = lax.axis_index("branch")
    z = lax.axis_index("zz")
    core = lax.axis_index("core")
    d = 2 * z + core
    rows, D = tokens.shape
    own = rows // nb
    cap = routed_slots.shape[0]
    half = cap // 2
    fh = routed_expand.shape[2] // 2

    n_own = routed_counts[d]
    offset = jnp.where(core == 0, 0, cap - n_own)
    ranks = jnp.arange(cap, dtype=jnp.int32)
    live = (ranks >= offset) & (ranks < offset + n_own)
    twice = jnp.concatenate([routed_slots, routed_slots])
    rolled = lax.dynamic_slice(twice, (jnp.mod(cap - offset, cap),), (cap,))
    ids = jnp.where(live, rolled, -1)[:, None]
    pick_own = (ids - b * own == jnp.arange(own, dtype=jnp.int32)[None, :]).astype(BF16)
    mask_own = (jnp.sum(pick_own.astype(F32), 0) > 0.5)[:, None]

    rheads = routed_heads.transpose(1, 2, 0)
    f = front(
        nb, nz, tokens, cotangent, ids, gain_before[None], router_vector[None], rheads, routed_merge,
        local_heads.transpose(1, 0, 2), local_merge, local_expand.transpose(1, 0, 2), local_reduce,
    )
    gate, mixed_r, local_attn = f["gate"], f["mixed"], f["attn_l"]
    tok_r, cot_r = f["tok_r"].astype(F32), f["cot_r"].astype(F32)
    tok_own = lax.dynamic_slice(tokens, (b * own, 0), (own, D)).astype(F32)
    cot_own = lax.dynamic_slice(cotangent, (b * own, 0), (own, D))
    r1, xh1 = norm_parts(tok_own)

    mixed_own = jnp.where(mask_own, mm(pick_own, mixed_r, 0, 0), local_attn)
    middle_own = tok_own + mixed_own
    middle_r = tok_r + mixed_r.astype(F32)
    r2, xh2 = norm_parts(middle_own)
    second_own = (xh2 * gain_middle).astype(BF16)
    r2r, xh2r = norm_parts(middle_r)
    second_r = (xh2r * gain_middle).astype(BF16)

    ff_l, dn_l, d_lg, d_lu, d_ld = feed(second_own, cot_own, f["le"][0], f["le"][1], f["lr"])
    re_half = lax.dynamic_slice(routed_expand, (0, 0, core * fh), (D, 2, fh))
    rr_half = lax.dynamic_slice(routed_reduce, (core * fh, 0), (fh, D))
    seed_r = (gate * cot_r).astype(BF16)
    ff_r, dn_r, d_rg, d_ru, d_rd = feed(second_r, seed_r, re_half[:, 0], re_half[:, 1], rr_half)
    gate_feed = jnp.sum(cot_r * ff_r, -1, keepdims=True)

    both = jnp.concatenate(
        [ff_r.astype(BF16), (dn_r + mm(pick_own, dn_l.astype(BF16), 1, 0)).astype(BF16)], 1
    )
    both = group_sum(both, nb, 2)
    ffr_sum, dn2_r = both[:, :D].astype(F32), both[:, D:]
    layer_own = (
        middle_own + ff_l + mm(pick_own, (gate * ffr_sum).astype(BF16), 0, 0)
    ).astype(BF16)
    layer_output = lax.all_gather(layer_own, "branch", axis=0, tiled=True).astype(F32)

    dn2_own = jnp.where(mask_own, mm(pick_own, dn2_r, 0, 0), dn_l)
    gm_own = cot_own.astype(F32) + norm_back(dn2_own, xh2, r2, gain_middle)
    gm_r = cot_r + norm_back(dn2_r.astype(F32), xh2r, r2r, gain_middle)
    delta_gain_middle = jnp.sum(dn2_own * xh2, 0)

    k = back(
        nb, nz,
        dict(
            f, gm_own=gm_own, gm_r=gm_r, gate_feed=gate_feed, ids=ids, rmerge=routed_merge,
            rheads=rheads, router_vector=router_vector[None],
        ),
    )
    gf_own = jnp.where(mask_own, mm(pick_own, k["gf_r"], 0, 0), k["gf_l"])
    td_own = (gm_own + norm_back(gf_own, xh1, r1, gain_before)).astype(BF16)
    delta_gain_before = jnp.sum(gf_own * xh1, 0)
    tokens_delta = lax.all_gather(td_own, "branch", axis=0, tiled=True).astype(F32)

    vectors = lax.psum(
        jnp.stack([delta_gain_before, delta_gain_middle, k["router"][0]]).astype(F32),
        ("branch",) + DP,
    )

    def over_branch(x, dim):
        return lax.psum_scatter(x.astype(BF16), "branch", scatter_dimension=dim, tiled=True)

    g_le = lax.psum(over_branch(jnp.stack([d_lg, d_lu], 0), 2), DP)
    g_lr = lax.psum(over_branch(d_ld, 0), DP)
    g_lh = lax.psum(over_branch(k["d_lh"], 2), DP)
    g_lm = lax.psum(over_branch(k["d_lm"], 0), DP)
    g_re = lax.all_gather(
        lax.psum(jnp.stack([d_rg, d_ru], 0).astype(BF16), "zz"), "core", axis=2, tiled=True
    )
    g_rr = lax.all_gather(lax.psum(d_rd.astype(BF16), "zz"), "core", axis=0, tiled=True)
    g_rh = lax.psum(k["d_rh"], DP)
    g_rm = lax.psum(k["d_rm"], DP)
    return (
        layer_output,
        tokens_delta,
        vectors[0],
        vectors[1],
        vectors[2],
        g_lh.transpose(1, 0, 2).astype(F32),
        g_lm.astype(F32),
        g_rh.transpose(2, 0, 1).astype(F32),
        g_rm.astype(F32),
        g_le.transpose(1, 0, 2).astype(F32),
        g_lr.astype(F32),
        g_re.transpose(1, 0, 2).astype(F32),
        g_rr.astype(F32),
    )


def solution(mesh):
    nb = mesh.shape["branch"]
    fine = Mesh(mesh.devices.reshape(nb, -1, 2), ("branch", "zz", "core"))
    rows = P(DP, None)
    cols = P(None, None, "branch")
    deep = P("branch", None)
    return jax.shard_map(
        per_device,
        mesh=fine,
        in_specs=(
            rows, rows, P(), P(), P(), cols, deep, cols, deep, cols, deep, cols, deep, P(DP), P(),
        ),
        out_specs=(
            rows, rows, P(), P(), P(), cols, deep, cols, deep, cols, deep, cols, deep,
        ),
        check_vma=False,
    )
```

time: 699 us -> 555 us (0.79)
  Pallas kernels: 0 us -> 190 us
  waiting for transfers between devices: 356 us -> 177 us
  matrix products: 99.4 us -> 42.1 us
  local copies, waits for them, and re-layouts: 88 us -> 40.2 us
  other arithmetic: 60.8 us -> 37.9 us
  blocking collectives: 55.4 us -> 41 us
  starting transfers between devices: 10.8 us -> 0.82 us
    pallas_call x0 -> x3, Pallas kernels: none -> 190 us  [the longest x1 82 us: front(): pl.pallas_call(functools.partial(front_kernel, nb, nz, pool), out_shape=t...]
    psum x4 -> x0, waiting for transfers between devices: 121 us -> none  [the longest x1 54.6 us: per_device(): both = lax.psum(both, GROUP)]
    reduce_scatter x3, waiting for transfers between devices: 95.3 us -> 141 us  [over_branch(): lax.psum_scatter(x.astype(BF16), 'branch', scatter_dimension=dim, tiled=T...]
    all_gather x1, waiting for transfers between devices: 38.2 us -> 0.01 us  [per_device(): lax.all_gather(td_own, 'branch', axis=0, tiled=True).astype(F32)]
    psum x1, waiting for transfers between devices: 34.6 us -> 0.02 us  [per_device(): lax.psum(jnp.stack([d_rg, d_ru], 0).astype(BF16), 'zz')]
    dot_general x41 -> x23, matrix products: 76.3 us -> 42.1 us  [mm(): lax.dot_general(a, b, (((ca,), (cb,)), ((), ())), preferred_element_type=...]
    psum x1, waiting for transfers between devices: 50.5 us -> 17 us  [per_device(): g_le = lax.psum(over_branch(jnp.stack([d_lg, d_lu], 0), 2), DP)]
    dot_general x14 -> x0, matrix products: 22.3 us -> none  [the longest x1 4.57 us: per_device(): dp_ = jnp.einsum('nqhe,nkhe->nhqk', do4, vw, preferred_element_type=F32)]
  transfers between devices with their start and end apart: 23 -> 10, of which waited for: 12 -> 5; matrix products, arithmetic and copies ran while one was open for 26% -> 14% of each run, Pallas kernels for 0% -> 20%
where the time goes in v3:
time: 555 us; the launch traced here: 547 us
  Pallas kernels  190 us (34%)
  waiting for transfers between devices  177 us (32%)
  matrix products  42.1 us (8%)
  blocking collectives  41 us (7%)
  local copies, waits for them, and re-layouts  40.2 us (7%)
  other arithmetic  37.9 us (7%)
  between operations  17.8 us (3%)
    reduce_scatter x3, waiting for transfers between devices, over_branch(): lax.psum_scatter(x.astype(BF16), 'branch', scatter_dimension=dim, tiled=T...  141 us
    pallas_call x1, Pallas kernels, front(): pl.pallas_call(functools.partial(front_kernel, nb, nz, pool), out_shape=t...  82 us
    pallas_call x1, Pallas kernels, back(): pl.pallas_call(functools.partial(back_kernel, nb, nz, pool, inner), out_s...  81.6 us
    dot_general x23, matrix products, mm(): lax.dot_general(a, b, (((ca,), (cb,)), ((), ())), preferred_element_type=...  42.1 us
    psum x1, blocking collectives, per_device(): lax.psum(jnp.stack([delta_gain_before, delta_gain_middle, k['router'][0]]...  41 us
    unnamed x85, local copies, waits for them, and re-layouts  27.2 us
    pallas_call x1, Pallas kernels, group_sum(): pl.pallas_call(functools.partial(sum_kernel, nb, pool), out_shape=jax.Sha...  26.5 us
    unnamed x11, waiting for transfers between devices  18.7 us
  transfers between devices with their start and end apart: 10, of which 5 were waited for; matrix products, arithmetic and copies ran while one was open for 14% of the time, Pallas kernels for 20%

profile of v3, /device:TPU:0, one launch (start us, length us, event | category | flops | bytes accessed | tf_op | source)
XLA Modules:
  0.0 546.7 jit_solution(2897339003181410944)
XLA Ops:
  15.0 2.1 copy.67
  17.3 82.0 %shard_map.246 = (bf16[512,768]{1,0:T(8,128)(2,1)}, bf16[512,768]{1,0:T(8,128)(2,1)}, bf16[512,768]{1,0:T(8,128)(2,1)}, f32[512,1]{1,0:T(8,128)}, bf16[256,192]{...) custom-call(bf16[2048,768]{1,0:T(8,128)(2,1)} %refs_0_.1, ...), custom_call_target="tpu_custom_call" | custom-call | tf_op jit(solution)/shard_map/pallas_call | solution.py:452
  101.1 2.5 multiply_reduce_fusion.4
  103.7 6.8 %constant_dynamic-slice_fusion.1 = (bf16[768,1,512]{2,1,0:T(2,128)(2,1)}, bf16[768,1,512]{2,1,0:T(2,128)(2,1)S(1)}) fusion(bf16[768,2,1024]{2,1,0:T(2,128)(2,1)} %param.26, s32[]{:T(128)S(6)} %add.163, s32[]{:T(128)S(6)} %select_n.46), kind=kLoop, calls=%fused_computation.128 | loop fusion | bytes 3145736 | tf_op jit(solution)/shard_map/slice | solution.py:811
  115.5 2.4 multiply_convert_fusion.6
  123.2 2.3 fusion.66
  125.5 2.3 fusion.57
  128.8 3.4 fusion.9
  138.3 26.5 %shard_map.247 = bf16[512,1536]{1,0:T(8,128)(2,1)S(1)} custom-call(bf16[512,1536]{1,0:T(8,128)(2,1)S(1)} %pad_maximum_fusion.1.x), custom_call_target="tpu_custom_call" | custom-call | tf_op jit(solution)/shard_map/pallas_call | solution.py:193
  165.7 3.5 multiply_reduce_fusion
  169.2 3.8 convert_add_fusion
  173.1 81.6 %shard_map.248 = (bf16[512,768]{1,0:T(8,128)(2,1)}, f32[512,768]{1,0:T(8,128)}, bf16[3,768,512]{2,1,0:T(8,128)(2,1)}, bf16[512,768]{1,0:T(8,128)(2,1)}, bf16[3,1...) custom-call(f32[512,768]{1,0:T(8,128)} %get-tuple-element.146.refs_0_, ...), custom_call_target="tpu_custom_call" | custom-call | tf_op jit(solution)/shard_map/pallas_call | solution.py:736
  254.6 5.7 %copy.52 = bf16[3,768,512]{1,0,2:T(4,128)(2,1)} copy(bf16[3,768,512]{2,1,0:T(8,128)(2,1)} %get-tuple-element.61) | data formatting | bytes 4718592
  260.3 3.8 copy.57
  264.8 3.6 convolution_convert_fusion
  268.5 2.6 fusion.31
  274.9 2.7 fusion.74
  281.2 2.7 fusion.15
  283.8 2.5 fusion.14
  287.1 16.8 %reduce-scatter.13.cloned.1.call-done = bf16[128,2304]{1,0:T(8,128)(2,1)} async-done(((bf16[512,2304]{1,0:T(8,128)(2,1)}), bf16[128,2304]{1,0:T(8,128)(2,1)}) %reduce-scatter.13.cloned.1.call-update) | async-done | bytes 589840
  306.6 42.8 %reduce-scatter.7.cloned.1.call-done = bf16[128,768]{1,0:T(8,128)(2,1)} async-done(((bf16[512,768]{1,0:T(8,128)(2,1)}), bf16[128,768]{1,0:T(8,128)(2,1)}) %reduce-scatter.7.cloned.1.call-update) | async-done | bytes 196624 | tf_op jit(solution)/shard_map/reduce_scatter | solution.py:847
  349.4 51.0 %reduce-scatter.11.cloned.1.call-done = bf16[256,768]{1,0:T(8,128)(2,1)} async-done(((bf16[1024,768]{1,0:T(8,128)(2,1)}), bf16[256,768]{1,0:T(8,128)(2,1)}) %reduce-scatter.11.cloned.1.call-update) | async-done | bytes 393232 | tf_op jit(solution)/shard_map/reduce_scatter | solution.py:847
  400.4 47.4 %reduce-scatter.9.cloned.1.call-done = bf16[2,768,256]{2,1,0:T(8,128)(2,1)} async-done(((bf16[2,768,1024]{2,1,0:T(8,128)(2,1)}), bf16[2,768,256]{2,1,0:T(8,128)(2,1)}) %reduce-scatter.9.cloned.1.call-update) | async-done | bytes 786448 | tf_op jit(solution)/shard_map/reduce_scatter | solution.py:847
  448.5 41.0 %psum.63 = f32[3,768]{1,0:T(4,128)S(1)} all-reduce(f32[3,768]{1,0:T(4,128)S(1)} %pad_maximum_fusion.3), channel_id=1, replica_groups=mesh['branch'=4,'zz'=4,'core'=2] {'branch','zz','core'}, use_global_device_ids=true, to_apply=%region_10.11 | all-reduce | flops 2304 | bytes 18432 | tf_op jit(solution)/shard_map/psum | solution.py:841
  490.1 3.3 convert_element_type.161
  493.4 5.1 convert_element_type.143
  498.5 5.1 convert_element_type.147
  503.6 2.6 convert_bitcast_fusion
  506.3 7.6 %copy.51 = f32[768,2,1024]{2,1,0:T(2,128)} copy(f32[768,2,1024]{2,0,1:T(8,128)S(1)} %convert_bitcast_fusion) | data formatting | bytes 12582912
  513.8 17.0 %all-reduce.5.cloned.1.call-done = (bf16[768,2,256]{2,0,1:T(8,128)(2,1)}, bf16[768,3,128]{2,0,1:T(8,128)(2,1)}, bf16[128,768]{1,0:T(8,128)(2,1)}, bf16[768,3,192...) async-done(((bf16[768,2,256]{2,0,1:T(8,128)(2,1)}, bf16[768,3,128]{2,0,1:T(8,128)(2,1)}, bf16[128,768]{1,0:T(8,128)(2,1)}, ...) | async-done | bytes 3145744 | tf_op jit(solution)/shard_map/psum | solution.py:849
  530.8 2.2 convert_element_type.149
  536.0 2.0 copy.50
  (147 shorter events, 42.1 us)
Async XLA Ops:
  8.0 105.6 %copy-start = (bf16[1024,768]{1,0:T(8,128)(2,1)S(1)}, bf16[1024,768]{1,0:T(8,128)(2,1)}, u32[]{:S(2)}) copy-start(bf16[1024,768]{1,0:T(8,128)(2,1)} %param.27) | copy-start | bytes 4718596
  8.0 266.1 %all-reduce.7.cloned.1.call-start = ((), (), s32[]{:S(2)}) async-start(), calls=%async_computation.13 | async-start | bytes 4718592 | tf_op jit(solution)/shard_map/psum | solution.py:854
  99.3 1.8 copy-start.3
  103.7 6.8 %copy-start.4 = (bf16[512,768]{1,0:T(8,128)(2,1)S(1)}, bf16[512,768]{1,0:T(8,128)(2,1)}, u32[]{:S(2)}) copy-start(bf16[512,768]{1,0:T(8,128)(2,1)} %get-tuple-element.39) | copy-start | bytes 2359300
  103.7 6.8 %copy-start.6 = (bf16[512,768]{1,0:T(8,128)(2,1)S(1)}, bf16[512,768]{1,0:T(8,128)(2,1)}, u32[]{:S(2)}) copy-start(bf16[512,768]{1,0:T(8,128)(2,1)} %get-tuple-element.44) | copy-start | bytes 2359300
  103.7 6.8 %copy-start.28 = (f32[768]{0:T(1024)S(1)}, f32[768]{0:T(1024)}, u32[]{:S(2)}) copy-start(f32[768]{0:T(1024)} %param.18) | copy-start | bytes 9220
  113.6 1.9 copy-start.9
  113.6 1.9 copy-start.12
  122.7 181.2 %reduce-scatter.13.cloned.1.call-start = ((), (), s32[]{:S(2)}) async-start(), calls=%async_computation.11 | async-start | bytes 2949120
  123.2 2.3 copy-start.32
  125.5 2.3 copy-start.19
  125.5 2.4 copy-start.31
  165.7 3.6 copy-start.5
  165.7 3.6 copy-start.7
  165.7 3.6 copy-start.15
  264.1 85.2 %reduce-scatter.7.cloned.1.call-start = ((), (), s32[]{:S(2)}) async-start(), calls=%async_computation.6 | async-start | bytes 983040 | tf_op jit(solution)/shard_map/reduce_scatter | solution.py:847
  264.7 135.7 %reduce-scatter.11.cloned.1.call-start = ((), (), s32[]{:S(2)}) async-start(), calls=%async_computation.8 | async-start | bytes 1966080 | tf_op jit(solution)/shard_map/reduce_scatter | solution.py:847
  268.4 179.4 %reduce-scatter.9.cloned.1.call-start = ((), (), s32[]{:S(2)}) async-start(), calls=%async_computation.7 | async-start | bytes 3932160 | tf_op jit(solution)/shard_map/reduce_scatter | solution.py:847
  268.5 2.6 copy-start.20
  268.5 2.6 copy-start.35
  274.1 216.0 %all-gather.11.cloned.1.call-start = ((), (), s32[]{:S(2)}) async-start(), calls=%async_computation.10 | async-start | bytes 2359296 | tf_op jit(solution)/shard_map/all_gather | solution.py:856
  274.9 218.6 %all-gather.5.cloned.1.call-start = ((), (), s32[]{:S(2)}) async-start(), calls=%async_computation.4 | async-start | bytes 3932160 | tf_op jit(solution)/shard_map/all_gather | solution.py:822
  279.4 219.1 %all-gather.7.cloned.1.call-start = ((), (), s32[]{:S(2)}) async-start(), calls=%async_computation.5 | async-start | bytes 3932160 | tf_op jit(solution)/shard_map/all_gather | solution.py:839
  281.2 2.7 copy-start.2
  286.4 217.2 %all-gather.9.cloned.1.call-start = ((), (), s32[]{:S(2)}) async-start(), calls=%async_computation.9 | async-start | bytes 4718592 | tf_op jit(solution)/shard_map/all_gather | solution.py:853
  287.0 243.8 %all-reduce.5.cloned.1.call-start = ((), (), s32[]{:S(2)}) async-start(), calls=%async_computation.12 | async-start | bytes 6291456 | tf_op jit(solution)/shard_map/psum | solution.py:849
  530.8 2.3 copy-start.27
  530.8 3.0 copy-start.18
  533.0 2.1 copy-start.26
  533.8 2.2 copy-start.21
  535.2 2.8 copy-start.25
  536.0 2.9 copy-start.1
  (17 other events, 22.4 us)
Sparse Core Ops, SparseCore 0:
  122.8 112.9 all-reduce.6
  276.5 12.4 all-gather.10
  291.4 45.5 all-gather.4
  339.3 45.0 all-gather.6
  385.8 12.9 all-gather.8
Sparse Core Ops, SparseCore 1:
  264.2 39.6 reduce-scatter.12
  306.7 42.7 reduce-scatter.6
  352.8 47.5 reduce-scatter.10
  404.0 43.8 reduce-scatter.8
  451.2 79.5 all-reduce.4

commit v4 on v3

--- a/solution.py
+++ b/solution.py
@@ -462,10 +462,452 @@
     return dict(zip(FRONT_OUT, got))
 
 
-BACK_OUT = ("gf_r", "gf_l", "d_lh", "d_lm", "d_rh", "d_rm", "router")
+MID_IN = (
+    "tok_own", "cot_own", "ids", "gain", "tok_r", "cot_r", "gate", "mixed", "attn_l",
+    "le", "lr", "re", "rr",
+)
+MID_OUT = ("layer", "gm_own", "gm_r", "gate_feed", "gain_part", "g_feed", "g_rx")
+
+
+def lane_blocks(x):
+    return [x[:, n * 128 : (n + 1) * 128] for n in range(x.shape[1] // 128)]
+
+
+def pack_rows(g, start, parts):
+    for part in parts:
+        size = part.shape[0] // 2
+        for core in range(2):
+            g[core, pl.ds(start, size)] = part[core * size : (core + 1) * size].astype(BF16)
+        start += size
+    return start
+
+
+def down_pieces(rows, D):
+    steps = 8
+    per, step = D // steps // 32, rows // steps
+    pieces = []
+    for n in range(steps):
+        spots = [(r, k) for k in range(D // 128) for r in range(0, step, 32)]
+        pieces += [(p // per, n * (D // steps) + p % per * 32, n * step + r, k) for p, (r, k) in enumerate(spots)]
+    return pieces
+
+
+def pack_down(g, start, x):
+    for block, at, row, k in down_pieces(*x.shape):
+        g[start + block, pl.ds(at, 32)] = x[row : row + 32, k * 128 : (k + 1) * 128].astype(BF16)
+
+
+def mid_kernel(nb, pool, *refs):
+    i = dict(zip(MID_IN, refs[: len(MID_IN)]))
+    out = dict(zip(MID_OUT, refs[len(MID_IN) : len(MID_IN) + len(MID_OUT)]))
+    m = pool.bind(refs[len(MID_IN) + len(MID_OUT) :])
+    b, z, c = here()
+    greet([(b, z, 1 - c)] + [(j, z, c) for j in others(b, nb)])
+    own, D = i["tok_own"].shape
+    cap = i["ids"].shape[0]
+    fl = i["le"].shape[2] // nb
+    fh = i["re"].shape[2]
+    gain = i["gain"][...]
+
+    pick, pick_t = m["pick"], m["pick_t"]
+    hot = hot_rows(i["ids"][...] - b * own, own)
+    pick[...] = hot
+    pick_t[...] = hot.T
+    owned = jnp.sum(pick_t[...].astype(F32), axis=1, keepdims=True) > 0.5
+    mid_o, mid_r = m["mid_o"], m["mid_r"]
+    mid_o[...] = i["tok_own"][...].astype(F32) + jnp.where(
+        owned, mm(pick_t[...], i["mixed"][...], 1, 0), i["attn_l"][...]
+    )
+    mid_r[...] = i["tok_r"][...].astype(F32) + i["mixed"][...].astype(F32)
+    n_o, n_r = m["n_o"], m["n_r"]
+    n_o[...] = normed(mid_o[...], gain)
+    n_r[...] = normed(mid_r[...], gain)
+    gate = i["gate"][...]
+    seed_r = m["seed_r"]
+    seed_r[...] = (gate * i["cot_r"][...].astype(F32)).astype(BF16)
+
+    def both_ways(n, seed, expand, narrow, row0, tile, count, hid, du, dv, ff, dn):
+        def one(t, carry):
+            lanes = band(t * tile, tile)
+            wd = narrow[band(row0 + t * tile, tile)]
+            u = mm(n[...], expand[0, :, lanes], 1, 0)
+            v = mm(n[...], expand[1, :, lanes], 1, 0)
+            g, dg = gelu_parts(u)
+            low = (g * v).astype(BF16)
+            hid[:, lanes] = low
+            dh = mm(seed[...], wd, 1, 1)
+            du[:, lanes] = (dh * v * dg).astype(BF16)
+            dv[:, lanes] = (dh * g).astype(BF16)
+            one_ff = mm(low, wd, 1, 0)
+            one_dn = mm(du[:, lanes], expand[0, :, lanes], 1, 1) + mm(dv[:, lanes], expand[1, :, lanes], 1, 1)
+            ff[...] = jnp.where(t == 0, one_ff, ff[...] + one_ff)
+            dn[...] = jnp.where(t == 0, one_dn, dn[...] + one_dn)
+            return carry
+
+        lax.fori_loop(0, count, one, 0)
+
+    ff_r, dn_r, ff_o, dn_o = m["ff_r"], m["dn_r"], m["ff_o"], m["dn_o"]
+    both_ways(
+        n_r, seed_r, i["re"], i["rr"], c * fh, fl, fh // fl, m["hid_r"], m["du_r"], m["dv_r"], ff_r, dn_r
+    )
+    both_ways(
+        n_o, i["cot_own"], i["le"], i["lr"], 0, fl, nb, m["hid_o"], m["du_o"], m["dv_o"], ff_o, dn_o
+    )
+    out["gate_feed"][...] = jnp.sum(i["cot_r"][...].astype(F32) * ff_r[...], axis=-1, keepdims=True)
+    part = m["part"]
+    part[:, :D] = ff_r[...].astype(BF16)
+    part[:, D:] = (dn_r[...] + mm(pick[...], dn_o[...].astype(BF16), 1, 0)).astype(BF16)
+
+    n_t = m["n_t"]
+
+    def weights_heavy():
+        n_t[...] = n_r[...].T
+        gx = out["g_rx"]
+        for k, x in enumerate(lane_blocks(mm(n_t[...], m["du_r"][...], 1, 0)) + lane_blocks(mm(n_t[...], m["dv_r"][...], 1, 0))):
+            gx[k] = x.astype(BF16)
+        pack_down(gx, 2 * fh // 128, mm(m["hid_r"][...], seed_r[...], 0, 0))
+
+    def weights_light():
+        n_t[...] = n_o[...].T
+        g = out["g_feed"]
+
+        def one(t, carry):
+            lanes = band(t * fl, fl)
+            gate_part = mm(n_t[...], m["du_o"][:, lanes], 1, 0)
+            up_part = mm(n_t[...], m["dv_o"][:, lanes], 1, 0)
+            down = mm(m["hid_o"][:, lanes], i["cot_own"][...], 0, 0)
+            pack_rows(g.at[t], 0, lane_blocks(gate_part) + lane_blocks(up_part) + lane_blocks(down))
+            return carry
+
+        lax.fori_loop(0, nb, one, 0)
+
+    sums = m["sums"]
+    group_sum_steps(nb, part, sums, m, [weights_heavy, weights_light])
+    dn_sum = sums[:, D:]
+    scaled = (gate * sums[:, :D].astype(F32)).astype(BF16)
+    out["layer"][...] = (mid_o[...] + ff_o[...] + mm(pick_t[...], scaled, 1, 0)).astype(BF16)
+    dn_own = jnp.where(owned, mm(pick_t[...], dn_sum, 1, 0), dn_o[...])
+    r, xh = norm_parts(mid_o[...])
+    out["gm_own"][...] = i["cot_own"][...].astype(F32) + norm_back(dn_own, xh, r, gain)
+    out["gain_part"][...] = jnp.sum(dn_own * xh, axis=0, keepdims=True)
+    r, xh = norm_parts(mid_r[...])
+    out["gm_r"][...] = i["cot_r"][...].astype(F32) + norm_back(dn_sum.astype(F32), xh, r, gain)
+
+
+def middle(nb, given):
+    own, D = given["tok_own"].shape
+    cap = given["ids"].shape[0]
+    wide = given["le"].shape[2]
+    fl = wide // nb
+    fh = given["re"].shape[2]
+    shape = lambda *dims: jax.ShapeDtypeStruct(dims, BF16)
+    shape32 = lambda *dims: jax.ShapeDtypeStruct(dims, F32)
+    packed = (2 * D * fl + fl * D) // 2 // 128
+    outs = dict(
+        layer=shape(own, D), gm_own=shape32(own, D), gm_r=shape32(cap, D), gate_feed=shape32(cap, 1),
+        gain_part=shape32(1, D), g_feed=shape(nb, 2, packed, 128), g_rx=shape(3 * fh // 128, D, 128),
+    )
+    pool = Pool()
+    pool.vmem("pick", (cap, own))
+    pool.vmem("pick_t", (own, cap))
+    for name, count in (("o", own), ("r", cap)):
+        pool.vmem(f"mid_{name}", (count, D), F32)
+        pool.vmem(f"n_{name}", (count, D))
+        pool.vmem(f"ff_{name}", (count, D), F32)
+        pool.vmem(f"dn_{name}", (count, D), F32)
+        for kind in ("hid", "du", "dv"):
+            pool.vmem(f"{kind}_{name}", (count, wide if name == "o" else fh))
+    pool.vmem("seed_r", (cap, D))
+    pool.vmem("n_t", (D, own))
+    pool.vmem("part", (cap, 2 * D))
+    pool.vmem("sums", (cap, 2 * D))
+    group_sum_scratch(pool, nb, cap, 2 * D)
+    got = pl.pallas_call(
+        functools.partial(mid_kernel, nb, pool),
+        out_shape=tuple(outs[name] for name in MID_OUT),
+        in_specs=[VM] * len(MID_IN),
+        out_specs=(VM,) * len(MID_OUT),
+        scratch_shapes=pool.shapes,
+        compiler_params=pltpu.CompilerParams(
+            collective_id=2, has_side_effects=True, vmem_limit_bytes=60 << 20
+        ),
+    )(*(given[name] for name in MID_IN))
+    return dict(zip(MID_OUT, got))
+
+
+class Gather:
+    def __init__(self, nb, src, dst, m, name):
+        b, z, c = here()
+        self.own = pltpu.make_async_copy(src, dst.at[b], m[f"{name}_own"])
+        self.out = [
+            remote(src, dst.at[b], m[f"{name}_s"].at[j], m[f"{name}_r"].at[b], (j, z, c)) for j in others(b, nb)
+        ]
+        self.come = [
+            remote(dst.at[j], dst.at[j], m[f"{name}_s"].at[j], m[f"{name}_r"].at[j], (j, z, c))
+            for j in others(b, nb)
+        ]
+
+    def start(self):
+        self.own.start()
+        for copy in self.out:
+            copy.start()
+
+    def wait(self):
+        for copy in self.come:
+            copy.wait_recv()
+        for copy in self.out:
+            copy.wait_send()
+        self.own.wait()
+
+    @staticmethod
+    def scratch(pool, nb, name):
+        pool.shapes.append(pltpu.SemaphoreType.DMA)
+        pool.names.append(f"{name}_own")
+        pool.dma(f"{name}_s", nb)
+        pool.dma(f"{name}_r", nb)
+
+
+class ShardSum:
+    def __init__(self, nb, g, h, m, name):
+        self.b, self.z, self.c = here()
+        self.peers = others(self.b, nb)
+        self.g, self.h, self.m, self.name = g, h, m, name
+        self.sends = []
+
+    def pair(self, j):
+        m, n = self.m, self.name
+        return remote(
+            self.g.at[j, 1 - self.c], m[f"{n}_sib"].at[j], m[f"{n}_a_s"].at[j], m[f"{n}_a_r"].at[j],
+            (self.b, self.z, 1 - self.c),
+        )
+
+    def start(self):
+        for j in self.peers + [self.b]:
+            copy = self.pair(j)
+            copy.start()
+            self.sends.append(copy)
+
+    def spread(self):
+        m, n = self.m, self.name
+        for j in self.peers:
+            self.pair(j).wait_recv()
+            sib = m[f"{n}_sib"]
+            sib[j] = (self.g[j, self.c].astype(F32) + sib[j].astype(F32)).astype(BF16)
+            copy = remote(
+                sib.at[j], m[f"{n}_came"].at[self.b], m[f"{n}_b_s"].at[j], m[f"{n}_b_r"].at[self.b],
+                (j, self.z, self.c),
+            )
+            copy.start()
+            self.sends.append(copy)
+
+    def collect(self):
+        m, n = self.m, self.name
+        sib, came, b = m[f"{n}_sib"], m[f"{n}_came"], self.b
+        self.pair(b).wait_recv()
+        total = self.g[b, self.c].astype(F32) + sib[b].astype(F32)
+        for j in self.peers:
+            remote(sib.at[j], came.at[j], m[f"{n}_b_s"].at[j], m[f"{n}_b_r"].at[j], (j, self.z, self.c)).wait_recv()
+            total = total + came[j].astype(F32)
+        self.h[...] = total.astype(BF16)
+
+    def end(self):
+        finish(self.sends)
+
+    @staticmethod
+    def scratch(pool, nb, rows, name):
+        pool.vmem(f"{name}_sib", (nb, rows, 128))
+        pool.vmem(f"{name}_came", (nb, rows, 128))
+        for step in ("a", "b"):
+            pool.dma(f"{name}_{step}_s", nb)
+            pool.dma(f"{name}_{step}_r", nb)
+
+
+class BlockSum:
+    def __init__(self, nz, h, f, m, name):
+        self.b, self.z, self.c = here()
+        self.peers = others(self.z, nz)
+        self.h, self.f, self.m, self.name = h, f, m, name
+        self.ch = h.shape[0] // nz
+        self.sends = []
+
+    def go(self, copy):
+        copy.start()
+        self.sends.append(copy)
+
+    def rows(self, j):
+        return band(j * self.ch, self.ch)
+
+    def start(self):
+        m, n = self.m, self.name
+        for j in self.peers:
+            self.go(
+                remote(
+                    self.h.at[self.rows(j)], m[f"{n}_came"].at[self.z], m[f"{n}_a_s"].at[j],
+                    m[f"{n}_a_r"].at[self.z], (self.b, j, self.c),
+                )
+            )
+
+    def spread(self):
+        m, n = self.m, self.name
+        came, z, c = m[f"{n}_came"], self.z, self.c
+        total = self.h[self.rows(z)].astype(F32)
+        for j in self.peers:
+            remote(
+                self.h.at[self.rows(j)], came.at[j], m[f"{n}_a_s"].at[j], m[f"{n}_a_r"].at[j], (self.b, j, c)
+            ).wait_recv()
+            total = total + came[j].astype(F32)
+        mine = self.f.at[c, self.rows(z)]
+        mine[...] = total.astype(BF16)
+        for j in self.peers:
+            self.go(remote(mine, mine, m[f"{n}_b_s"].at[j], m[f"{n}_b_r"].at[z], (self.b, j, c)))
+        self.go(remote(mine, mine, m[f"{n}_c_s"].at[z], m[f"{n}_c_r"].at[z], (self.b, z, 1 - c)))
+
+    def forward(self):
+        m, n, c = self.m, self.name, self.c
+        for j in self.peers:
+            piece = self.f.at[c, self.rows(j)]
+            remote(piece, piece, m[f"{n}_b_s"].at[j], m[f"{n}_b_r"].at[j], (self.b, j, c)).wait_recv()
+            self.go(remote(piece, piece, m[f"{n}_c_s"].at[j], m[f"{n}_c_r"].at[j], (self.b, self.z, 1 - c)))
+
+    def end(self):
+        m, n, c = self.m, self.name, self.c
+        for j in self.peers + [self.z]:
+            piece = self.f.at[1 - c, self.rows(j)]
+            remote(piece, piece, m[f"{n}_c_s"].at[j], m[f"{n}_c_r"].at[j], (self.b, self.z, 1 - c)).wait_recv()
+        finish(self.sends)
+
+    @staticmethod
+    def scratch(pool, nz, rows, name):
+        pool.vmem(f"{name}_came", (nz, rows // nz, 128))
+        for step in ("a", "b", "c"):
+            pool.dma(f"{name}_{step}_s", nz)
+            pool.dma(f"{name}_{step}_r", nz)
+
+
+TAIL_IN = ("g_att", "g_heavy", "gm_own", "gf_l", "gf_r", "ids", "tok_own", "gain", "vec")
+TAIL_OUT = ("delta", "f_att", "f_heavy", "vectors")
+
+
+def tail_kernel(nb, nz, pool, *refs):
+    i = dict(zip(TAIL_IN, refs[: len(TAIL_IN)]))
+    out = dict(zip(TAIL_OUT, refs[len(TAIL_IN) : len(TAIL_IN) + len(TAIL_OUT)]))
+    m = pool.bind(refs[len(TAIL_IN) + len(TAIL_OUT) :])
+    b, z, c = here()
+    twin = (b, z, 1 - c)
+    bpeers, zpeers = others(b, nb), others(z, nz)
+    own, D = i["gm_own"].shape
+    greet([twin] + [(j, z, c) for j in bpeers] + [(b, j, c) for j in zpeers])
+    gh, sib_h, h_heavy = i["g_heavy"], m["sib_h"], m["h_heavy"]
+    to_twin = remote(gh.at[1 - c], sib_h, m["sib_h_s"].at[0], m["sib_h_r"].at[0], twin)
+    to_twin.start()
+    shard = ShardSum(nb, i["g_att"], m["h_att"], m, "ga")
+    shard.start()
+    att = BlockSum(nz, m["h_att"], out["f_att"], m, "za")
+    heavy = BlockSum(nz, h_heavy, out["f_heavy"], m, "zh")
+    to_twin.wait_recv()
+    h_heavy[...] = (gh[c].astype(F32) + sib_h[...].astype(F32)).astype(BF16)
+    heavy.start()
+    shard.spread()
+
+    hot_t = hot_rows(i["ids"][...] - b * own, own).T
+    owned = jnp.sum(hot_t.astype(F32), axis=1, keepdims=True) > 0.5
+    gf = jnp.where(owned, mm(hot_t, i["gf_r"][...], 1, 0), i["gf_l"][...])
+    r, xh = norm_parts(i["tok_own"][...].astype(F32))
+    gain_part = jnp.sum(gf * xh, axis=0, keepdims=True)
+    low = m["low"]
+    low[...] = (i["gm_own"][...] + norm_back(gf, xh, r, i["gain"][...])).astype(BF16)
+    rows = Gather(nb, low, out["delta"], m, "td")
+    rows.start()
+
+    vec = m["vec_mine"]
+    vec[pl.ds(0, 8)] = i["vec"][...]
+    vec[pl.ds(0, 1)] = gain_part
+    sends = [to_twin]
+
+    def vec_step(name, me, peers, device):
+        got = m[f"{name}_got"]
+        got[me] = vec[...]
+        for j in peers:
+            copy = remote(vec, got.at[me], m[f"{name}_s"].at[j], m[f"{name}_r"].at[me], device(j))
+            copy.start()
+            sends.append(copy)
+
+    def vec_end(name, peers, device):
+        got = m[f"{name}_got"]
+        for j in peers:
+            remote(got.at[j], got.at[j], m[f"{name}_s"].at[j], m[f"{name}_r"].at[j], device(j)).wait_recv()
+        return functools.reduce(lambda x, y: x + y, [got[j] for j in range(got.shape[0])])
+
+    by_core, by_branch, by_block = (lambda j: (b, z, j)), (lambda j: (j, z, c)), (lambda j: (b, j, c))
+    vec_step("vc", c, [1 - c], by_core)
+    shard.collect()
+    att.start()
+    total = vec_end("vc", [1 - c], by_core)
+    vec2 = m["vec_pair"]
+    vec2[...] = total
+    vec = vec2
+    vec_step("vb", b, bpeers, by_branch)
+    heavy.spread()
+    total = vec_end("vb", bpeers, by_branch)
+    vec3 = m["vec_group"]
+    vec3[...] = total
+    vec = vec3
+    vec_step("vz", z, zpeers, by_block)
+    att.spread()
+    heavy.forward()
+    out["vectors"][...] = vec_end("vz", zpeers, by_block)
+    att.forward()
+    heavy.end()
+    att.end()
+    shard.end()
+    rows.wait()
+    finish(sends)
+
+
+def tail(nb, nz, given):
+    own, D = given["gm_own"].shape
+    ra, rh = given["g_att"].shape[2], given["g_heavy"].shape[1]
+    shape = lambda *dims: jax.ShapeDtypeStruct(dims, BF16)
+    outs = dict(
+        delta=shape(nb, own, D), f_att=shape(2, ra, 128), f_heavy=shape(2, rh, 128),
+        vectors=jax.ShapeDtypeStruct((8, D), F32),
+    )
+    pool = Pool()
+    pool.vmem("sib_h", (rh, 128))
+    pool.vmem("h_heavy", (rh, 128))
+    pool.vmem("h_att", (ra, 128))
+    pool.vmem("low", (own, D))
+    pool.dma("sib_h_s", 1)
+    pool.dma("sib_h_r", 1)
+    ShardSum.scratch(pool, nb, ra, "ga")
+    BlockSum.scratch(pool, nz, ra, "za")
+    BlockSum.scratch(pool, nz, rh, "zh")
+    Gather.scratch(pool, nb, "td")
+    for name in ("vec_mine", "vec_pair", "vec_group"):
+        pool.vmem(name, (8, D), F32)
+    for name, count in (("vc", 2), ("vb", nb), ("vz", nz)):
+        pool.vmem(f"{name}_got", (count, 8, D), F32)
+        pool.dma(f"{name}_s", count)
+        pool.dma(f"{name}_r", count)
+    got = pl.pallas_call(
+        functools.partial(tail_kernel, nb, nz, pool),
+        out_shape=tuple(outs[name] for name in TAIL_OUT),
+        in_specs=[VM] * len(TAIL_IN),
+        out_specs=(HB,) + (VM,) * (len(TAIL_OUT) - 1),
+        scratch_shapes=pool.shapes,
+        compiler_params=pltpu.CompilerParams(
+            collective_id=4, has_side_effects=True, vmem_limit_bytes=56 << 20
+        ),
+        cost_estimate=pl.CostEstimate(flops=40 * 10**9, bytes_accessed=200 * 2**20, transcendentals=0),
+    )(*(given[name] for name in TAIL_IN))
+    return dict(zip(TAIL_OUT, got))
+
+
+BACK_OUT = ("gf_r", "gf_l", "g_att", "g_heavy", "router", "lay", "f_feed")
 BACK_IN = (
     "gm_own", "gm_r", "gate", "gate_feed", "ids", "q", "k", "v", "lm", "lh", "first_w", "ctx_l",
     "qr", "kv", "rmerge", "rheads", "first_r", "ctx_r", "attn_r", "router_vector",
+    "layer", "g_feed",
 )
 
 
@@ -553,6 +995,11 @@
     greet([twin, after, before] + [(j, z, c) for j in bpeers] + [(b, j, c) for j in zpeers])
     mine_at, other_at = band(c * half, half), band((1 - c) * half, half)
     sends = []
+    layer = Gather(nb, i["layer"], out["lay"], m, "ly")
+    shard = ShardSum(nb, i["g_feed"], m["h_feed"], m, "gf")
+    feeds = BlockSum(nz, m["h_feed"], out["f_feed"], m, "zf")
+    shard.start()
+    layer.start()
 
     def go(copy):
         copy.start()
@@ -561,7 +1008,7 @@
     gm_half = i["gm_r"][mine_at]
     gate_half = i["gate"][mine_at]
     seed = (gate_half * gm_half).astype(BF16)
-    out["d_rm"][...] = mm(i["ctx_r"][...], seed, 0, 0).astype(BF16)
+    pack_rows(out["g_heavy"], 3 * rw // 2 * (D // 128), lane_blocks(mm(i["ctx_r"][...], seed, 0, 0)))
     trio = m["trio"] if inner else i["trio"]
 
     def spot(core, j):
@@ -576,6 +1023,7 @@
         for j in zpeers + [z]:
             go(to_twin(j))
 
+    shard.spread()
     low, do_l = m["low"], m["do_l"]
     low[...] = i["gm_own"][...].astype(BF16)
     do_l[...] = mm(low[...], i["lm"][...], 1, 1).astype(BF16)
@@ -620,6 +1068,8 @@
         return carry
 
     lax.fori_loop(0, blocks * (wl // (2 * DH)), light, 0)
+    shard.collect()
+    feeds.start()
     rim, came_rim = m["rim"], m["came_rim"]
     for n, start in ((0, WIN + own), (1, 0)):
         rim[n, :, :wl] = (dkl[pl.ds(start, WIN)] * SCALE).astype(BF16)
@@ -652,6 +1102,7 @@
     gf_l = out["gf_l"]
     gf_l[...] = mm(dql[...], lh[0], 1, 1) + mm(dk_own[...], lh[1], 1, 1) + mm(dv_own[...], lh[2], 1, 1)
 
+    feeds.spread()
     gate, first_r = i["gate"], i["first_r"]
     gate_attn = jnp.sum(gm_half * i["attn_r"][...], axis=-1, keepdims=True)
     total_part = m["part"]
@@ -669,20 +1120,39 @@
         total_part[at] = sum_.astype(BF16)
     out["router"][...] = router_sum
 
+    first_t, g_att = m["first_t"], out["g_att"]
+    hl = wl // nb
+
     def weights_light():
-        first_t = m["first_t"]
         first_t[...] = i["first_w"][pl.ds(WIN, own)].T
-        out["d_lh"][0] = mm(first_t[...], dql[...], 1, 0).astype(BF16)
-        out["d_lh"][1] = mm(first_t[...], dk_own[...], 1, 0).astype(BF16)
+
+        def one(t, carry):
+            lanes = band(t * 2 * hl, 2 * hl)
+            for n, x in enumerate((dql, dk_own, dv_own)):
+                both = mm(first_t[...], x[:, lanes], 1, 0)
+                for k in range(2):
+                    pack_rows(g_att.at[2 * t + k], n * D // 2, [both[:, k * hl : (k + 1) * hl]])
+            return carry
+
+        lax.fori_loop(0, nb // 2, one, 0)
 
     def weights_rest():
-        out["d_lh"][2] = mm(m["first_t"][...], dv_own[...], 1, 0).astype(BF16)
-        out["d_lm"][...] = mm(i["ctx_l"][...], low[...], 0, 0).astype(BF16)
+        def one(t, carry):
+            both = mm(i["ctx_l"][:, band(t * 2 * hl, 2 * hl)], low[...], 0, 0)
+            for k in range(2):
+                pack_rows(g_att.at[2 * t + k], 3 * D // 2, lane_blocks(both[k * hl : (k + 1) * hl]))
+            return carry
+
+        lax.fori_loop(0, nb // 2, one, 0)
         first_half = first_r[mine_at]
         for n in range(3):
-            out["d_rh"][n] = mm(trio[n], first_half, 0, 0).astype(BF16)
+            pack_rows(out["g_heavy"], n * rw // 2 * (D // 128), lane_blocks(mm(trio[n], first_half, 0, 0)))
+        feeds.forward()
 
     group_sum_steps(nb, total_part, out["gf_r"], m, [weights_light, weights_rest])
+    feeds.end()
+    shard.end()
+    layer.wait()
     finish(sends)
 
 
@@ -693,11 +1163,13 @@
     rw = given["rmerge"].shape[0]
     wl = given["q"].shape[1]
     deep = 2 * nz * half
+    feed_rows = given["g_feed"].shape[2]
     shape = lambda *dims: jax.ShapeDtypeStruct(dims, BF16)
     outs = dict(
-        gf_r=shape(cap, D), gf_l=jax.ShapeDtypeStruct((own, D), F32), d_lh=shape(3, D, wl),
-        d_lm=shape(wl, D), d_rh=shape(3, rw, D), d_rm=shape(rw, D),
+        gf_r=shape(cap, D), gf_l=jax.ShapeDtypeStruct((own, D), F32),
+        g_att=shape(nb, 2, 2 * D * wl // nb // 128, 128), g_heavy=shape(2, 2 * D * rw // 128, 128),
         router=jax.ShapeDtypeStruct((1, D), F32),
+        lay=shape(nb, own, D), f_feed=shape(2, feed_rows, 128),
     )
     pool = Pool()
     inner = deep <= 4096
@@ -731,19 +1203,118 @@
         pool.dma(f"{name}_r", nz)
     if not inner:
         given = dict(given, trio=heavy_back_plain(given))
+    pool.vmem("h_feed", (feed_rows, 128))
+    ShardSum.scratch(pool, nb, feed_rows, "gf")
+    BlockSum.scratch(pool, nz, feed_rows, "zf")
+    Gather.scratch(pool, nb, "ly")
     pool.dma("rim_s", 2)
     pool.dma("rim_r", 2)
     got = pl.pallas_call(
         functools.partial(back_kernel, nb, nz, pool, inner),
         out_shape=tuple(outs[name] for name in BACK_OUT),
         in_specs=[VM] * len(back_names(inner)),
-        out_specs=(VM,) * len(BACK_OUT),
+        out_specs=tuple(HB if name == "lay" else VM for name in BACK_OUT),
         scratch_shapes=pool.shapes,
         compiler_params=pltpu.CompilerParams(
-            collective_id=3, has_side_effects=True, vmem_limit_bytes=60 << 20
+            collective_id=3, has_side_effects=True, vmem_limit_bytes=62 << 20
         ),
+        cost_estimate=pl.CostEstimate(flops=80 * 10**9, bytes_accessed=200 * 2**20, transcendentals=0),
     )(*(given[name] for name in back_names(inner)))
     return dict(zip(BACK_OUT, got))
+
+
+FIN_OUT = ("layer", "delta", "re", "rr", "lh", "lm", "rh", "rm", "le", "lr")
+
+
+def finish_kernel(lay, dlt, rx, att, heavy, feed_in, *outs):
+    o = dict(zip(FIN_OUT, outs))
+    o["layer"][...] = lay[...].astype(F32)
+    o["delta"][...] = dlt[...].astype(F32)
+    size = rx.shape[2]
+    blocks = rx.shape[1] // 3
+    for core in range(2):
+        for part in range(2):
+            for k in range(blocks):
+                at = 2 * (core * blocks + k) + part
+                o["re"][pl.ds(at, size, 4 * blocks), :] = rx[core, part * blocks + k].astype(F32)
+        for block, at, row, k in down_pieces(blocks * 128, size * 8):
+            if row < blocks * 16:
+                o["rr"][core, pl.ds(row, 32), k * 128 : (k + 1) * 128] = rx[core, 2 * blocks + block, pl.ds(at, 32)].astype(F32)
+
+    @pl.when(pl.program_id(0) == 0)
+    def _():
+        for core in range(2):
+            D, hl = o["lh"].shape[1:]
+            start = 0
+            for n in range(3):
+                size = D // 2
+                o["lh"][n, pl.ds(core * size, size)] = att[core, pl.ds(start, size)].astype(F32)
+                start += size
+            for k in range(D // 128):
+                size = hl // 2
+                o["lm"][pl.ds(core * size, size), k * 128 : (k + 1) * 128] = att[core, pl.ds(start, size)].astype(F32)
+                start += size
+            start = 0
+            size = o["rm"].shape[0] // 2
+            for n in range(4):
+                dst = o["rm"] if n == 3 else o["rh"].at[n]
+                for k in range(D // 128):
+                    dst[pl.ds(core * size, size), k * 128 : (k + 1) * 128] = heavy[core, pl.ds(start, size)].astype(F32)
+                    start += size
+            start = 0
+            fl = o["lr"].shape[0]
+            lanes = fl // 128
+            size = D // 2
+            for part in range(2):
+                for k in range(lanes):
+                    o["le"][pl.ds(core * size * 2 * lanes + 2 * k + part, size, 2 * lanes), :] = feed_in[
+                        core, pl.ds(start, size)
+                    ].astype(F32)
+                    start += size
+            size = fl // 2
+            for k in range(D // 128):
+                o["lr"][pl.ds(core * size, size), k * 128 : (k + 1) * 128] = feed_in[core, pl.ds(start, size)].astype(F32)
+                start += size
+
+
+def finish_all(lay, dlt, rx, att, heavy, feed_in, hl, fl, rw):
+    steps = 8
+    rows, D = lay.shape
+    fh = rx.shape[1] // 3 * 128
+    shape = lambda *dims: jax.ShapeDtypeStruct(dims, F32)
+    whole = lambda *dims: pl.BlockSpec(dims, lambda n: (0,) * len(dims))
+    tall = lambda count, width: pl.BlockSpec((count // steps, width), lambda n: (n, 0))
+    return dict(
+        zip(
+            FIN_OUT,
+            pl.pallas_call(
+                finish_kernel,
+                grid=(steps,),
+                out_shape=(
+                    shape(rows, D), shape(rows, D), shape(D * 4 * fh // 128, 128), shape(2, fh, D),
+                    shape(3, D, hl), shape(hl, D), shape(3, rw, D), shape(rw, D),
+                    shape(D * 2 * fl // 128, 128), shape(fl, D),
+                ),
+                in_specs=[
+                    tall(rows, D), tall(rows, D),
+                    pl.BlockSpec((2, 3 * fh // 128, D // steps, 128), lambda n: (0, 0, n, 0)),
+                    whole(*att.shape), whole(*heavy.shape), whole(*feed_in.shape),
+                ],
+                out_specs=(
+                    tall(rows, D), tall(rows, D), tall(D * 4 * fh // 128, 128),
+                    pl.BlockSpec((2, fh // steps, D), lambda n: (0, n, 0)),
+                    whole(3, D, hl), whole(hl, D), whole(3, rw, D), whole(rw, D),
+                    whole(D * 2 * fl // 128, 128), whole(fl, D),
+                ),
+                compiler_params=pltpu.CompilerParams(vmem_limit_bytes=50 << 20),
+            )(lay, dlt, rx, att, heavy, feed_in),
+        )
+    )
+
+
+def woven(x, width):
+    blocks = width // 128
+    return x.reshape(-1, blocks, 2, 128).transpose(0, 2, 1, 3).reshape(-1, 2, width)
 
 
 def per_device(
@@ -782,94 +1353,47 @@
     twice = jnp.concatenate([routed_slots, routed_slots])
     rolled = lax.dynamic_slice(twice, (jnp.mod(cap - offset, cap),), (cap,))
     ids = jnp.where(live, rolled, -1)[:, None]
-    pick_own = (ids - b * own == jnp.arange(own, dtype=jnp.int32)[None, :]).astype(BF16)
-    mask_own = (jnp.sum(pick_own.astype(F32), 0) > 0.5)[:, None]
-
     rheads = routed_heads.transpose(1, 2, 0)
     f = front(
         nb, nz, tokens, cotangent, ids, gain_before[None], router_vector[None], rheads, routed_merge,
         local_heads.transpose(1, 0, 2), local_merge, local_expand.transpose(1, 0, 2), local_reduce,
     )
-    gate, mixed_r, local_attn = f["gate"], f["mixed"], f["attn_l"]
-    tok_r, cot_r = f["tok_r"].astype(F32), f["cot_r"].astype(F32)
-    tok_own = lax.dynamic_slice(tokens, (b * own, 0), (own, D)).astype(F32)
+    tok_own = lax.dynamic_slice(tokens, (b * own, 0), (own, D))
     cot_own = lax.dynamic_slice(cotangent, (b * own, 0), (own, D))
-    r1, xh1 = norm_parts(tok_own)
-
-    mixed_own = jnp.where(mask_own, mm(pick_own, mixed_r, 0, 0), local_attn)
-    middle_own = tok_own + mixed_own
-    middle_r = tok_r + mixed_r.astype(F32)
-    r2, xh2 = norm_parts(middle_own)
-    second_own = (xh2 * gain_middle).astype(BF16)
-    r2r, xh2r = norm_parts(middle_r)
-    second_r = (xh2r * gain_middle).astype(BF16)
-
-    ff_l, dn_l, d_lg, d_lu, d_ld = feed(second_own, cot_own, f["le"][0], f["le"][1], f["lr"])
-    re_half = lax.dynamic_slice(routed_expand, (0, 0, core * fh), (D, 2, fh))
-    rr_half = lax.dynamic_slice(routed_reduce, (core * fh, 0), (fh, D))
-    seed_r = (gate * cot_r).astype(BF16)
-    ff_r, dn_r, d_rg, d_ru, d_rd = feed(second_r, seed_r, re_half[:, 0], re_half[:, 1], rr_half)
-    gate_feed = jnp.sum(cot_r * ff_r, -1, keepdims=True)
-
-    both = jnp.concatenate(
-        [ff_r.astype(BF16), (dn_r + mm(pick_own, dn_l.astype(BF16), 1, 0)).astype(BF16)], 1
-    )
-    both = group_sum(both, nb, 2)
-    ffr_sum, dn2_r = both[:, :D].astype(F32), both[:, D:]
-    layer_own = (
-        middle_own + ff_l + mm(pick_own, (gate * ffr_sum).astype(BF16), 0, 0)
-    ).astype(BF16)
-    layer_output = lax.all_gather(layer_own, "branch", axis=0, tiled=True).astype(F32)
-
-    dn2_own = jnp.where(mask_own, mm(pick_own, dn2_r, 0, 0), dn_l)
-    gm_own = cot_own.astype(F32) + norm_back(dn2_own, xh2, r2, gain_middle)
-    gm_r = cot_r + norm_back(dn2_r.astype(F32), xh2r, r2r, gain_middle)
-    delta_gain_middle = jnp.sum(dn2_own * xh2, 0)
-
-    k = back(
-        nb, nz,
-        dict(
-            f, gm_own=gm_own, gm_r=gm_r, gate_feed=gate_feed, ids=ids, rmerge=routed_merge,
-            rheads=rheads, router_vector=router_vector[None],
-        ),
-    )
-    gf_own = jnp.where(mask_own, mm(pick_own, k["gf_r"], 0, 0), k["gf_l"])
-    td_own = (gm_own + norm_back(gf_own, xh1, r1, gain_before)).astype(BF16)
-    delta_gain_before = jnp.sum(gf_own * xh1, 0)
-    tokens_delta = lax.all_gather(td_own, "branch", axis=0, tiled=True).astype(F32)
-
-    vectors = lax.psum(
-        jnp.stack([delta_gain_before, delta_gain_middle, k["router"][0]]).astype(F32),
-        ("branch",) + DP,
-    )
-
-    def over_branch(x, dim):
-        return lax.psum_scatter(x.astype(BF16), "branch", scatter_dimension=dim, tiled=True)
-
-    g_le = lax.psum(over_branch(jnp.stack([d_lg, d_lu], 0), 2), DP)
-    g_lr = lax.psum(over_branch(d_ld, 0), DP)
-    g_lh = lax.psum(over_branch(k["d_lh"], 2), DP)
-    g_lm = lax.psum(over_branch(k["d_lm"], 0), DP)
-    g_re = lax.all_gather(
-        lax.psum(jnp.stack([d_rg, d_ru], 0).astype(BF16), "zz"), "core", axis=2, tiled=True
-    )
-    g_rr = lax.all_gather(lax.psum(d_rd.astype(BF16), "zz"), "core", axis=0, tiled=True)
-    g_rh = lax.psum(k["d_rh"], DP)
-    g_rm = lax.psum(k["d_rm"], DP)
+    re_half = lax.dynamic_slice(routed_expand, (0, 0, core * fh), (D, 2, fh)).transpose(1, 0, 2)
+    f = dict(
+        f, tok_own=tok_own, cot_own=cot_own, ids=ids, gain=gain_middle[None], re=re_half, rr=routed_reduce,
+        rmerge=routed_merge, rheads=rheads, router_vector=router_vector[None],
+    )
+    f = dict(f, **middle(nb, f))
+    rx_sum = lax.psum(f["g_rx"], "zz")
+    f = dict(f, **back(nb, nz, f))
+    rx_sum, f["gf_r"] = lax.optimization_barrier((rx_sum, f["gf_r"]))
+    vec = jnp.concatenate(
+        [jnp.zeros((1, D), F32), f["gain_part"], f["router"], jnp.zeros((5, D), F32)], 0
+    )
+    f = dict(f, gain=gain_before[None], vec=vec)
+    f = dict(f, **tail(nb, nz, f))
+    rx_sum = lax.all_gather(rx_sum, "core")
+    g = finish_all(
+        f["lay"].reshape(rows, D), f["delta"].reshape(rows, D), rx_sum,
+        f["f_att"], f["f_heavy"], f["f_feed"], hl=local_merge.shape[0], fl=local_reduce.shape[0],
+        rw=routed_merge.shape[0],
+    )
     return (
-        layer_output,
-        tokens_delta,
-        vectors[0],
-        vectors[1],
-        vectors[2],
-        g_lh.transpose(1, 0, 2).astype(F32),
-        g_lm.astype(F32),
-        g_rh.transpose(2, 0, 1).astype(F32),
-        g_rm.astype(F32),
-        g_le.transpose(1, 0, 2).astype(F32),
-        g_lr.astype(F32),
-        g_re.transpose(1, 0, 2).astype(F32),
-        g_rr.astype(F32),
+        g["layer"],
+        g["delta"],
+        f["vectors"][0],
+        f["vectors"][1],
+        f["vectors"][2],
+        g["lh"].transpose(1, 0, 2),
+        g["lm"],
+        g["rh"].transpose(2, 0, 1),
+        g["rm"],
+        woven(g["le"], local_reduce.shape[0]),
+        g["lr"],
+        woven(g["re"], 2 * fh),
+        g["rr"].reshape(2 * fh, D),
     )
 
 

time: 555 us -> 411 us (0.74)
  Pallas kernels: 190 us -> 368 us
  waiting for transfers between devices: 177 us -> 0.06 us
  matrix products: 42.1 us -> 0 us
  blocking collectives: 41 us -> 0 us
  other arithmetic: 37.9 us -> 1.52 us
  local copies, waits for them, and re-layouts: 40.2 us -> 19 us
    reduce_scatter x3 -> x0, waiting for transfers between devices: 141 us -> none  [over_branch(): lax.psum_scatter(x.astype(BF16), 'branch', scatter_dimension=dim, tiled=T...]
    pallas_call x1 -> x3, Pallas kernels: 26.5 us -> 145 us  [the longest x1 81.9 us: tail(): pl.pallas_call(functools.partial(tail_kernel, nb, nz, pool), out_shape=tu...]
    pallas_call x1, Pallas kernels: 81.6 us -> 142 us  [back(): pl.pallas_call(functools.partial(back_kernel, nb, nz, pool, inner), out_s...]
    dot_general x23 -> x0, matrix products: 42.1 us -> none  [mm(): lax.dot_general(a, b, (((ca,), (cb,)), ((), ())), preferred_element_type=...]
    psum x1 -> x0, blocking collectives: 41 us -> none  [per_device(): lax.psum(jnp.stack([delta_gain_before, delta_gain_middle, k['router'][0]]...]
    convert_element_type x11 -> x0, other arithmetic: 26.2 us -> none  [the longest x1 5.14 us: per_device(): lax.all_gather(td_own, 'branch', axis=0, tiled=True).astype(F32)]
    unnamed x85 -> x12, local copies, waits for them, and re-layouts: 27.2 us -> 6.44 us
    unnamed x11 -> x2, waiting for transfers between devices: 18.7 us -> 0.03 us
  transfers between devices with their start and end apart: 10 -> 2, of which waited for: 5 -> 0; matrix products, arithmetic and copies ran while one was open for 14% -> 1% of each run, Pallas kernels for 20% -> 55%
where the time goes in v4:
time: 411 us; the launch traced here: 405 us
  Pallas kernels  368 us (90%)
  local copies, waits for them, and re-layouts  19 us (5%)
  between operations  15.9 us (4%)
    pallas_call x1, Pallas kernels, back(): pl.pallas_call(functools.partial(back_kernel, nb, nz, pool, inner), out_s...  142 us
    pallas_call x1, Pallas kernels, tail(): pl.pallas_call(functools.partial(tail_kernel, nb, nz, pool), out_shape=tu...  81.9 us
    pallas_call x1, Pallas kernels, front(): pl.pallas_call(functools.partial(front_kernel, nb, nz, pool), out_shape=t...  81.8 us
    pallas_call x1, Pallas kernels, middle(): pl.pallas_call(functools.partial(mid_kernel, nb, pool), out_shape=tuple((...  46.8 us
    pallas_call x1, Pallas kernels, finish_all(): pl.pallas_call(finish_kernel, grid=(steps,), out_shape=(shape(rows, D), s...  15.9 us
  transfers between devices with their start and end apart: 2, of which 0 were waited for; matrix products, arithmetic and copies ran while one was open for 1% of the time, Pallas kernels for 55%

profile of v4, /device:TPU:0, one launch (start us, length us, event | category | flops | bytes accessed | tf_op | source)
XLA Modules:
  0.0 404.7 jit_solution(3587945381300276152)
XLA Ops:
  7.2 0.0 all-reduce.2.cloned.1.call-start
  7.2 1.2 dynamic_slice.17
  9.8 1.3 broadcast_in_dim.27.refs_3_.refs_7_
  11.1 1.3 broadcast_in_dim.28.refs_4_.refs_19_
  12.3 1.3 broadcast_in_dim.26.refs_3_
  13.6 0.8 pad_add_fusion
  14.4 0.1 dynamic-slice_select_fusion
  14.5 0.9 copy.43.refs_2_.refs_4_.refs_5_
  15.3 2.1 copy.52
  17.4 2.5 constant_dynamic-slice_fusion
  19.9 1.4 copy.51
  21.3 2.6 constant_dynamic-slice_fusion.1
  23.9 81.8 %shard_map.246 = (bf16[512,768]{1,0:T(8,128)(2,1)}, bf16[512,768]{1,0:T(8,128)(2,1)}, bf16[512,768]{1,0:T(8,128)(2,1)}, f32[512,1]{1,0:T(8,128)}, bf16[256,192]{...) custom-call(bf16[2048,768]{1,0:T(8,128)(2,1)} %refs_0_.1, ...), custom_call_target="tpu_custom_call" | custom-call | tf_op jit(solution)/shard_map/pallas_call | solution.py:452
  105.8 46.8 %shard_map.247 = (bf16[512,768]{1,0:T(8,128)(2,1)}, f32[512,768]{1,0:T(8,128)}, f32[512,768]{1,0:T(8,128)}, f32[512,1]{1,0:T(8,128)}, f32[1,768]{1,0:T(1,128)}, ...) custom-call(bf16[512,768]{1,0:T(8,128)(2,1)} %get-tuple-element.115.refs_0_.refs_6_, ...), custom_call_target="tpu_custom_call" | custom-call | tf_op jit(solution)/shard_map/pallas_call | solution.py:625
  152.6 0.0 all-reduce.2.cloned.1.call-update
  152.6 0.0 all-gather.3.cloned.1.call-start
  152.7 141.6 %shard_map.248 = (bf16[512,768]{1,0:T(8,128)(2,1)}, f32[512,768]{1,0:T(8,128)}, bf16[4,2,1536,128]{3,2,1,0:T(8,128)(2,1)}, bf16[2,2304,128]{2,1,0:T(8,128)(2,1)}...) custom-call(f32[512,768]{1,0:T(8,128)} %get-tuple-element.69.refs_0_.refs_2_, ...), custom_call_target="tpu_custom_call" | custom-call | flops 80000000000 | bytes 209715200 | tf_op jit(solution)/shard_map/pallas_call | solution.py:1212
  294.3 0.0 copy-start.3
  294.3 0.0 copy-start.4
  294.3 0.0 all-reduce.2.cloned.1.call-done
  294.3 0.0 all-gather.3.cloned.1.call-update
  294.4 0.1 pad.3.clone
  294.5 0.5 copy-done.3
  294.9 0.0 copy-done.4
  295.0 0.7 maximum_maximum_fusion.refs_8_
  295.7 0.0 copy-start
  295.7 81.9 %shard_map.249 = (bf16[4,512,768]{2,1,0:T(8,128)(2,1)}, bf16[2,1536,128]{2,1,0:T(8,128)(2,1)}, bf16[2,2304,128]{2,1,0:T(8,128)(2,1)}, f32[8,768]{1,0:T(8,128)}) custom-call(bf16[4,2,1536,128]{3,2,1,0:T(8,128)(2,1)} %get-tuple-element.87.refs_0_, bf16[2,2304,128]{2,1,0:T(8,128)(2,1)} %get-tuple-element.88.refs_1_, ...), custom_call_target="tpu_custom_call" | custom-call | flops 40000000000 | bytes 209715200 | tf_op jit(solution)/shard_map/pallas_call | solution.py:892
  377.6 1.5 slice_reduce_fusion
  379.1 0.0 copy-done
  379.1 1.3 copy-done.1
  380.4 1.1 copy-done.2
  381.5 15.9 %shard_map.250 = (f32[2048,768]{1,0:T(8,128)}, f32[2048,768]{1,0:T(8,128)}, f32[12288,128]{1,0:T(8,128)}, f32[2,512,768]{2,1,0:T(8,128)}, f32[3,768,128]{2,1,0:T...) custom-call(bf16[2048,768]{1,0:T(8,128)(2,1)} %bitcast.29, ...), custom_call_target="tpu_custom_call" | custom-call | tf_op jit(solution)/shard_map/pallas_call | solution.py:1290
  (5 shorter events, 0.0 us)
Async XLA Ops:
  7.2 287.1 %all-reduce.2.cloned.1.call-start = ((), (), s32[]{:S(2)}) async-start(), calls=%async_computation | async-start | bytes 4718592 | tf_op jit(solution)/shard_map/psum | solution.py:1369
  152.6 226.4 %all-gather.3.cloned.1.call-start = ((), (), s32[]{:S(2)}) async-start(), calls=%async_computation.1 | async-start | bytes 7077888 | tf_op jit(solution)/shard_map/all_gather | solution.py:1377
  294.3 0.7 copy-start.3
  294.3 0.7 copy-start.4
  295.7 83.4 %copy-start = (bf16[2,2304,128]{2,1,0:T(8,128)(2,1)S(1)}, bf16[2,2304,128]{2,1,0:T(8,128)(2,1)}, u32[]{:S(2)}) copy-start(bf16[2,2304,128]{2,1,0:T(8,128)(2,1)} %get-tuple-element.99.feed_in) | copy-start | bytes 3538948
  379.1 1.3 copy-start.1
  380.4 1.1 copy-start.2
Sparse Core Ops, SparseCore 0:
  152.8 139.2 all-reduce.1
  294.5 17.8 all-gather.2

commit v5 on v4

--- a/solution.py
+++ b/solution.py
@@ -235,20 +235,22 @@
 
 FRONT_OUT = (
     "tok_r", "cot_r", "first_r", "gate", "qr", "kv", "lh", "lm", "le", "lr", "first_w",
-    "q", "k", "v", "ctx_l", "attn_l", "ctx_r", "attn_r", "mixed",
+    "q", "k", "v", "ctx_l", "attn_l", "ctx_r", "attn_r", "mixed", "ids", "tok_own", "cot_own",
 )
 
 
 def front_kernel(nb, nz, pool, *refs):
-    tokens, cotangent, ids, gain, router, rheads, rmerge, s_lh, s_lm, s_le, s_lr = refs[:11]
+    tokens, cotangent, slots, counts, vecs, rheads, rmerge, s_lh, s_lm, s_le, s_lr = refs[:11]
     out = dict(zip(FRONT_OUT, refs[11 : 11 + len(FRONT_OUT)]))
     m = pool.bind(refs[11 + len(FRONT_OUT) :])
+    ids = out["ids"]
+    gain, router = vecs[0:1], vecs[2:3]
     b, z, c = here()
     twin = (b, z, 1 - c)
     bpeers, zpeers = others(b, nb), others(z, nz)
     rows, D = tokens.shape
     own = rows // nb
-    cap = ids.shape[0]
+    cap = slots.shape[0]
     half = cap // 2
     rw = rmerge.shape[0]
     after = (b, lax.rem(z + c, nz), 1 - c)
@@ -276,15 +278,30 @@
         size = ref.shape[0] // 2
         return ref.at[band(core * size, size)]
 
-    for i in range(4):
+    def send_weights(i):
         for j in bpeers:
             go(remote(cut(i, pairs[i][0], c), cut(i, place(i, b), c), m["w_s"].at[i, j], m["w_r"].at[i, b], (j, z, c)))
+
+    send_weights(0)
+    send_weights(1)
     for i in range(4):
         go(pltpu.make_async_copy(pairs[i][0], place(i, b), m["own_s"].at[i]))
     halo = m["halo"]
     go(remote(tokens.at[pl.ds(rows - WIN, WIN)], halo.at[0], m["halo_s"].at[0], m["halo_r"].at[0], after))
     go(remote(tokens.at[pl.ds(0, WIN)], halo.at[1], m["halo_s"].at[1], m["halo_r"].at[1], before))
 
+    n_own = counts[2 * z + c]
+    offset = jnp.where(c == 0, 0, cap - n_own)
+    rank = lax.broadcasted_iota(jnp.int32, (cap, cap), 0)
+    slot = lax.broadcasted_iota(jnp.int32, (cap, cap), 1)
+    shift = jnp.where((rank == slot + offset) & (slot < n_own), 1.0, 0.0).astype(BF16)
+    lane = lax.broadcasted_iota(jnp.int32, (cap, 128), 1)
+    high, rest = slots[...] // 64, slots[...] % 64
+    digits = jnp.where(lane == 0, high, jnp.where(lane == 1, rest, jnp.where(lane == 2, 1, 0)))
+    found = mm(shift, digits.astype(F32).astype(BF16), 1, 0)
+    ids[...] = jnp.where(found[:, 2:3] > 0.5, found[:, 0:1] * 64.0 + found[:, 1:2], -1.0).astype(jnp.int32)
+    out["tok_own"][...] = tokens[band(b * own, own)]
+    out["cot_own"][...] = cotangent[band(b * own, own)]
     picks, sib = m["picks"], m["sib"]
     step = cap // 4
     for k in range(4):
@@ -299,9 +316,9 @@
         tok = picks[at, :D].astype(F32) + sib[at, :D].astype(F32)
         out["tok_r"][at] = tok.astype(BF16)
         out["cot_r"][at] = (picks[at, D:].astype(F32) + sib[at, D:].astype(F32)).astype(BF16)
-        first = normed(tok, gain[...])
+        first = normed(tok, gain)
         out["first_r"][at] = first
-        logit = jnp.sum(first.astype(F32) * router[...], axis=-1, keepdims=True)
+        logit = jnp.sum(first.astype(F32) * router, axis=-1, keepdims=True)
         out["gate"][at] = 1.0 / (1.0 + jnp.exp(-logit))
 
     own_rows = out["first_r"][band(c * half, half)]
@@ -315,13 +332,13 @@
     go(remote(mine, mine, m["kf_s"].at[z], m["kf_r"].at[z], twin))
 
     first_w = out["first_w"]
-    first_w[pl.ds(WIN, own)] = normed(tokens[band(b * own, own)], gain[...])
+    first_w[pl.ds(WIN, own)] = normed(tokens[band(b * own, own)], gain)
     for i in range(2):
         remote(halo.at[i], halo.at[i], m["halo_s"].at[i], m["halo_r"].at[i], twin).wait_recv()
     lead = tokens[band(jnp.maximum(b * own - WIN, 0), WIN)]
     trail = tokens[band(jnp.minimum((b + 1) * own, rows - WIN), WIN)]
-    first_w[pl.ds(0, WIN)] = normed(jnp.where(b > 0, lead, halo[0]), gain[...])
-    first_w[pl.ds(WIN + own, WIN)] = normed(jnp.where(b < nb - 1, trail, halo[1]), gain[...])
+    first_w[pl.ds(0, WIN)] = normed(jnp.where(b > 0, lead, halo[0]), gain)
+    first_w[pl.ds(WIN + own, WIN)] = normed(jnp.where(b < nb - 1, trail, halo[1]), gain)
 
     def pass_weights(i):
         for j in bpeers:
@@ -340,6 +357,8 @@
         remote(piece, piece, m["kv_s"].at[j], m["kv_r"].at[j], (b, j, c)).wait_recv()
         go(remote(piece, piece, m["kf_s"].at[j], m["kf_r"].at[j], twin))
     take_weights(0)
+    send_weights(2)
+    send_weights(3)
     pltpu.make_async_copy(pairs[0][0], place(0, b), m["own_s"].at[0]).wait()
     lh, q, k, v = out["lh"], out["q"], out["k"], out["v"]
     q[...] = mm(first_w[pl.ds(WIN, own)], lh[0], 1, 0).astype(BF16)
@@ -380,7 +399,7 @@
     keys, values, qr, ctx_r = m["keys"], m["values"], out["qr"], out["ctx_r"]
     keys[...] = kv[:, :rw]
     values[...] = kv[:, rw:]
-    some = 64
+    some = 128
 
     def heavy(i, carry):
         at = band(i * some, some)
@@ -394,6 +413,7 @@
         return carry
 
     lax.fori_loop(0, half // some, heavy, 0)
+    pass_weights(2)
     attn_r = out["attn_r"]
     attn_r[...] = mm(ctx_r[...], rmerge[...], 1, 0)
 
@@ -404,7 +424,7 @@
     part[mine_at] = (
         mm(hot_rows(ids[mine_at] - b * own, own), low, 1, 0) + out["gate"][mine_at] * attn_r[...]
     ).astype(BF16)
-    group_sum_steps(nb, part, out["mixed"], m, [lambda: pass_weights(2), lambda: pass_weights(3)])
+    group_sum_steps(nb, part, out["mixed"], m, [lambda: pass_weights(3)])
     take_weights(2)
     take_weights(3)
     finish([copy for copy in sends if copy.is_remote])
@@ -412,10 +432,10 @@
         pltpu.make_async_copy(pairs[i][0], place(i, b), m["own_s"].at[i]).wait()
 
 
-def front(nb, nz, tokens, cotangent, ids, gain, router, rheads, rmerge, s_lh, s_lm, s_le, s_lr):
+def front(nb, nz, tokens, cotangent, slots, counts, vecs, rheads, rmerge, s_lh, s_lm, s_le, s_lr):
     rows, D = tokens.shape
     own = rows // nb
-    cap = ids.shape[0]
+    cap = slots.shape[0]
     half = cap // 2
     rw = rmerge.shape[0]
     wl = nb * s_lm.shape[0]
@@ -429,6 +449,7 @@
         first_w=shape(own + 2 * WIN, D), q=shape(own, wl), k=shape(own + 2 * WIN, wl),
         v=shape(own + 2 * WIN, wl), ctx_l=shape(own, wl), attn_l=shape32(own, D),
         ctx_r=shape(half, rw), attn_r=shape32(half, D), mixed=shape(cap, D),
+        ids=jax.ShapeDtypeStruct((cap, 1), jnp.int32), tok_own=shape(own, D), cot_own=shape(own, D),
     )
     pool = Pool()
     pool.vmem("picks", (cap, 2 * D))
@@ -452,18 +473,18 @@
     got = pl.pallas_call(
         functools.partial(front_kernel, nb, nz, pool),
         out_shape=tuple(outs[name] for name in FRONT_OUT),
-        in_specs=[VM] * 7 + [HB] * 4,
+        in_specs=[VM] * 3 + [pl.BlockSpec(memory_space=pltpu.SMEM)] + [VM] * 3 + [HB] * 4,
         out_specs=tuple(HB if name in ("le", "lr") else VM for name in FRONT_OUT),
         scratch_shapes=pool.shapes,
         compiler_params=pltpu.CompilerParams(
             collective_id=0, has_side_effects=True, vmem_limit_bytes=56 << 20
         ),
-    )(tokens, cotangent, ids, gain, router, rheads, rmerge, s_lh, s_lm, s_le, s_lr)
+    )(tokens, cotangent, slots, counts, vecs, rheads, rmerge, s_lh, s_lm, s_le, s_lr)
     return dict(zip(FRONT_OUT, got))
 
 
 MID_IN = (
-    "tok_own", "cot_own", "ids", "gain", "tok_r", "cot_r", "gate", "mixed", "attn_l",
+    "tok_own", "cot_own", "ids", "vecs", "tok_r", "cot_r", "gate", "mixed", "attn_l",
     "le", "lr", "re", "rr",
 )
 MID_OUT = ("layer", "gm_own", "gm_r", "gate_feed", "gain_part", "g_feed", "g_rx")
@@ -507,7 +528,7 @@
     cap = i["ids"].shape[0]
     fl = i["le"].shape[2] // nb
     fh = i["re"].shape[2]
-    gain = i["gain"][...]
+    gain = i["vecs"][1:2]
 
     pick, pick_t = m["pick"], m["pick_t"]
     hot = hot_rows(i["ids"][...] - b * own, own)
@@ -635,157 +656,258 @@
     return dict(zip(MID_OUT, got))
 
 
+def neighbours(b):
+    return b + 1 - 2 * lax.rem(b, 2), lax.rem(b + 2, 4), 3 - b
+
+
 class Gather:
-    def __init__(self, nb, src, dst, m, name):
+    def __init__(self, src, dst, m, name):
         b, z, c = here()
-        self.own = pltpu.make_async_copy(src, dst.at[b], m[f"{name}_own"])
-        self.out = [
-            remote(src, dst.at[b], m[f"{name}_s"].at[j], m[f"{name}_r"].at[b], (j, z, c)) for j in others(b, nb)
-        ]
-        self.come = [
-            remote(dst.at[j], dst.at[j], m[f"{name}_s"].at[j], m[f"{name}_r"].at[j], (j, z, c))
-            for j in others(b, nb)
-        ]
+        self.src, self.dst, self.m, self.name, self.b = src, dst, m, name, b
+        self.bx, self.by, self.bd = neighbours(b)
+        self.dx, self.dy = (self.bx, z, c), (self.by, z, c)
+        self.sends = []
+
+    def half(self, ref, k):
+        size = self.src.shape[0] // 2
+        return ref.at[pl.ds(k * size, size)]
+
+    def go(self, copy):
+        copy.start()
+        self.sends.append(copy)
+
+    def copy(self, way, k, src, slot, device):
+        m, n = self.m, self.name
+        return remote(
+            self.half(src, k), self.half(self.dst.at[slot], k), m[f"{n}_{way}_s"].at[k], m[f"{n}_{way}_r"].at[k], device
+        )
 
     def start(self):
-        self.own.start()
-        for copy in self.out:
-            copy.start()
+        own = pltpu.make_async_copy(self.src, self.dst.at[self.b], self.m[f"{self.name}_own"].at[0])
+        self.go(own)
+        for first, second in ((0, 1), (1, 0)):
+            self.go(self.copy("x", second, self.src, self.b, self.dx))
+            self.go(self.copy("y", first, self.src, self.b, self.dy))
+
+    def relay(self):
+        came = self.dst.at[self.bx]
+        self.copy("x", 1, came, self.bx, self.dx).wait_recv()
+        self.go(self.copy("f", 1, came, self.bx, self.dy))
+        came = self.dst.at[self.by]
+        self.copy("y", 0, came, self.by, self.dy).wait_recv()
+        self.go(self.copy("f", 0, came, self.by, self.dx))
 
     def wait(self):
-        for copy in self.come:
-            copy.wait_recv()
-        for copy in self.out:
-            copy.wait_send()
-        self.own.wait()
+        self.copy("x", 0, self.dst.at[self.bx], self.bx, self.dx).wait_recv()
+        self.copy("y", 1, self.dst.at[self.by], self.by, self.dy).wait_recv()
+        far = self.dst.at[self.bd]
+        self.copy("f", 0, far, self.bd, self.dx).wait_recv()
+        self.copy("f", 1, far, self.bd, self.dy).wait_recv()
+        finish(self.sends)
 
     @staticmethod
-    def scratch(pool, nb, name):
-        pool.shapes.append(pltpu.SemaphoreType.DMA)
-        pool.names.append(f"{name}_own")
-        pool.dma(f"{name}_s", nb)
-        pool.dma(f"{name}_r", nb)
+    def scratch(pool, name):
+        pool.dma(f"{name}_own", 1)
+        for way in ("x", "y", "f"):
+            pool.dma(f"{name}_{way}_s", 2)
+            pool.dma(f"{name}_{way}_r", 2)
 
 
 class ShardSum:
-    def __init__(self, nb, g, h, m, name):
+    def __init__(self, g, h, m, name):
         self.b, self.z, self.c = here()
-        self.peers = others(self.b, nb)
+        self.bx, self.by, self.bd = neighbours(self.b)
         self.g, self.h, self.m, self.name = g, h, m, name
+        self.sib = m[f"{name}_sib"]
+        size = g.shape[2] // 2
+        self.parts = (pl.ds(0, size), pl.ds(size, size))
         self.sends = []
+
+    def go(self, copy):
+        copy.start()
+        self.sends.append(copy)
 
     def pair(self, j):
         m, n = self.m, self.name
         return remote(
-            self.g.at[j, 1 - self.c], m[f"{n}_sib"].at[j], m[f"{n}_a_s"].at[j], m[f"{n}_a_r"].at[j],
+            self.g.at[j, 1 - self.c], self.sib.at[j], m[f"{n}_a_s"].at[j], m[f"{n}_a_r"].at[j],
             (self.b, self.z, 1 - self.c),
         )
 
     def start(self):
-        for j in self.peers + [self.b]:
-            copy = self.pair(j)
-            copy.start()
-            self.sends.append(copy)
+        for j in (self.bd, self.bx, self.by, self.b):
+            self.go(self.pair(j))
+
+    def step(self, n, src, k):
+        m = self.m
+        device = (self.bx if n in (0, 1, 5) else self.by, self.z, self.c)
+        return remote(
+            src.at[self.parts[k]], m[f"{self.name}_came"].at[n], m[f"{self.name}_b_s"].at[n], m[f"{self.name}_b_r"].at[n],
+            device,
+        )
+
+    def add(self, j):
+        self.pair(j).wait_recv()
+        self.sib[j] = (self.g[j, self.c].astype(F32) + self.sib[j].astype(F32)).astype(BF16)
 
     def spread(self):
-        m, n = self.m, self.name
-        for j in self.peers:
-            self.pair(j).wait_recv()
-            sib = m[f"{n}_sib"]
-            sib[j] = (self.g[j, self.c].astype(F32) + sib[j].astype(F32)).astype(BF16)
-            copy = remote(
-                sib.at[j], m[f"{n}_came"].at[self.b], m[f"{n}_b_s"].at[j], m[f"{n}_b_r"].at[self.b],
-                (j, self.z, self.c),
-            )
-            copy.start()
-            self.sends.append(copy)
+        self.add(self.bd)
+        self.go(self.step(1, self.sib.at[self.bd], 0))
+        self.go(self.step(3, self.sib.at[self.bd], 1))
+        self.add(self.bx)
+        self.go(self.step(0, self.sib.at[self.bx], 0))
+        self.add(self.by)
+        self.go(self.step(2, self.sib.at[self.by], 1))
+        self.add(self.b)
+
+    def relay(self):
+        came = self.m[f"{self.name}_came"]
+        for n, j, k, then in ((1, self.by, 0, 4), (3, self.bx, 1, 5)):
+            self.step(n, self.sib.at[j], k).wait_recv()
+            at = self.parts[k]
+            self.sib[j, at] = (self.sib[j, at].astype(F32) + came[n].astype(F32)).astype(BF16)
+            self.go(self.step(then, self.sib.at[j], k))
 
     def collect(self):
-        m, n = self.m, self.name
-        sib, came, b = m[f"{n}_sib"], m[f"{n}_came"], self.b
-        self.pair(b).wait_recv()
-        total = self.g[b, self.c].astype(F32) + sib[b].astype(F32)
-        for j in self.peers:
-            remote(sib.at[j], came.at[j], m[f"{n}_b_s"].at[j], m[f"{n}_b_r"].at[j], (j, self.z, self.c)).wait_recv()
-            total = total + came[j].astype(F32)
-        self.h[...] = total.astype(BF16)
+        came = self.m[f"{self.name}_came"]
+        for k, one, two in ((0, 0, 4), (1, 2, 5)):
+            at = self.parts[k]
+            self.step(one, self.sib.at[self.b], k).wait_recv()
+            self.step(two, self.sib.at[self.b], k).wait_recv()
+            total = self.sib[self.b, at].astype(F32) + came[one].astype(F32) + came[two].astype(F32)
+            self.h[at] = total.astype(BF16)
 
     def end(self):
         finish(self.sends)
 
     @staticmethod
-    def scratch(pool, nb, rows, name):
-        pool.vmem(f"{name}_sib", (nb, rows, 128))
-        pool.vmem(f"{name}_came", (nb, rows, 128))
-        for step in ("a", "b"):
-            pool.dma(f"{name}_{step}_s", nb)
-            pool.dma(f"{name}_{step}_r", nb)
-
-
-class BlockSum:
-    def __init__(self, nz, h, f, m, name):
+    def scratch(pool, rows, name):
+        pool.vmem(f"{name}_sib", (4, rows, 128))
+        pool.vmem(f"{name}_came", (6, rows // 2, 128))
+        pool.dma(f"{name}_a_s", 4)
+        pool.dma(f"{name}_a_r", 4)
+        pool.dma(f"{name}_b_s", 6)
+        pool.dma(f"{name}_b_r", 6)
+
+
+class ChainSum:
+    def __init__(self, nz, pieces, h, f, m, name):
         self.b, self.z, self.c = here()
-        self.peers = others(self.z, nz)
-        self.h, self.f, self.m, self.name = h, f, m, name
-        self.ch = h.shape[0] // nz
-        self.sends = []
-
-    def go(self, copy):
-        copy.start()
-        self.sends.append(copy)
-
-    def rows(self, j):
-        return band(j * self.ch, self.ch)
-
-    def start(self):
+        self.nz, self.pieces, self.h, self.f, self.m, self.name = nz, pieces, h, f, m, name
+        self.ch = h.shape[0] // 2 // pieces
+        self.steps = pieces + 2 * (nz - 1)
+        self.next = 0
+
+    def rows(self, side, p):
+        return band(side * self.pieces * self.ch + p * self.ch, self.ch)
+
+    def copies(self, side, p):
         m, n = self.m, self.name
-        for j in self.peers:
-            self.go(
-                remote(
-                    self.h.at[self.rows(j)], m[f"{n}_came"].at[self.z], m[f"{n}_a_s"].at[j],
-                    m[f"{n}_a_r"].at[self.z], (self.b, j, self.c),
-                )
-            )
-
-    def spread(self):
-        m, n = self.m, self.name
-        came, z, c = m[f"{n}_came"], self.z, self.c
-        total = self.h[self.rows(z)].astype(F32)
-        for j in self.peers:
-            remote(
-                self.h.at[self.rows(j)], came.at[j], m[f"{n}_a_s"].at[j], m[f"{n}_a_r"].at[j], (self.b, j, c)
-            ).wait_recv()
-            total = total + came[j].astype(F32)
-        mine = self.f.at[c, self.rows(z)]
-        mine[...] = total.astype(BF16)
-        for j in self.peers:
-            self.go(remote(mine, mine, m[f"{n}_b_s"].at[j], m[f"{n}_b_r"].at[z], (self.b, j, c)))
-        self.go(remote(mine, mine, m[f"{n}_c_s"].at[z], m[f"{n}_c_r"].at[z], (self.b, z, 1 - c)))
-
-    def forward(self):
-        m, n, c = self.m, self.name, self.c
-        for j in self.peers:
-            piece = self.f.at[c, self.rows(j)]
-            remote(piece, piece, m[f"{n}_b_s"].at[j], m[f"{n}_b_r"].at[j], (self.b, j, c)).wait_recv()
-            self.go(remote(piece, piece, m[f"{n}_c_s"].at[j], m[f"{n}_c_r"].at[j], (self.b, self.z, 1 - c)))
+        came = m[f"{n}_came"].at[side, p]
+        piece = self.f.at[self.c, self.rows(side, p)]
+        step = 1 - 2 * side
+        on = (self.b, lax.rem(self.z + step + self.nz, self.nz), self.c)
+        back = (self.b, lax.rem(self.z - step + self.nz, self.nz), self.c)
+        over = (self.b, self.z, 1 - self.c)
+        sem = lambda kind: m[f"{n}_{kind}"].at[side, p]
+        return (
+            lambda src: remote(src, came, sem("a_s"), sem("a_r"), on),
+            lambda src: remote(src, piece, sem("b_s"), sem("b_r"), back),
+            lambda src: remote(src, piece, sem("c_s"), sem("c_r"), over),
+            piece,
+        )
+
+    def pump(self, s):
+        last = self.nz - 1
+        for side in range(2):
+            pos = self.z if side == 0 else last - self.z
+            p = s - pos
+
+            @pl.when((p >= 0) & (p < self.pieces))
+            def _():
+                on, back, over, piece = self.copies(side, p)
+                own = self.h.at[self.rows(side, p)]
+                came = self.m[f"{self.name}_came"].at[side, p]
+
+                @pl.when(pos == 0)
+                def _():
+                    on(own).start()
+
+                @pl.when(pos > 0)
+                def _():
+                    on(came).wait_recv()
+                    came[...] = (own[...].astype(F32) + came[...].astype(F32)).astype(BF16)
+
+                @pl.when((pos > 0) & (pos < last))
+                def _():
+                    on(came).start()
+
+                @pl.when(pos == last)
+                def _():
+                    pltpu.make_async_copy(came, piece, self.m[f"{self.name}_own"].at[side, p]).start()
+                    back(came).start()
+                    over(came).start()
+
+            q = s - last - (last - pos)
+
+            @pl.when((q >= 0) & (q < self.pieces) & (pos < last))
+            def _():
+                on, back, over, piece = self.copies(side, q)
+                back(piece).wait_recv()
+                over(piece).start()
+
+                @pl.when(pos > 0)
+                def _():
+                    back(piece).start()
+
+    def go(self, count=None):
+        upto = self.steps if count is None else min(self.steps, self.next + count)
+        if upto - self.next > 4:
+            lax.fori_loop(self.next, upto, lambda s, carry: (self.pump(s), carry)[1], 0)
+        else:
+            for s in range(self.next, upto):
+                self.pump(s)
+        self.next = upto
 
     def end(self):
-        m, n, c = self.m, self.name, self.c
-        for j in self.peers + [self.z]:
-            piece = self.f.at[1 - c, self.rows(j)]
-            remote(piece, piece, m[f"{n}_c_s"].at[j], m[f"{n}_c_r"].at[j], (self.b, self.z, 1 - c)).wait_recv()
-        finish(self.sends)
+        self.go()
+        last = self.nz - 1
+
+        def one(p, carry):
+            for side in range(2):
+                pos = self.z if side == 0 else last - self.z
+                on, back, over, piece = self.copies(side, p)
+                other = self.f.at[1 - self.c, self.rows(side, p)]
+                came = self.m[f"{self.name}_came"].at[side, p]
+                sem = lambda kind: self.m[f"{self.name}_{kind}"].at[side, p]
+                remote(other, other, sem("c_s"), sem("c_r"), (self.b, self.z, 1 - self.c)).wait_recv()
+                over(piece).wait_send()
+
+                @pl.when(pos < last)
+                def _():
+                    on(came).wait_send()
+
+                @pl.when(pos > 0)
+                def _():
+                    back(piece).wait_send()
+
+                @pl.when(pos == last)
+                def _():
+                    pltpu.make_async_copy(came, piece, self.m[f"{self.name}_own"].at[side, p]).wait()
+
+            return carry
+
+        lax.fori_loop(0, self.pieces, one, 0)
 
     @staticmethod
-    def scratch(pool, nz, rows, name):
-        pool.vmem(f"{name}_came", (nz, rows // nz, 128))
-        for step in ("a", "b", "c"):
-            pool.dma(f"{name}_{step}_s", nz)
-            pool.dma(f"{name}_{step}_r", nz)
-
-
-TAIL_IN = ("g_att", "g_heavy", "gm_own", "gf_l", "gf_r", "ids", "tok_own", "gain", "vec")
-TAIL_OUT = ("delta", "f_att", "f_heavy", "vectors")
+    def scratch(pool, rows, pieces, name):
+        pool.vmem(f"{name}_came", (2, pieces, rows // 2 // pieces, 128))
+        for kind in ("a_s", "a_r", "b_s", "b_r", "c_s", "c_r", "own"):
+            pool.dma(f"{name}_{kind}", 2, pieces)
+
+
+TAIL_IN = ("g_att", "g_heavy", "h_feed", "gm_own", "gf_l", "gf_r", "ids", "tok_own", "vecs", "gain_part", "router")
+TAIL_OUT = ("delta", "f_att", "f_heavy", "f_feed", "vectors")
 
 
 def tail_kernel(nb, nz, pool, *refs):
@@ -800,14 +922,17 @@
     gh, sib_h, h_heavy = i["g_heavy"], m["sib_h"], m["h_heavy"]
     to_twin = remote(gh.at[1 - c], sib_h, m["sib_h_s"].at[0], m["sib_h_r"].at[0], twin)
     to_twin.start()
-    shard = ShardSum(nb, i["g_att"], m["h_att"], m, "ga")
+    shard = ShardSum(i["g_att"], m["h_att"], m, "ga")
     shard.start()
-    att = BlockSum(nz, m["h_att"], out["f_att"], m, "za")
-    heavy = BlockSum(nz, h_heavy, out["f_heavy"], m, "zh")
+    feeds = ChainSum(nz, 4, i["h_feed"], out["f_feed"], m, "zf")
+    heavy = ChainSum(nz, 4, h_heavy, out["f_heavy"], m, "zh")
+    att = ChainSum(nz, 4, m["h_att"], out["f_att"], m, "za")
+    feeds.go(1)
+    shard.spread()
     to_twin.wait_recv()
     h_heavy[...] = (gh[c].astype(F32) + sib_h[...].astype(F32)).astype(BF16)
-    heavy.start()
-    shard.spread()
+    feeds.go(1)
+    heavy.go(1)
 
     hot_t = hot_rows(i["ids"][...] - b * own, own).T
     owned = jnp.sum(hot_t.astype(F32), axis=1, keepdims=True) > 0.5
@@ -815,13 +940,18 @@
     r, xh = norm_parts(i["tok_own"][...].astype(F32))
     gain_part = jnp.sum(gf * xh, axis=0, keepdims=True)
     low = m["low"]
-    low[...] = (i["gm_own"][...] + norm_back(gf, xh, r, i["gain"][...])).astype(BF16)
-    rows = Gather(nb, low, out["delta"], m, "td")
+    low[...] = (i["gm_own"][...] + norm_back(gf, xh, r, i["vecs"][0:1])).astype(BF16)
+    rows = Gather(low, out["delta"], m, "td")
     rows.start()
+    shard.relay()
+    feeds.go(1)
+    heavy.go(1)
 
     vec = m["vec_mine"]
-    vec[pl.ds(0, 8)] = i["vec"][...]
+    vec[...] = jnp.zeros_like(vec)
     vec[pl.ds(0, 1)] = gain_part
+    vec[pl.ds(1, 1)] = i["gain_part"][...]
+    vec[pl.ds(2, 1)] = i["router"][...]
     sends = [to_twin]
 
     def vec_step(name, me, peers, device):
@@ -840,23 +970,30 @@
 
     by_core, by_branch, by_block = (lambda j: (b, z, j)), (lambda j: (j, z, c)), (lambda j: (b, j, c))
     vec_step("vc", c, [1 - c], by_core)
+    feeds.go(1)
+    heavy.go(1)
     shard.collect()
-    att.start()
+    att.go(1)
     total = vec_end("vc", [1 - c], by_core)
     vec2 = m["vec_pair"]
     vec2[...] = total
     vec = vec2
     vec_step("vb", b, bpeers, by_branch)
-    heavy.spread()
+    feeds.go(1)
+    heavy.go(1)
+    att.go(1)
+    rows.relay()
     total = vec_end("vb", bpeers, by_branch)
     vec3 = m["vec_group"]
     vec3[...] = total
     vec = vec3
     vec_step("vz", z, zpeers, by_block)
-    att.spread()
-    heavy.forward()
+    while att.next < att.steps:
+        feeds.go(1)
+        heavy.go(1)
+        att.go(1)
     out["vectors"][...] = vec_end("vz", zpeers, by_block)
-    att.forward()
+    feeds.end()
     heavy.end()
     att.end()
     shard.end()
@@ -866,10 +1003,10 @@
 
 def tail(nb, nz, given):
     own, D = given["gm_own"].shape
-    ra, rh = given["g_att"].shape[2], given["g_heavy"].shape[1]
+    ra, rh, rf = given["g_att"].shape[2], given["g_heavy"].shape[1], given["h_feed"].shape[0]
     shape = lambda *dims: jax.ShapeDtypeStruct(dims, BF16)
     outs = dict(
-        delta=shape(nb, own, D), f_att=shape(2, ra, 128), f_heavy=shape(2, rh, 128),
+        delta=shape(nb, own, D), f_att=shape(2, ra, 128), f_heavy=shape(2, rh, 128), f_feed=shape(2, rf, 128),
         vectors=jax.ShapeDtypeStruct((8, D), F32),
     )
     pool = Pool()
@@ -879,10 +1016,11 @@
     pool.vmem("low", (own, D))
     pool.dma("sib_h_s", 1)
     pool.dma("sib_h_r", 1)
-    ShardSum.scratch(pool, nb, ra, "ga")
-    BlockSum.scratch(pool, nz, ra, "za")
-    BlockSum.scratch(pool, nz, rh, "zh")
-    Gather.scratch(pool, nb, "td")
+    ShardSum.scratch(pool, ra, "ga")
+    ChainSum.scratch(pool, ra, 4, "za")
+    ChainSum.scratch(pool, rh, 4, "zh")
+    ChainSum.scratch(pool, rf, 4, "zf")
+    Gather.scratch(pool, "td")
     for name in ("vec_mine", "vec_pair", "vec_group"):
         pool.vmem(name, (8, D), F32)
     for name, count in (("vc", 2), ("vb", nb), ("vz", nz)):
@@ -893,21 +1031,21 @@
         functools.partial(tail_kernel, nb, nz, pool),
         out_shape=tuple(outs[name] for name in TAIL_OUT),
         in_specs=[VM] * len(TAIL_IN),
-        out_specs=(HB,) + (VM,) * (len(TAIL_OUT) - 1),
+        out_specs=(HB,) * 4 + (VM,),
         scratch_shapes=pool.shapes,
         compiler_params=pltpu.CompilerParams(
             collective_id=4, has_side_effects=True, vmem_limit_bytes=56 << 20
         ),
-        cost_estimate=pl.CostEstimate(flops=40 * 10**9, bytes_accessed=200 * 2**20, transcendentals=0),
     )(*(given[name] for name in TAIL_IN))
     return dict(zip(TAIL_OUT, got))
 
 
-BACK_OUT = ("gf_r", "gf_l", "g_att", "g_heavy", "router", "lay", "f_feed")
+RX_PIECES = 8
+BACK_OUT = ("gf_r", "gf_l", "g_att", "g_heavy", "router", "lay", "h_feed", "f_rx")
 BACK_IN = (
     "gm_own", "gm_r", "gate", "gate_feed", "ids", "q", "k", "v", "lm", "lh", "first_w", "ctx_l",
-    "qr", "kv", "rmerge", "rheads", "first_r", "ctx_r", "attn_r", "router_vector",
-    "layer", "g_feed",
+    "qr", "kv", "rmerge", "rheads", "first_r", "ctx_r", "attn_r", "vecs",
+    "layer", "g_feed", "g_rx",
 )
 
 
@@ -915,7 +1053,7 @@
     return BACK_IN if inner else BACK_IN + ("trio",)
 
 
-def heavy_back(i, m, seed, x):
+def heavy_back(i, m, seed, x, chain):
     kv, qr = i["kv"], i["qr"]
     half, rw = qr.shape
     keys, values, keys_t, dk, dv, dq_t, do = (
@@ -933,6 +1071,7 @@
     def heavy(n, carry):
         at = band(n * some, some)
         for h in range(rw // DH):
+            chain.pump(n * (rw // DH) + h)
             qh, doh = only_head(qr[at], h), only_head(do[at], h)
             s = mm(keys[...], qh, 1, 1) * SCALE
             w = jnp.exp(s - jnp.max(s, axis=0, keepdims=True))
@@ -946,6 +1085,7 @@
         return carry
 
     lax.fori_loop(0, half // some, heavy, 0)
+    chain.next = half // some * (rw // DH)
     x[:, :rw] = (dk[...] * SCALE).astype(BF16)
     x[:, rw:] = dv[...].astype(BF16)
 
@@ -995,9 +1135,9 @@
     greet([twin, after, before] + [(j, z, c) for j in bpeers] + [(b, j, c) for j in zpeers])
     mine_at, other_at = band(c * half, half), band((1 - c) * half, half)
     sends = []
-    layer = Gather(nb, i["layer"], out["lay"], m, "ly")
-    shard = ShardSum(nb, i["g_feed"], m["h_feed"], m, "gf")
-    feeds = BlockSum(nz, m["h_feed"], out["f_feed"], m, "zf")
+    layer = Gather(i["layer"], out["lay"], m, "ly")
+    shard = ShardSum(i["g_feed"], out["h_feed"], m, "gf")
+    chain = ChainSum(nz, RX_PIECES, i["g_rx"], out["f_rx"], m, "zx")
     shard.start()
     layer.start()
 
@@ -1017,13 +1157,15 @@
     def to_twin(j):
         return remote(x.at[spot(1 - c, j)], sib.at[j], m["bs_sib_s"].at[j], m["bs_sib_r"].at[j], twin)
 
+    shard.spread()
     if inner:
         x, sib, part, came = m["dkv"], m["bs_sib"], m["bs_part"], m["bs_came"]
-        heavy_back(i, m, seed, x)
+        heavy_back(i, m, seed, x, chain)
         for j in zpeers + [z]:
             go(to_twin(j))
 
-    shard.spread()
+    shard.relay()
+    layer.relay()
     low, do_l = m["low"], m["do_l"]
     low[...] = i["gm_own"][...].astype(BF16)
     do_l[...] = mm(low[...], i["lm"][...], 1, 1).astype(BF16)
@@ -1065,11 +1207,13 @@
         dvl[near, lanes] += got_v
         both = jnp.where(head_lanes((2 * DH, WIN), 0, 0), got_q[0], got_q[1])
         dql[at, lanes] = (both.T * SCALE).astype(BF16)
+        pl.when(lax.rem(n_, 4) == 3)(lambda: chain.pump(pumped + n_ // 4))
         return carry
 
+    pumped = chain.next
     lax.fori_loop(0, blocks * (wl // (2 * DH)), light, 0)
+    chain.next = pumped + blocks * (wl // (2 * DH)) // 4
     shard.collect()
-    feeds.start()
     rim, came_rim = m["rim"], m["came_rim"]
     for n, start in ((0, WIN + own), (1, 0)):
         rim[n, :, :wl] = (dkl[pl.ds(start, WIN)] * SCALE).astype(BF16)
@@ -1102,7 +1246,7 @@
     gf_l = out["gf_l"]
     gf_l[...] = mm(dql[...], lh[0], 1, 1) + mm(dk_own[...], lh[1], 1, 1) + mm(dv_own[...], lh[2], 1, 1)
 
-    feeds.spread()
+    chain.go(1)
     gate, first_r = i["gate"], i["first_r"]
     gate_attn = jnp.sum(gm_half * i["attn_r"][...], axis=-1, keepdims=True)
     total_part = m["part"]
@@ -1114,7 +1258,7 @@
         d_logit = d_gate * g * (1.0 - g)
         one = jnp.sum(d_logit * first_r[at].astype(F32), axis=0, keepdims=True)
         router_sum = one if router_sum is None else router_sum + one
-        sum_ = mm(hot_rows(i["ids"][at] - b * own, own), low_gf, 1, 0) + d_logit * i["router_vector"][...]
+        sum_ = mm(hot_rows(i["ids"][at] - b * own, own), low_gf, 1, 0) + d_logit * i["vecs"][2:3]
         if more is not None:
             sum_ = sum_ + more
         total_part[at] = sum_.astype(BF16)
@@ -1135,6 +1279,7 @@
             return carry
 
         lax.fori_loop(0, nb // 2, one, 0)
+        chain.go(1)
 
     def weights_rest():
         def one(t, carry):
@@ -1147,10 +1292,10 @@
         first_half = first_r[mine_at]
         for n in range(3):
             pack_rows(out["g_heavy"], n * rw // 2 * (D // 128), lane_blocks(mm(trio[n], first_half, 0, 0)))
-        feeds.forward()
+        chain.go(1)
 
     group_sum_steps(nb, total_part, out["gf_r"], m, [weights_light, weights_rest])
-    feeds.end()
+    chain.end()
     shard.end()
     layer.wait()
     finish(sends)
@@ -1163,13 +1308,13 @@
     rw = given["rmerge"].shape[0]
     wl = given["q"].shape[1]
     deep = 2 * nz * half
-    feed_rows = given["g_feed"].shape[2]
+    feed_rows, rx_rows = given["g_feed"].shape[2], given["g_rx"].shape[0]
     shape = lambda *dims: jax.ShapeDtypeStruct(dims, BF16)
     outs = dict(
         gf_r=shape(cap, D), gf_l=jax.ShapeDtypeStruct((own, D), F32),
         g_att=shape(nb, 2, 2 * D * wl // nb // 128, 128), g_heavy=shape(2, 2 * D * rw // 128, 128),
         router=jax.ShapeDtypeStruct((1, D), F32),
-        lay=shape(nb, own, D), f_feed=shape(2, feed_rows, 128),
+        lay=shape(nb, own, D), h_feed=shape(feed_rows, 128), f_rx=shape(2, rx_rows, 128),
     )
     pool = Pool()
     inner = deep <= 4096
@@ -1203,22 +1348,20 @@
         pool.dma(f"{name}_r", nz)
     if not inner:
         given = dict(given, trio=heavy_back_plain(given))
-    pool.vmem("h_feed", (feed_rows, 128))
-    ShardSum.scratch(pool, nb, feed_rows, "gf")
-    BlockSum.scratch(pool, nz, feed_rows, "zf")
-    Gather.scratch(pool, nb, "ly")
+    ShardSum.scratch(pool, feed_rows, "gf")
+    ChainSum.scratch(pool, rx_rows, RX_PIECES, "zx")
+    Gather.scratch(pool, "ly")
     pool.dma("rim_s", 2)
     pool.dma("rim_r", 2)
     got = pl.pallas_call(
         functools.partial(back_kernel, nb, nz, pool, inner),
         out_shape=tuple(outs[name] for name in BACK_OUT),
         in_specs=[VM] * len(back_names(inner)),
-        out_specs=tuple(HB if name == "lay" else VM for name in BACK_OUT),
+        out_specs=tuple(HB if name in ("lay", "f_rx") else VM for name in BACK_OUT),
         scratch_shapes=pool.shapes,
         compiler_params=pltpu.CompilerParams(
             collective_id=3, has_side_effects=True, vmem_limit_bytes=62 << 20
         ),
-        cost_estimate=pl.CostEstimate(flops=80 * 10**9, bytes_accessed=200 * 2**20, transcendentals=0),
     )(*(given[name] for name in back_names(inner)))
     return dict(zip(BACK_OUT, got))
 
@@ -1336,47 +1479,23 @@
 ):
     nb = lax.axis_size("branch")
     nz = lax.axis_size("zz")
-    b = lax.axis_index("branch")
-    z = lax.axis_index("zz")
     core = lax.axis_index("core")
-    d = 2 * z + core
     rows, D = tokens.shape
-    own = rows // nb
-    cap = routed_slots.shape[0]
-    half = cap // 2
     fh = routed_expand.shape[2] // 2
-
-    n_own = routed_counts[d]
-    offset = jnp.where(core == 0, 0, cap - n_own)
-    ranks = jnp.arange(cap, dtype=jnp.int32)
-    live = (ranks >= offset) & (ranks < offset + n_own)
-    twice = jnp.concatenate([routed_slots, routed_slots])
-    rolled = lax.dynamic_slice(twice, (jnp.mod(cap - offset, cap),), (cap,))
-    ids = jnp.where(live, rolled, -1)[:, None]
+    vecs = jnp.stack([gain_before, gain_middle, router_vector])
     rheads = routed_heads.transpose(1, 2, 0)
     f = front(
-        nb, nz, tokens, cotangent, ids, gain_before[None], router_vector[None], rheads, routed_merge,
+        nb, nz, tokens, cotangent, routed_slots[:, None], routed_counts, vecs, rheads, routed_merge,
         local_heads.transpose(1, 0, 2), local_merge, local_expand.transpose(1, 0, 2), local_reduce,
     )
-    tok_own = lax.dynamic_slice(tokens, (b * own, 0), (own, D))
-    cot_own = lax.dynamic_slice(cotangent, (b * own, 0), (own, D))
     re_half = lax.dynamic_slice(routed_expand, (0, 0, core * fh), (D, 2, fh)).transpose(1, 0, 2)
-    f = dict(
-        f, tok_own=tok_own, cot_own=cot_own, ids=ids, gain=gain_middle[None], re=re_half, rr=routed_reduce,
-        rmerge=routed_merge, rheads=rheads, router_vector=router_vector[None],
-    )
+    f = dict(f, vecs=vecs, re=re_half, rr=routed_reduce, rmerge=routed_merge, rheads=rheads)
     f = dict(f, **middle(nb, f))
-    rx_sum = lax.psum(f["g_rx"], "zz")
+    f["g_rx"] = f["g_rx"].reshape(-1, 128)
     f = dict(f, **back(nb, nz, f))
-    rx_sum, f["gf_r"] = lax.optimization_barrier((rx_sum, f["gf_r"]))
-    vec = jnp.concatenate(
-        [jnp.zeros((1, D), F32), f["gain_part"], f["router"], jnp.zeros((5, D), F32)], 0
-    )
-    f = dict(f, gain=gain_before[None], vec=vec)
     f = dict(f, **tail(nb, nz, f))
-    rx_sum = lax.all_gather(rx_sum, "core")
     g = finish_all(
-        f["lay"].reshape(rows, D), f["delta"].reshape(rows, D), rx_sum,
+        f["lay"].reshape(rows, D), f["delta"].reshape(rows, D), f["f_rx"].reshape(2, -1, D, 128),
         f["f_att"], f["f_heavy"], f["f_feed"], hl=local_merge.shape[0], fl=local_reduce.shape[0],
         rw=routed_merge.shape[0],
     )

time: 411 us -> 376 us (0.915)
  Pallas kernels: 368 us -> 353 us
  between operations: 15.9 us -> 1.15 us
  local copies, waits for them, and re-layouts: 19 us -> 14.7 us
    pallas_call x1, Pallas kernels: 142 us -> 130 us  [back(): pl.pallas_call(functools.partial(back_kernel, nb, nz, pool, inner), out_s...]
    pallas_call x1, Pallas kernels: 81.8 us -> 76.7 us  [front(): pl.pallas_call(functools.partial(front_kernel, nb, nz, pool), out_shape=t...]
  transfers between devices with their start and end apart: 2 -> 0, of which waited for: 0 -> 0; matrix products, arithmetic and copies ran while one was open for 1% -> 0% of each run, Pallas kernels for 55% -> 0%
where the time goes in v5:
time: 376 us; the launch traced here: 369 us
  Pallas kernels  353 us (94%)
  local copies, waits for them, and re-layouts  14.7 us (4%)
    pallas_call x1, Pallas kernels, back(): pl.pallas_call(functools.partial(back_kernel, nb, nz, pool, inner), out_s...  130 us
    pallas_call x1, Pallas kernels, tail(): pl.pallas_call(functools.partial(tail_kernel, nb, nz, pool), out_shape=tu...  83.5 us
    pallas_call x1, Pallas kernels, front(): pl.pallas_call(functools.partial(front_kernel, nb, nz, pool), out_shape=t...  76.7 us
    pallas_call x1, Pallas kernels, middle(): pl.pallas_call(functools.partial(mid_kernel, nb, pool), out_shape=tuple((...  46.4 us
    pallas_call x1, Pallas kernels, finish_all(): pl.pallas_call(finish_kernel, grid=(steps,), out_shape=(shape(rows, D), s...  15.9 us

profile of v5, /device:TPU:0, one launch (start us, length us, event | category | flops | bytes accessed | tf_op | source)
XLA Modules:
  0.0 369.0 jit_solution(17837111371479982463)
XLA Ops:
  0.6 0.7 stack.12
  1.3 0.7 stack.13
  2.0 0.7 stack.14
  2.7 0.6 pad_maximum_fusion.refs_4_.refs_3_.refs_19_.refs_8_
  3.3 1.5 copy.33.refs_2_
  4.9 2.1 copy.41
  7.0 2.5 constant_dynamic-slice_fusion
  9.5 1.4 copy.40
  10.9 76.7 %shard_map.246 = (bf16[512,768]{1,0:T(8,128)(2,1)}, bf16[512,768]{1,0:T(8,128)(2,1)}, bf16[512,768]{1,0:T(8,128)(2,1)}, f32[512,1]{1,0:T(8,128)}, bf16[256,192]{...) custom-call(bf16[2048,768]{1,0:T(8,128)(2,1)} %refs_0_.1, ...), custom_call_target="tpu_custom_call" | custom-call | tf_op jit(solution)/shard_map/pallas_call | solution.py:473
  87.6 46.4 %shard_map.247 = (bf16[512,768]{1,0:T(8,128)(2,1)}, f32[512,768]{1,0:T(8,128)}, f32[512,768]{1,0:T(8,128)}, f32[512,1]{1,0:T(8,128)}, f32[1,768]{1,0:T(1,128)}, ...) custom-call(bf16[512,768]{1,0:T(8,128)(2,1)} %get-tuple-element.65.refs_0_.refs_7_, ...), custom_call_target="tpu_custom_call" | custom-call | tf_op jit(solution)/shard_map/pallas_call | solution.py:646
  134.0 130.0 %shard_map.248 = (bf16[512,768]{1,0:T(8,128)(2,1)}, f32[512,768]{1,0:T(8,128)}, bf16[4,2,1536,128]{3,2,1,0:T(8,128)(2,1)}, bf16[2,2304,128]{2,1,0:T(8,128)(2,1)}...) custom-call(f32[512,768]{1,0:T(8,128)} %get-tuple-element.75.refs_0_, ...), custom_call_target="tpu_custom_call" | custom-call | tf_op jit(solution)/shard_map/pallas_call | solution.py:1356
  264.0 83.5 %shard_map.249 = (bf16[4,512,768]{2,1,0:T(8,128)(2,1)}, bf16[2,1536,128]{2,1,0:T(8,128)(2,1)}, bf16[2,2304,128]{2,1,0:T(8,128)(2,1)}, bf16[2,2304,128]{2,1,0:T(8,128)(2,1)}, f32[8,768]{1,0:T(8,128)}) custom-call(bf16[4,2,1536,128]{3,2,1,0:T(8,128)(2,1)} %get-tuple-element.94.refs_0_, bf16[2,2304,128]{2,1,0:T(8,128)(2,1)} %get-tuple-element.95.refs_1_, ...), custom_call_target="tpu_custom_call" | custom-call | tf_op jit(solution)/shard_map/pallas_call | solution.py:1030
  347.5 1.5 slice_reduce_fusion
  349.0 0.0 copy-start
  349.0 1.3 copy-done
  350.3 0.0 copy-start.1
  350.3 1.3 copy-done.1
  351.5 0.0 copy-start.2
  351.5 1.1 copy-done.2
  352.7 15.9 %shard_map.250 = (f32[2048,768]{1,0:T(8,128)}, f32[2048,768]{1,0:T(8,128)}, f32[12288,128]{1,0:T(8,128)}, f32[2,512,768]{2,1,0:T(8,128)}, f32[3,768,128]{2,1,0:T...) custom-call(bf16[2048,768]{1,0:T(8,128)(2,1)} %bitcast.30, ...), custom_call_target="tpu_custom_call" | custom-call | tf_op jit(solution)/shard_map/pallas_call | solution.py:1433
Async XLA Ops:
  349.0 1.3 copy-start
  350.3 1.3 copy-start.1
  351.5 1.1 copy-start.2
